TPU v7x, 32 devices: a whole 2x2x4 slice. The times are simulated.
32 devices in a mesh: chan: 4 (over y, x), pair: 8 (over z, core).
Axes of the slice: x: 2, y: 2, z: 4, core: 2. Of those that a mesh axis runs over, the one named last changes fastest.
Arguments:
- visibility: bfloat16 [4, 4096, 256], P('chan', 'pair'), may hold values from -6 to 6
- pair_counts: int32 [4096], P('pair'), may hold values from 1 to 4
- owner_ids: int32 [4096, 1], P('pair'), may hold values from 0 to 7; in each aligned block of 512 rows (0 to 511, 512 to 1023, ...) at most 132 rows name the same one
- slot_ids: int32 [4096], P('pair'), may hold values from 0 to 2047
- beam: float32 [4, 2, 2, 16384, 1024], P('chan', None, None, 'pair'), may hold values from -0.046875 to 0.046875
Outputs:
- modes: float32 [4, 1024, 2, 2, 64], P('chan', 'pair')
- mode_power: float32 [1024, 2], P('pair')
Inputs may be any that keep to these rules, and one draw needn't show every extreme that they name: `owner_ids`: among the 512 feed pairs of one device, no owner is named more than 132 times, a bound that some block reaches.
All inputs are finite; a program needn't handle non-finite values.
Results may differ from a plain program's by a relative error of at most 0.0017.
Values may be sent and summed in bfloat16 or wider, within the bound.
No kernel may reach another device: no remote copies, remote signals or barrier semaphores. Data moves between devices by JAX's collectives and lax.ppermute only.
A program may use at most 64 MiB of HBM per device.

v0:
```python
import jax
import jax.numpy as jnp
from jax import lax
from jax.sharding import PartitionSpec as P


def per_device(visibility, pair_counts, owner_ids, slot_ids, beam):
    peers = lax.axis_size("pair")
    pair_rows = pair_counts.shape[0]
    capacity = 2 * pair_rows // peers + 4
    owner = owner_ids[:, 0]
    order = jnp.argsort(owner, stable=True)
    sorted_owner = owner[order]
    owner_list = jnp.arange(peers, dtype=jnp.int32)
    first_at = jnp.searchsorted(sorted_owner, owner_list, side="left")
    last_at = jnp.searchsorted(sorted_owner, owner_list, side="right")
    ranks = jnp.arange(capacity, dtype=jnp.int32)
    valid = ranks[None, :] < (last_at - first_at)[:, None]
    where_at = jnp.clip(first_at[:, None] + ranks[None, :], 0, pair_rows - 1)
    picked = order[where_at]
    weights = jnp.where(valid, pair_counts[picked], 0)
    offsets = jnp.where(valid, slot_ids[picked], 0)
    rows = visibility[0][picked]
    weighted = (rows.astype(jnp.float32) * weights[:, :, None].astype(jnp.float32)).astype(
        jnp.bfloat16
    )
    got_rows, got_offsets, got_weights = (
        lax.all_to_all(weighted, "pair", split_axis=0, concat_axis=0, tiled=True),
        lax.all_to_all(offsets, "pair", split_axis=0, concat_axis=0, tiled=True),
        lax.all_to_all(weights, "pair", split_axis=0, concat_axis=0, tiled=True),
    )
    columns = got_rows.shape[2]
    got_rows = got_rows.reshape(peers * capacity, columns)
    got_offsets = got_offsets.reshape(peers * capacity)
    got_weights = got_weights.reshape(peers * capacity).astype(jnp.float32)
    beam_local = beam[0]
    mwin = beam_local.shape[0]
    base_dev = beam_local.shape[2]
    sets = columns // (2 * mwin)
    matches = jnp.arange(base_dev, dtype=jnp.int32)[:, None] == got_offsets[None, :]
    numer = jnp.dot(matches.astype(jnp.bfloat16), got_rows, preferred_element_type=jnp.float32)
    denom = jnp.sum(jnp.where(matches, got_weights[None, :], 0.0), axis=1)
    stacked = numer / jnp.maximum(denom, 1.0)[:, None]
    stacked = stacked.reshape(base_dev, mwin, 2 * sets)
    real_part = stacked[:, :, :sets]
    imag_part = stacked[:, :, sets:]
    swapped = jnp.concatenate([imag_part, -real_part], axis=2)
    right = jnp.stack([stacked, swapped], axis=0)
    amplitudes = lax.psum_scatter(
        jnp.einsum(
            "mrbk,rbmc->kmc",
            beam_local,
            right,
            precision=lax.Precision.HIGHEST,
            preferred_element_type=jnp.float32,
        ),
        "pair",
        scatter_dimension=0,
        tiled=True,
    )
    power_local = jnp.sum(amplitudes * amplitudes, axis=2)
    total_power = lax.psum(power_local, "chan")
    mode_power = total_power / (lax.axis_size("chan") * sets)
    shaped = amplitudes.reshape(amplitudes.shape[0], mwin, 2, sets)
    return (shaped[None], mode_power)


def solution(mesh):
    in_specs = (
        P("chan", "pair", None),
        P("pair"),
        P("pair", None),
        P("pair"),
        P("chan", None, None, "pair", None),
    )
    out_specs = (P("chan", "pair", None, None, None), P("pair", None))
    return jax.shard_map(
        per_device, mesh=mesh, in_specs=in_specs, out_specs=out_specs, check_vma=False
    )
```

profile of v0, /device:TPU:0, one launch (start us, length us, event | category | flops | bytes accessed | tf_op | source)
XLA Modules:
  0.0 169.5 jit_solution(9162694231471934099)
XLA Ops:
  7.2 0.0 copy-start
  7.2 4.5 %sort.17 = (s32[512]{0:T(512)}, s32[512]{0:T(512)S(1)}) sort(s32[512]{0:T(512)} %bitcast.25, s32[512]{0:T(512)S(1)} %iota.29), dimensions={0}, to_apply=%region_0.0 | sort | flops 4608 | bytes 8192 | tf_op jit(solution)/shard_map/jit(argsort)/sort | solution.py:12
  11.7 3.6 %gather_fusion.2 = s32[512]{0:T(512)S(1)} fusion(s32[512]{0:T(512)} %bitcast.26, s32[1024]{0:T(1024)S(1)} %pad_clamp_fusion.4), kind=kCustom, calls=%fused_computation.2 | custom fusion | bytes 6144 | tf_op jit(solution)/shard_map/gather | solution.py:13
  15.3 7.0 %while.49 = (s32[]{:T(128)}, u32[8]{0:T(128)S(1)}, u32[8]{0:T(128)S(1)}, s32[512]{0:T(512)S(1)}, s32[]{:T(128)}, /*index=5*/s32[]{:T(128)}, s32[]{}) while((s32[]{:T(128)}, u32[8]{0:T(128)S(1)}, u32[8]{0:T(128)S(1)}, s32[512]{0:T(512)S(1)}, s32[]{:T(128)}, /*index=5*/s32[]{:T(128)}, s32[]{}) %tuple.66), condition=%wide.region_4.5_spmd.clone, body=%wide.region_3.4_spmd.clone.sunk | while | flops 1132 | bytes 4580 | solution.py:15
  15.4 0.6 gather_fusion.1
  16.1 0.6 gather_fusion.1
  16.8 0.6 gather_fusion.1
  17.5 0.6 gather_fusion.1
  18.2 0.6 gather_fusion.1
  18.9 0.6 gather_fusion.1
  19.6 0.6 gather_fusion.1
  20.3 0.6 gather_fusion.1
  21.0 0.6 gather_fusion.1
  21.7 0.6 gather_fusion.1
  22.4 7.0 %while.48 = (s32[]{:T(128)}, u32[8]{0:T(128)S(1)}, u32[8]{0:T(128)S(1)}, s32[512]{0:T(512)S(1)}, s32[]{:T(128)}, /*index=5*/s32[]{:T(128)}, s32[]{}) while((s32[]{:T(128)}, u32[8]{0:T(128)S(1)}, u32[8]{0:T(128)S(1)}, s32[512]{0:T(512)S(1)}, s32[]{:T(128)}, /*index=5*/s32[]{:T(128)}, s32[]{}) %tuple.74), condition=%wide.region_2.3_spmd.clone, body=%wide.region_1.2_spmd.clone.sunk | while | flops 1132 | bytes 4580 | solution.py:16
  22.4 0.6 gather_fusion
  23.1 0.6 gather_fusion
  23.8 0.6 gather_fusion
  24.5 0.6 gather_fusion
  25.2 0.6 gather_fusion
  25.9 0.6 gather_fusion
  26.6 0.6 gather_fusion
  27.3 0.6 gather_fusion
  28.0 0.6 gather_fusion
  28.7 0.6 gather_fusion
  29.4 0.1 compare_select_fusion.1
  29.5 0.1 reshape.195
  29.6 0.0 copy-start.1
  29.6 6.9 %gather_fusion.3 = s32[1056]{0:T(1024)S(1)} fusion(s32[512]{0:T(512)S(1)} %get-tuple-element.133, s32[2048]{0:T(1024)S(1)} %pad_clamp_fusion.3), kind=kCustom, calls=%fused_computation.3 | custom fusion | bytes 12672 | tf_op jit(solution)/shard_map/gather | solution.py:20
  36.6 0.1 gather.35
  36.7 0.1 reshape.203
  36.8 0.0 copy-done.1
  36.8 0.0 copy-start.2
  36.8 6.9 %gather_fusion.6 = s32[1056]{0:T(1024)S(1)} fusion(s32[512]{0:T(512)S(1)} %copy-done.1, s32[2048]{0:T(1024)S(1)} %pad_clamp_fusion.2), kind=kCustom, calls=%fused_computation.6 | custom fusion | bytes 12672 | tf_op jit(solution)/shard_map/gather | solution.py:21
  43.7 0.1 gather.40
  43.8 6.9 %gather_fusion.4 = s32[1056]{0:T(1024)S(1)} fusion(s32[512]{0:T(512)S(1)} %copy-done.2, s32[2048]{0:T(1024)S(1)} %pad_clamp_fusion.2), kind=kCustom, calls=%fused_computation.4 | custom fusion | bytes 12672 | tf_op jit(solution)/shard_map/gather | solution.py:22
  50.8 0.1 gather.37
  50.9 0.7 compare_select_fusion.2
  51.6 6.3 %all-to-all-start.2 = ((s32[8,1,132]{2,1,0:T(1,128)}), s32[8,1,132]{2,1,0:T(1,128)S(1)}, u32[]{:S(2)}, u32[]{:S(2)}) async-start(s32[8,1,132]{2,1,0:T(1,128)} %get-tuple-element.192), calls=%async_computation.2 | async-start | bytes 16384 | tf_op jit(solution)/shard_map/all_to_all | solution.py:30
  57.9 0.1 reshape.218
  58.0 0.1 select_convert_fusion
  58.0 0.0 copy-done
  58.0 4.1 %gather_fusion.5 = bf16[1056,256]{1,0:T(8,128)(2,1)S(1)} fusion(bf16[512,256]{1,0:T(8,128)(2,1)S(1)} %bitcast.24, s32[2048]{0:T(1024)S(1)} %pad_clamp_fusion.2), kind=kCustom, calls=%fused_computation.5 | custom fusion | bytes 1085568 | tf_op jit(solution)/shard_map/gather | solution.py:23
  62.2 0.1 reshape.237
  62.3 1.2 all-to-all-done.2
  63.5 3.9 %all-to-all-start = ((s32[8,1,132]{2,1,0:T(1,128)}), s32[8,1,132]{2,1,0:T(1,128)S(1)}, u32[]{:S(2)}, u32[]{:S(2)}) async-start(s32[8,1,132]{2,1,0:T(1,128)} %get-tuple-element.193), calls=%async_computation | async-start | bytes 16384 | tf_op jit(solution)/shard_map/all_to_all | solution.py:29
  67.4 1.0 multiply_convert_fusion
  68.4 4.6 %all-to-all-done = s32[8,1,132]{2,1,0:T(1,128)S(1)} async-done(((s32[8,1,132]{2,1,0:T(1,128)}), s32[8,1,132]{2,1,0:T(1,128)S(1)}, u32[]{:S(2)}, u32[]{:S(2)}) %all-to-all-start) | async-done | bytes 4256 | tf_op jit(solution)/shard_map/all_to_all | solution.py:29
  73.0 3.5 %all-to-all-start.1 = ((bf16[8,132,256]{2,1,0:T(8,128)(2,1)}), bf16[8,132,256]{2,1,0:T(8,128)(2,1)S(1)}, u32[]{:S(2)}, u32[]{:S(2)}) async-start(bf16[8,132,256]{2,1,0:T(8,128)(2,1)} %multiply_convert_fusion), calls=%async_computation.1 | async-start | bytes 1114112 | tf_op jit(solution)/shard_map/all_to_all | solution.py:28
  76.6 0.2 reduce-scatter.2.cloned.1.call-start
  76.8 0.1 convert_element_type.50
  76.9 0.1 eq.16
  77.0 1.3 select_reduce_fusion
  78.3 14.2 %all-to-all-done.1 = bf16[8,132,256]{2,1,0:T(8,128)(2,1)S(1)} async-done(((bf16[8,132,256]{2,1,0:T(8,128)(2,1)}), bf16[8,132,256]{2,1,0:T(8,128)(2,1)S(1)}, u32[]{:S(2)}, u32[]{:S(2)}) %all-to-all-start.1) | async-done | bytes 540704 | tf_op jit(solution)/shard_map/all_to_all | solution.py:28
  92.5 0.1 reshape.167
  92.6 2.2 %fusion.15 = f32[2048,256]{0,1:T(8,128)S(1)} fusion(bf16[1056,256]{1,0:T(8,128)(2,1)S(1)} %reshape.167, s32[1056]{0:T(1024)S(1)} %eq.16, f32[2048]{0:T(1024)S(1)} %broadcast_maximum_fusion), kind=kOutput, calls=%fused_computation.33 | convolution fusion | flops 1109983232 | bytes 2650240 | tf_op jit(solution)/shard_map/dot_general | solution.py:41
  94.8 0.2 fusion.22
  95.0 1.5 maximum_bitcast_fusion
  96.5 23.3 %fusion.16 = f32[1024,2,128]{0,2,1:T(8,128)} fusion(f32[1,2,2,2048,1024]{4,3,2,1,0:T(8,128)} %param.13, f32[1,2048,2,128]{1,3,0,2:T(8,128)} %maximum_bitcast_fusion, f32[1,2048,2,128]{1,3,0,2:T(8,128)S(1)} %bitcast.28), kind=kOutput, calls=%fused_computation.34 | convolution fusion | flops 12885950464 | bytes 38797312 | tf_op jit(solution)/shard_map/mrbk,rbmc->kmc/dot_general | solution.py:50
  119.7 0.0 reduce-scatter.2.cloned.1.call-update
  119.8 31.4 %reduce-scatter.2.cloned.1.call-done = f32[128,2,128]{0,2,1:T(8,128)} async-done(((f32[1024,2,128]{0,2,1:T(8,128)}), f32[128,2,128]{0,2,1:T(8,128)}) %reduce-scatter.2.cloned.1.call-update) | async-done | bytes 131088 | tf_op jit(solution)/shard_map/reduce_scatter | solution.py:49
  151.2 0.9 multiply_reduce_fusion
  152.1 10.0 %psum.7 = f32[128,2]{0,1:T(2,128)S(1)} all-reduce(f32[128,2]{0,1:T(2,128)S(1)} %multiply_reduce_fusion), channel_id=1, replica_groups=mesh['chan'=4,'pair'=8] {'chan'}, use_global_device_ids=true, to_apply=%region_8.9 | all-reduce | flops 256 | bytes 2048 | tf_op jit(solution)/shard_map/psum | solution.py:62
  162.1 0.6 broadcast_multiply_fusion
  (76 shorter events, 0.7 us)
Async XLA Ops:
  7.2 50.9 %copy-start = (bf16[1,512,256]{2,1,0:T(8,128)(2,1)S(1)}, bf16[1,512,256]{2,1,0:T(8,128)(2,1)}, u32[]{:S(2)}) copy-start(bf16[1,512,256]{2,1,0:T(8,128)(2,1)} %param.9) | copy-start | bytes 786436
  29.6 7.2 %copy-start.1 = (s32[512]{0:T(512)S(1)}, s32[512]{0:T(512)}, u32[]{:S(2)}) copy-start(s32[512]{0:T(512)} %param.10) | copy-start | bytes 6148
  36.8 7.1 %copy-start.2 = (s32[512]{0:T(512)S(1)}, s32[512]{0:T(512)}, u32[]{:S(2)}) copy-start(s32[512]{0:T(512)} %param.12) | copy-start | bytes 6148
  51.6 11.9 %all-to-all-start.2 = ((s32[8,1,132]{2,1,0:T(1,128)}), s32[8,1,132]{2,1,0:T(1,128)S(1)}, u32[]{:S(2)}, u32[]{:S(2)}) async-start(s32[8,1,132]{2,1,0:T(1,128)} %get-tuple-element.192), calls=%async_computation.2 | async-start | bytes 16384 | tf_op jit(solution)/shard_map/all_to_all | solution.py:30
  63.5 9.5 %all-to-all-start = ((s32[8,1,132]{2,1,0:T(1,128)}), s32[8,1,132]{2,1,0:T(1,128)S(1)}, u32[]{:S(2)}, u32[]{:S(2)}) async-start(s32[8,1,132]{2,1,0:T(1,128)} %get-tuple-element.193), calls=%async_computation | async-start | bytes 16384 | tf_op jit(solution)/shard_map/all_to_all | solution.py:29
  73.0 19.5 %all-to-all-start.1 = ((bf16[8,132,256]{2,1,0:T(8,128)(2,1)}), bf16[8,132,256]{2,1,0:T(8,128)(2,1)S(1)}, u32[]{:S(2)}, u32[]{:S(2)}) async-start(bf16[8,132,256]{2,1,0:T(8,128)(2,1)} %multiply_convert_fusion), calls=%async_computation.1 | async-start | bytes 1114112 | tf_op jit(solution)/shard_map/all_to_all | solution.py:28
  76.6 74.6 %reduce-scatter.2.cloned.1.call-start = ((), (), s32[]{:S(2)}) async-start(), calls=%async_computation.4 | async-start | bytes 1179648 | tf_op jit(solution)/shard_map/reduce_scatter | solution.py:49
Sparse Core Ops, SparseCore 0:
  119.9 31.2 reduce-scatter.1
where the time goes:
time: 170 us
  waiting for transfers between devices  51.5 us (30%)
  local copies, waits for them, and re-layouts  42.4 us (25%)
  matrix products  25.4 us (15%)
  between operations  14.3 us (8%)
  starting transfers between devices  14 us (8%)
  other arithmetic  11.4 us (7%)
  blocking collectives  9.97 us (6%)
    reduce_scatter x1, waiting for transfers between devices, per_device(): lax.psum_scatter(jnp.einsum('mrbk,rbmc->kmc', beam_local, right, precisio...  31.4 us
    dot_general x1, matrix products, per_device(): jnp.einsum('mrbk,rbmc->kmc', beam_local, right, precision=lax.Precision.H...  23.3 us
    all_to_all x1, waiting for transfers between devices, per_device(): lax.all_to_all(weighted, 'pair', split_axis=0, concat_axis=0, tiled=True)  14.2 us
    psum x1, blocking collectives, per_device(): total_power = lax.psum(power_local, 'chan')  9.97 us
    gather x3, local copies, waits for them, and re-layouts, per_device(): weights = jnp.where(valid, pair_counts[picked], 0)  7.11 us
    gather x2, local copies, waits for them, and re-layouts, per_device(): offsets = jnp.where(valid, slot_ids[picked], 0)  7.03 us
    gather x2, local copies, waits for them, and re-layouts, per_device(): picked = order[where_at]  7.02 us
    gather x10, local copies, waits for them, and re-layouts, per_device(): first_at = jnp.searchsorted(sorted_owner, owner_list, side='left')  6.46 us
  transfers between devices with their start and end apart: 4, of which 4 were waited for; matrix products, arithmetic and copies ran while one was open for 4% of the time, Pallas kernels for 0%

commit v1 on v0

--- a/solution.py
+++ b/solution.py
@@ -1,10 +1,249 @@
+import functools
+
 import jax
 import jax.numpy as jnp
 from jax import lax
+from jax.experimental import pallas as pl
+from jax.experimental.pallas import tpu as pltpu
 from jax.sharding import PartitionSpec as P
 
-
-def per_device(visibility, pair_counts, owner_ids, slot_ids, beam):
+MIB = 1 << 20
+
+
+def round_up(value, unit):
+    return -(-value // unit) * unit
+
+
+def block_rows(capacity):
+    first = capacity if capacity % 8 <= 5 else round_up(capacity, 8)
+    return first, round_up(first + 3, 8)
+
+
+def swap(value, axis, distance):
+    size = lax.axis_size(axis)
+    return lax.ppermute(value, axis, [(i, i ^ distance) for i in range(size)])
+
+
+def pack_kernel(peers, capacity, vis_ref, counts_ref, owner_ref, slot_ref, mine_ref, theirs_ref):
+    rows, columns = vis_ref.shape
+    first, size = block_rows(capacity)
+    padded = round_up(size, 16)
+    me = lax.axis_index("pair")
+    relative = owner_ref[...] ^ me
+    hot = lax.broadcasted_iota(jnp.int32, (peers, rows), 0) == relative
+    earlier = lax.broadcasted_iota(jnp.int32, (rows, rows), 0) < lax.broadcasted_iota(
+        jnp.int32, (rows, rows), 1
+    )
+    counted = jnp.dot(
+        jnp.where(hot, 1.0, 0.0).astype(jnp.bfloat16),
+        jnp.where(earlier, 1.0, 0.0).astype(jnp.bfloat16),
+        preferred_element_type=jnp.float32,
+    )
+    rank = jnp.sum(jnp.where(hot, counted, 0.0), axis=0, keepdims=True).astype(jnp.int32)
+    slot = slot_ref[...]
+    weight = counts_ref[...].astype(jnp.float32)
+    line = lax.broadcasted_iota(jnp.int32, (8, rows), 0)
+    facts = jnp.where(
+        line == first % 8,
+        (slot >> 8).astype(jnp.float32),
+        jnp.where(
+            line == first % 8 + 1,
+            (slot & 255).astype(jnp.float32),
+            jnp.where(line == first % 8 + 2, weight, 0.0),
+        ),
+    ).astype(jnp.bfloat16)
+    places = lax.broadcasted_iota(jnp.int32, (columns, rows), 0)
+    beyond = (lax.broadcasted_iota(jnp.int32, (8, columns), 0) == first % 8) & (
+        lax.broadcasted_iota(jnp.int32, (8, columns), 1) >= capacity
+    )
+    for j in range(peers):
+        match = places == jnp.where(relative == j, rank, -1)
+        named = dot_rows(facts, jnp.where(match, 1.0, 0.0).astype(jnp.bfloat16))
+        named = jnp.where(beyond, 255.0, named)
+        scaled = jnp.where(match[:padded], weight, 0.0).astype(jnp.bfloat16)
+        body = jnp.dot(scaled, vis_ref[...], preferred_element_type=jnp.float32)
+        block = jnp.concatenate([body[: size - 8], body[size - 8 : size] + named], axis=0)
+        out_ref = theirs_ref if j % 2 else mine_ref
+        out_ref[j // 2] = block.astype(jnp.bfloat16)
+
+
+def dot_rows(left, right):
+    return lax.dot_general(
+        left, right, (((1,), (1,)), ((), ())), preferred_element_type=jnp.float32
+    )
+
+
+def load_kernel(chunk, beam_ref, after_ref, high_ref, low_ref, buffer, sems):
+    steps = beam_ref.shape[0] // chunk
+    slots = buffer.shape[0]
+
+    def copy(step):
+        return pltpu.make_async_copy(
+            beam_ref.at[pl.ds(step * chunk, chunk)],
+            buffer.at[step % slots],
+            sems.at[step % slots],
+        )
+
+    for step in range(min(slots, steps)):
+        copy(step).start()
+    for step in range(steps):
+        copy(step).wait()
+
+        @pl.loop(0, chunk // 32)
+        def _(i):
+            at = pl.multiple_of(i * 32, 32)
+            value = buffer[step % slots, pl.ds(at, 32)]
+            high = value.astype(jnp.bfloat16)
+            high_ref[pl.ds(step * chunk + at, 32)] = high
+            low_ref[pl.ds(step * chunk + at, 32)] = (value - high.astype(jnp.float32)).astype(
+                jnp.bfloat16
+            )
+
+        if step + slots < steps:
+            copy(step + slots).start()
+
+
+def project_kernel(peers, capacity, mwin, *refs):
+    pieces = refs[: peers // 2]
+    high_ref, low_ref, keep_ref, send_ref, left_ref, total_ref = refs[peers // 2 :]
+    first, size = block_rows(capacity)
+    columns = pieces[0].shape[1]
+    base_dev, modes = high_ref.shape[1:]
+    half = columns // (2 * mwin)
+    tile = 512 if base_dev % 512 == 0 else base_dev
+    rows, slots, weights = [], [], []
+    for piece in pieces:
+        values = piece[...].astype(jnp.float32)
+        rows.append(values)
+        for b in range(2):
+            facts = values[(b + 1) * size - 8 : (b + 1) * size].T[:size]
+            high = facts[:, first % 8 : first % 8 + 1]
+            low = facts[:, first % 8 + 1 : first % 8 + 2]
+            slots.append((high * 256.0 + low).astype(jnp.int32))
+            weights.append(jnp.broadcast_to(facts[:, first % 8 + 2 : first % 8 + 3], (size, 128)))
+    rows = jnp.concatenate(rows, axis=0).T
+    weights = jnp.concatenate(weights, axis=0).T[:16]
+    slots = jnp.concatenate(slots, axis=0)
+    left = jnp.concatenate([rows, weights], axis=0).astype(jnp.bfloat16)
+    places = lax.broadcasted_iota(jnp.int32, (slots.shape[0], tile), 1)
+    for n in range(base_dev // tile):
+        match = jnp.where(places == slots - n * tile, 1.0, 0.0).astype(jnp.bfloat16)
+        sums = jnp.dot(left, match, preferred_element_type=jnp.float32)
+        stacked = sums[:columns] / jnp.maximum(sums[columns : columns + 1], 1.0)
+        at_n = slice(n * tile, (n + 1) * tile)
+        for m in range(mwin):
+            at = 2 * half * m
+            real, imag = stacked[at : at + half], stacked[at + half : at + 2 * half]
+            for r, value in enumerate((stacked[at : at + 2 * half], (imag, -real))):
+                if r:
+                    value = jnp.concatenate(value, axis=0)
+                high = value.astype(jnp.bfloat16)
+                low = (value - high.astype(jnp.float32)).astype(jnp.bfloat16)
+                left_ref[m, r, : 2 * half, at_n] = high
+                left_ref[m, r, 2 * half :, at_n] = low
+    for m in range(mwin):
+        total = None
+        for r in range(2):
+            both = jnp.dot(
+                left_ref[m, r], high_ref[2 * m + r], preferred_element_type=jnp.float32
+            )
+            rest = jnp.dot(
+                left_ref[m, r, : 2 * half], low_ref[2 * m + r], preferred_element_type=jnp.float32
+            )
+            term = both[: 2 * half] + (both[2 * half :] + rest)
+            total = term if total is None else total + term
+        total_ref[2 * half * m : 2 * half * (m + 1)] = total
+    me = lax.axis_index("pair")
+    width = modes // peers
+    for k in range(peers // 2):
+        at = pl.multiple_of((me ^ (2 * k)) * width, width)
+        keep_ref[k] = total_ref[:, pl.ds(at, width)]
+        at = pl.multiple_of((me ^ (2 * k + 1)) * width, width)
+        send_ref[k] = total_ref[:, pl.ds(at, width)]
+
+
+def staged(visibility, pair_counts, owner_ids, slot_ids, beam):
+    peers = lax.axis_size("pair")
+    chips = peers // 2
+    rows, columns = visibility.shape[1:]
+    capacity = 2 * rows // peers + 4
+    mwin, _, base_dev, modes = beam.shape[1:]
+    width = modes // peers
+    _, size = block_rows(capacity)
+    vmem = pl.BlockSpec(memory_space=pltpu.VMEM)
+    anywhere = pl.BlockSpec(memory_space=pl.ANY)
+    block = jax.ShapeDtypeStruct((chips, size, columns), jnp.bfloat16)
+    mine, theirs = pl.pallas_call(
+        functools.partial(pack_kernel, peers, capacity),
+        out_shape=(block, block),
+        in_specs=[vmem] * 4,
+        out_specs=(vmem, vmem),
+        compiler_params=pltpu.CompilerParams(vmem_limit_bytes=8 * MIB),
+        name="pack",
+    )(
+        visibility[0],
+        pair_counts.reshape(1, rows),
+        owner_ids.reshape(1, rows),
+        slot_ids.reshape(1, rows),
+    )
+    got = swap(theirs, "pair", 1)
+    pieces = [jnp.concatenate([mine[k], got[k]], axis=0) for k in range(chips)]
+    moved = {k: swap(pieces[k], "pair", 2 * k) for k in reversed(range(1, chips))}
+    chunk = 512
+    planes = beam.reshape(mwin * 2 * base_dev, modes)
+    held = pl.pallas_call(
+        functools.partial(load_kernel, chunk),
+        out_shape=(pltpu.VMEM(planes.shape, jnp.bfloat16),) * 2,
+        in_specs=[anywhere, anywhere],
+        out_specs=(vmem, vmem),
+        scratch_shapes=[
+            pltpu.VMEM((4, chunk, modes), jnp.float32),
+            pltpu.SemaphoreType.DMA((4,)),
+        ],
+        compiler_params=pltpu.CompilerParams(vmem_limit_bytes=12 * MIB),
+        cost_estimate=pl.CostEstimate(
+            flops=0, bytes_accessed=8 * planes.size, transcendentals=0
+        ),
+        name="load",
+    )(planes, pieces[0])
+    held = [
+        pltpu.with_memory_space_constraint(
+            part.reshape(mwin * 2, base_dev, modes), pltpu.VMEM
+        )
+        for part in held
+    ]
+    keep, send = pl.pallas_call(
+        functools.partial(project_kernel, peers, capacity, mwin),
+        out_shape=(
+            jax.ShapeDtypeStruct((chips, columns, width), jnp.float32),
+            jax.ShapeDtypeStruct((chips, columns, width), jnp.float32),
+        ),
+        in_specs=[vmem] * (chips + 2),
+        out_specs=(vmem, vmem),
+        scratch_shapes=[
+            pltpu.VMEM((mwin, 2, 2 * columns // mwin, base_dev), jnp.bfloat16),
+            pltpu.VMEM((columns, modes), jnp.float32),
+        ],
+        compiler_params=pltpu.CompilerParams(vmem_limit_bytes=14 * MIB),
+        name="project",
+    )(pieces[0], *[moved[k] for k in range(1, chips)], *held)
+    summed = keep + swap(send, "pair", 1)
+    amplitudes = summed[0]
+    for k in reversed(range(1, chips)):
+        value = summed[k] if k == 1 else summed[k].astype(jnp.bfloat16)
+        amplitudes = amplitudes + swap(value, "pair", 2 * k).astype(jnp.float32)
+    sets = columns // (2 * mwin)
+    power = jnp.sum((amplitudes * amplitudes).reshape(mwin, 2 * sets, width), axis=1)
+    distance = 1
+    while distance < lax.axis_size("chan"):
+        power = power + swap(power, "chan", distance)
+        distance *= 2
+    power = power / (lax.axis_size("chan") * sets)
+    shaped = amplitudes.reshape(mwin, 2, sets, width).transpose(3, 0, 1, 2)
+    return shaped[None], power.T
+
+
+def plain(visibility, pair_counts, owner_ids, slot_ids, beam):
     peers = lax.axis_size("pair")
     pair_rows = pair_counts.shape[0]
     capacity = 2 * pair_rows // peers + 4
@@ -42,9 +281,7 @@
     denom = jnp.sum(jnp.where(matches, got_weights[None, :], 0.0), axis=1)
     stacked = numer / jnp.maximum(denom, 1.0)[:, None]
     stacked = stacked.reshape(base_dev, mwin, 2 * sets)
-    real_part = stacked[:, :, :sets]
-    imag_part = stacked[:, :, sets:]
-    swapped = jnp.concatenate([imag_part, -real_part], axis=2)
+    swapped = jnp.concatenate([stacked[:, :, sets:], -stacked[:, :, :sets]], axis=2)
     right = jnp.stack([stacked, swapped], axis=0)
     amplitudes = lax.psum_scatter(
         jnp.einsum(
@@ -65,6 +302,29 @@
     return (shaped[None], mode_power)
 
 
+def power_of_two(value):
+    return value & (value - 1) == 0
+
+
+def per_device(visibility, pair_counts, owner_ids, slot_ids, beam):
+    peers, channels = lax.axis_size("pair"), lax.axis_size("chan")
+    rows, columns = visibility.shape[1:]
+    mwin, _, base_dev, modes = beam.shape[1:]
+    capacity = 2 * rows // peers + 4
+    fits = (
+        1 < peers <= 8
+        and power_of_two(peers)
+        and power_of_two(channels)
+        and rows % 128 == 0
+        and columns % 128 == 0
+        and capacity + 8 <= columns
+        and base_dev % 512 == 0
+        and modes % (128 * peers) == 0
+        and columns % (32 * mwin) == 0
+    )
+    return (staged if fits else plain)(visibility, pair_counts, owner_ids, slot_ids, beam)
+
+
 def solution(mesh):
     in_specs = (
         P("chan", "pair", None),

time: 170 us -> 55.4 us (0.33)
  local copies, waits for them, and re-layouts: 42.4 us -> 3.04 us
  waiting for transfers between devices: 51.5 us -> 14.2 us
  matrix products: 25.4 us -> 0 us
  Pallas kernels: 0 us -> 21.9 us
  between operations: 14.3 us -> 0.76 us
  other arithmetic: 11.4 us -> 1.38 us
  blocking collectives: 9.97 us -> 0 us
    gather x29 -> x0, local copies, waits for them, and re-layouts: 41.8 us -> none  [the longest x3 7.11 us: per_device(): weights = jnp.where(valid, pair_counts[picked], 0)]
    reduce_scatter x1 -> x0, waiting for transfers between devices: 31.4 us -> none  [per_device(): lax.psum_scatter(jnp.einsum('mrbk,rbmc->kmc', beam_local, right, precisio...]
    dot_general x2 -> x0, matrix products: 25.4 us -> none  [the longest x1 23.3 us: per_device(): jnp.einsum('mrbk,rbmc->kmc', beam_local, right, precision=lax.Precision.H...]
    pallas_call x0 -> x3, Pallas kernels: none -> 21.9 us  [the longest x1 11.2 us: staged(): pl.pallas_call(functools.partial(load_kernel, chunk), out_shape=(pltpu.VM...]
    all_to_all x3 -> x0, waiting for transfers between devices: 20 us -> none  [the longest x1 14.2 us: per_device(): lax.all_to_all(weighted, 'pair', split_axis=0, concat_axis=0, tiled=True)]
    ppermute x0 -> x10, waiting for transfers between devices: none -> 14.2 us  [swap(): return lax.ppermute(value, axis, [(i, i ^ distance) for i in range(size)])]
    ppermute x0 -> x10, starting transfers between devices: none -> 13.9 us  [swap(): return lax.ppermute(value, axis, [(i, i ^ distance) for i in range(size)])]
    all_to_all x3 -> x0, starting transfers between devices: 13.8 us -> none  [the longest x1 6.33 us: per_device(): lax.all_to_all(weights, 'pair', split_axis=0, concat_axis=0, tiled=True)]
  transfers between devices with their start and end apart: 4 -> 10, of which waited for: 4 -> 6; matrix products, arithmetic and copies ran while one was open for 4% -> 0% of each run, Pallas kernels for 0% -> 20%
where the time goes in v1:
time: 55.4 us; the launch traced here: 55.2 us
  Pallas kernels  21.9 us (40%)
  waiting for transfers between devices  14.2 us (26%)
  starting transfers between devices  13.9 us (25%)
  local copies, waits for them, and re-layouts  3.04 us (5%)
  other arithmetic  1.38 us (2%)
  between operations  0.76 us (1%)
    ppermute x10, waiting for transfers between devices, swap(): return lax.ppermute(value, axis, [(i, i ^ distance) for i in range(size)])  14.2 us
    ppermute x10, starting transfers between devices, swap(): return lax.ppermute(value, axis, [(i, i ^ distance) for i in range(size)])  13.9 us
    pallas_call x1, Pallas kernels, staged(): pl.pallas_call(functools.partial(load_kernel, chunk), out_shape=(pltpu.VM...  11.2 us
    pallas_call x1, Pallas kernels, staged(): pl.pallas_call(functools.partial(project_kernel, peers, capacity, mwin),...  9.43 us
    unnamed x8, local copies, waits for them, and re-layouts  2.99 us
    pallas_call x1, Pallas kernels, staged(): pl.pallas_call(functools.partial(pack_kernel, peers, capacity), out_shape...  1.2 us
  transfers between devices with their start and end apart: 10, of which 6 were waited for; matrix products, arithmetic and copies ran while one was open for 0% of the time, Pallas kernels for 20%

profile of v1, /device:TPU:0, one launch (start us, length us, event | category | flops | bytes accessed | tf_op | source)
XLA Modules:
  0.0 55.2 jit_solution(9672074932505880873)
XLA Ops:
  0.6 0.0 copy-start
  0.6 0.9 %copy-done = bf16[1,512,256]{2,1,0:T(8,128)(2,1)S(1)} copy-done((bf16[1,512,256]{2,1,0:T(8,128)(2,1)S(1)}, bf16[1,512,256]{2,1,0:T(8,128)(2,1)}, u32[]{:S(2)}) %copy-start) | copy-done | bytes 262168
  1.6 0.0 copy-start.1
  1.6 0.7 %copy-done.1 = s32[512]{0:T(512)S(1)} copy-done((s32[512]{0:T(512)S(1)}, s32[512]{0:T(512)}, u32[]{:S(2)}) %copy-start.1) | copy-done | bytes 2072
  2.3 0.0 copy-start.2
  2.3 0.7 %copy-done.2 = s32[512,1]{0,1:T(1,128)S(1)} copy-done((s32[512,1]{0,1:T(1,128)S(1)}, s32[512,1]{0,1:T(1,128)}, u32[]{:S(2)}) %copy-start.2) | copy-done | bytes 2072
  2.9 0.0 copy-start.3
  2.9 0.7 %copy-done.3 = s32[512]{0:T(512)S(1)} copy-done((s32[512]{0:T(512)S(1)}, s32[512]{0:T(512)}, u32[]{:S(2)}) %copy-start.3) | copy-done | bytes 2072
  3.6 1.2 %pack.1 = (bf16[4,136,256]{2,1,0:T(8,128)(2,1)S(1)}, bf16[4,136,256]{2,1,0:T(8,128)(2,1)S(1)}) custom-call(bf16[512,256]{1,0:T(8,128)(2,1)S(1)} %bitcast.49, s32[1,512]{1,0:T(1,128)S(1)} %bitcast.50, s32[1,512]{1,0:T(1,128)S(1)} %bitcast.51, s32[1,512]{1,0:T(1,128)S(1)} %bitcast.52), custom_call_target="tpu_custom_call" | custom-call | tf_op jit(solution)/shard_map/pack/pallas_call | solution.py:176
  4.8 0.5 collective-permute-start
  5.4 1.2 %collective-permute-done = bf16[4,136,256]{2,1,0:T(8,128)(2,1)S(1)} collective-permute-done((bf16[4,136,256]{2,1,0:T(8,128)(2,1)S(1)}, bf16[4,136,256]{2,1,0:T(8,128)(2,1)S(1)}, u32[]{:S(2)}, u32[]{:S(2)}) %collective-permute-start) | collective-permute-done | bytes 278560 | tf_op jit(solution)/shard_map/ppermute | solution.py:24
  6.6 3.0 %collective-permute-start.1 = (bf16[272,256]{1,0:T(8,128)(2,1)S(1)}, bf16[272,256]{1,0:T(8,128)(2,1)S(1)}, u32[]{:S(2)}, u32[]{:S(2)}) collective-permute-start(bf16[272,256]{1,0:T(8,128)(2,1)S(1)} %pad_maximum_fusion.1), channel_id=1, source_target_pairs={{0,2},{1,3},{2,0},{3,1},{4,6},{5,7},{6,4},{7,5},{8,10},{9,11},{10,... | collective-permute-start | bytes 417800 | tf_op jit(solution)/shard_map/ppermute | solution.py:24
  9.6 2.7 %collective-permute-start.2 = (bf16[272,256]{1,0:T(8,128)(2,1)S(1)}, bf16[272,256]{1,0:T(8,128)(2,1)S(1)}, u32[]{:S(2)}, u32[]{:S(2)}) collective-permute-start(bf16[272,256]{1,0:T(8,128)(2,1)S(1)} %pad_maximum_fusion.2), channel_id=1, source_target_pairs={{0,4},{1,5},{2,6},{3,7},{4,0},{5,1},{6,2},{7,3},{8,12},{9,13},{10,... | collective-permute-start | bytes 417800 | tf_op jit(solution)/shard_map/ppermute | solution.py:24
  12.3 0.1 collective-permute-start.3
  12.4 11.2 %load.1 = (bf16[8192,1024]{1,0:T(8,128)(2,1)S(1)}, bf16[8192,1024]{1,0:T(8,128)(2,1)S(1)}) custom-call(f32[8192,1024]{1,0:T(8,128)} %bitcast.53, bf16[272,256]{1,0:T(8,128)(2,1)S(1)} %pad_maximum_fusion.after_ref.refs_0_), custom_call_target="tpu_custom_call" | custom-call | bytes 67108864 | tf_op jit(solution)/shard_map/load/pallas_call | solution.py:194
  23.6 0.0 collective-permute-done.1.refs_1_
  23.6 0.0 collective-permute-done.2.refs_2_
  23.6 0.0 collective-permute-done.3.refs_3_
  23.6 9.4 %project.1 = (f32[4,256,128]{2,1,0:T(8,128)S(1)}, f32[4,256,128]{2,1,0:T(8,128)S(1)}) custom-call(bf16[272,256]{1,0:T(8,128)(2,1)S(1)} %pad_maximum_fusion.after_ref.refs_0_, bf16[272,256]{1,0:T(8,128)(2,1)S(1)} %collective-permute-done.1.refs_1_, bf16[272,256]{1,0:T(8,128)(2,1)S(1)} %collective-permute-done.2.refs_2_, ...), custom_call_target="tpu_custom_call" | custom-call | tf_op jit(solution)/shard_map/project/pallas_call | solution.py:215
  33.1 0.1 collective-permute-start.4
  33.1 1.9 %collective-permute-done.4 = f32[4,256,128]{2,1,0:T(8,128)S(1)} collective-permute-done((f32[4,256,128]{2,1,0:T(8,128)S(1)}, f32[4,256,128]{2,1,0:T(8,128)S(1)}, u32[]{:S(2)}, u32[]{:S(2)}) %collective-permute-start.4) | collective-permute-done | bytes 524320 | tf_op jit(solution)/shard_map/ppermute | solution.py:24
  35.0 0.1 fusion.4
  35.1 2.0 %collective-permute-start.7 = (f32[256,128]{1,0:T(8,128)S(1)}, f32[256,128]{1,0:T(8,128)S(1)}, u32[]{:S(2)}, u32[]{:S(2)}) collective-permute-start(f32[256,128]{1,0:T(8,128)S(1)} %slice_bitcast_fusion), channel_id=1, source_target_pairs={{0,2},{1,3},{2,0},{3,1},{4,6},{5,7},{6,4},{7,5},{8,10},{9,11},{10,... | collective-permute-start | bytes 393224 | tf_op jit(solution)/shard_map/ppermute | solution.py:24
  37.1 2.5 %collective-permute-start.5 = (bf16[256,128]{1,0:T(8,128)(2,1)S(1)}, bf16[256,128]{1,0:T(8,128)(2,1)S(1)}, u32[]{:S(2)}, u32[]{:S(2)}) collective-permute-start(bf16[256,128]{1,0:T(8,128)(2,1)S(1)} %get-tuple-element.26), channel_id=1, source_target_pairs={{0,6},{1,7},{2,4},{3,5},{4,2},{5,3},{6,0},{7,1},{8,14},{9,15},{10,... | collective-permute-start | bytes 196616 | tf_op jit(solution)/shard_map/ppermute | solution.py:24
  39.7 0.1 collective-permute-start.6
  39.7 5.6 %collective-permute-done.5 = bf16[256,128]{1,0:T(8,128)(2,1)S(1)} collective-permute-done((bf16[256,128]{1,0:T(8,128)(2,1)S(1)}, bf16[256,128]{1,0:T(8,128)(2,1)S(1)}, u32[]{:S(2)}, u32[]{:S(2)}) %collective-permute-start.5) | collective-permute-done | bytes 65568 | tf_op jit(solution)/shard_map/ppermute | solution.py:24
  45.3 1.4 %collective-permute-done.6 = bf16[256,128]{1,0:T(8,128)(2,1)S(1)} collective-permute-done((bf16[256,128]{1,0:T(8,128)(2,1)S(1)}, bf16[256,128]{1,0:T(8,128)(2,1)S(1)}, u32[]{:S(2)}, u32[]{:S(2)}) %collective-permute-start.6) | collective-permute-done | bytes 65568 | tf_op jit(solution)/shard_map/ppermute | solution.py:24
  46.8 0.0 collective-permute-done.7
  46.8 0.7 %bitcast_reduce_fusion = (f32[2,128]{1,0:T(2,128)S(1)}, f32[256,128]{1,0:T(8,128)}) fusion(f32[256,128]{1,0:T(8,128)S(1)} %collective-permute-done.7, bf16[256,128]{1,0:T(8,128)(2,1)S(1)} %collective-permute-done.6, bf16[256,128]{1,0:T(8,128)(2,1)S(1)} %collective-permute-done.5, f32[4,256,128]{2,1,0:T(8,128)S(1)} %get-tuple-element.17), kind=kLoop, calls=%fused_computation.9 | loop fusion | flops 229120 | bytes 525312 | tf_op jit(solution)/shard_map/reduce_sum | solution.py:236
  47.5 1.5 %collective-permute-start.8 = (f32[2,128]{1,0:T(2,128)S(1)}, f32[2,128]{1,0:T(2,128)S(1)}, u32[]{:S(2)}, u32[]{:S(2)}) collective-permute-start(f32[2,128]{1,0:T(2,128)S(1)} %get-tuple-element.14), channel_id=1, source_target_pairs={{0,8},{8,0},{16,24},{24,16},{1,9},{9,1},{17,25},{25,17},{2,10},{10... | collective-permute-start | bytes 3080 | tf_op jit(solution)/shard_map/ppermute | solution.py:24
  49.0 2.1 %collective-permute-done.8 = f32[2,128]{1,0:T(2,128)S(1)} collective-permute-done((f32[2,128]{1,0:T(2,128)S(1)}, f32[2,128]{1,0:T(2,128)S(1)}, u32[]{:S(2)}, u32[]{:S(2)}) %collective-permute-start.8) | collective-permute-done | bytes 1056 | tf_op jit(solution)/shard_map/ppermute | solution.py:24
  51.0 1.5 %collective-permute-start.9 = (f32[2,128]{1,0:T(2,128)S(1)}, f32[2,128]{1,0:T(2,128)S(1)}, u32[]{:S(2)}, u32[]{:S(2)}) collective-permute-start(f32[2,128]{1,0:T(2,128)S(1)} %add.22), channel_id=1, source_target_pairs={{0,16},{8,24},{16,0},{24,8},{1,17},{9,25},{17,1},{25,9},{2,18},{10... | collective-permute-start | bytes 3080 | tf_op jit(solution)/shard_map/ppermute | solution.py:24
  52.6 2.0 %collective-permute-done.9 = f32[2,128]{1,0:T(2,128)S(1)} collective-permute-done((f32[2,128]{1,0:T(2,128)S(1)}, f32[2,128]{1,0:T(2,128)S(1)}, u32[]{:S(2)}, u32[]{:S(2)}) %collective-permute-start.9) | collective-permute-done | bytes 1056 | tf_op jit(solution)/shard_map/ppermute | solution.py:24
  54.6 0.6 %multiply_bitcast_fusion = f32[128,2]{0,1:T(2,128)} fusion(f32[2,128]{1,0:T(2,128)S(1)} %add.22, f32[2,128]{1,0:T(2,128)S(1)} %collective-permute-done.9), kind=kLoop, calls=%fused_computation.20 | loop fusion | flops 512 | bytes 3072 | tf_op jit(solution)/shard_map/transpose | solution.py:243
  (9 shorter events, 0.1 us)
Async XLA Ops:
  0.6 1.0 %copy-start = (bf16[1,512,256]{2,1,0:T(8,128)(2,1)S(1)}, bf16[1,512,256]{2,1,0:T(8,128)(2,1)}, u32[]{:S(2)}) copy-start(bf16[1,512,256]{2,1,0:T(8,128)(2,1)} %param.5) | copy-start | bytes 786436
  1.6 0.7 %copy-start.1 = (s32[512]{0:T(512)S(1)}, s32[512]{0:T(512)}, u32[]{:S(2)}) copy-start(s32[512]{0:T(512)} %param.6) | copy-start | bytes 6148
  2.3 0.7 %copy-start.2 = (s32[512,1]{0,1:T(1,128)S(1)}, s32[512,1]{0,1:T(1,128)}, u32[]{:S(2)}) copy-start(s32[512,1]{0,1:T(1,128)} %param.7) | copy-start | bytes 6148
  2.9 0.7 %copy-start.3 = (s32[512]{0:T(512)S(1)}, s32[512]{0:T(512)}, u32[]{:S(2)}) copy-start(s32[512]{0:T(512)} %param.8) | copy-start | bytes 6148
  4.8 1.7 %collective-permute-start = (bf16[4,136,256]{2,1,0:T(8,128)(2,1)S(1)}, bf16[4,136,256]{2,1,0:T(8,128)(2,1)S(1)}, u32[]{:S(2)}, u32[]{:S(2)}) collective-permute-start(bf16[4,136,256]{2,1,0:T(8,128)(2,1)S(1)} %get-tuple-element.9), channel_id=1, source_target_pairs={{0,1},{1,0},{2,3},{3,2},{4,5},{5,4},{6,7},{7,6},{8,9},{9,8},{10,11... | collective-permute-start | bytes 835592 | tf_op jit(solution)/shard_map/ppermute | solution.py:24
  6.6 17.0 %collective-permute-start.1 = (bf16[272,256]{1,0:T(8,128)(2,1)S(1)}, bf16[272,256]{1,0:T(8,128)(2,1)S(1)}, u32[]{:S(2)}, u32[]{:S(2)}) collective-permute-start(bf16[272,256]{1,0:T(8,128)(2,1)S(1)} %pad_maximum_fusion.1), channel_id=1, source_target_pairs={{0,2},{1,3},{2,0},{3,1},{4,6},{5,7},{6,4},{7,5},{8,10},{9,11},{10,... | collective-permute-start | bytes 417800 | tf_op jit(solution)/shard_map/ppermute | solution.py:24
  9.6 14.0 %collective-permute-start.2 = (bf16[272,256]{1,0:T(8,128)(2,1)S(1)}, bf16[272,256]{1,0:T(8,128)(2,1)S(1)}, u32[]{:S(2)}, u32[]{:S(2)}) collective-permute-start(bf16[272,256]{1,0:T(8,128)(2,1)S(1)} %pad_maximum_fusion.2), channel_id=1, source_target_pairs={{0,4},{1,5},{2,6},{3,7},{4,0},{5,1},{6,2},{7,3},{8,12},{9,13},{10,... | collective-permute-start | bytes 417800 | tf_op jit(solution)/shard_map/ppermute | solution.py:24
  12.3 11.4 %collective-permute-start.3 = (bf16[272,256]{1,0:T(8,128)(2,1)S(1)}, bf16[272,256]{1,0:T(8,128)(2,1)S(1)}, u32[]{:S(2)}, u32[]{:S(2)}) collective-permute-start(bf16[272,256]{1,0:T(8,128)(2,1)S(1)} %pad_maximum_fusion.3), channel_id=1, source_target_pairs={{0,6},{1,7},{2,4},{3,5},{4,2},{5,3},{6,0},{7,1},{8,14},{9,15},{10,... | collective-permute-start | bytes 417800 | tf_op jit(solution)/shard_map/ppermute | solution.py:24
  33.1 2.0 %collective-permute-start.4 = (f32[4,256,128]{2,1,0:T(8,128)S(1)}, f32[4,256,128]{2,1,0:T(8,128)S(1)}, u32[]{:S(2)}, u32[]{:S(2)}) collective-permute-start(f32[4,256,128]{2,1,0:T(8,128)S(1)} %get-tuple-element.13), channel_id=1, source_target_pairs={{0,1},{1,0},{2,3},{3,2},{4,5},{5,4},{6,7},{7,6},{8,9},{9,8},{10,11... | collective-permute-start | bytes 1572872 | tf_op jit(solution)/shard_map/ppermute | solution.py:24
  35.1 11.6 %collective-permute-start.7 = (f32[256,128]{1,0:T(8,128)S(1)}, f32[256,128]{1,0:T(8,128)S(1)}, u32[]{:S(2)}, u32[]{:S(2)}) collective-permute-start(f32[256,128]{1,0:T(8,128)S(1)} %slice_bitcast_fusion), channel_id=1, source_target_pairs={{0,2},{1,3},{2,0},{3,1},{4,6},{5,7},{6,4},{7,5},{8,10},{9,11},{10,... | collective-permute-start | bytes 393224 | tf_op jit(solution)/shard_map/ppermute | solution.py:24
  37.1 8.2 %collective-permute-start.5 = (bf16[256,128]{1,0:T(8,128)(2,1)S(1)}, bf16[256,128]{1,0:T(8,128)(2,1)S(1)}, u32[]{:S(2)}, u32[]{:S(2)}) collective-permute-start(bf16[256,128]{1,0:T(8,128)(2,1)S(1)} %get-tuple-element.26), channel_id=1, source_target_pairs={{0,6},{1,7},{2,4},{3,5},{4,2},{5,3},{6,0},{7,1},{8,14},{9,15},{10,... | collective-permute-start | bytes 196616 | tf_op jit(solution)/shard_map/ppermute | solution.py:24
  39.7 7.1 %collective-permute-start.6 = (bf16[256,128]{1,0:T(8,128)(2,1)S(1)}, bf16[256,128]{1,0:T(8,128)(2,1)S(1)}, u32[]{:S(2)}, u32[]{:S(2)}) collective-permute-start(bf16[256,128]{1,0:T(8,128)(2,1)S(1)} %get-tuple-element.27), channel_id=1, source_target_pairs={{0,4},{1,5},{2,6},{3,7},{4,0},{5,1},{6,2},{7,3},{8,12},{9,13},{10,... | collective-permute-start | bytes 196616 | tf_op jit(solution)/shard_map/ppermute | solution.py:24
  47.5 3.6 %collective-permute-start.8 = (f32[2,128]{1,0:T(2,128)S(1)}, f32[2,128]{1,0:T(2,128)S(1)}, u32[]{:S(2)}, u32[]{:S(2)}) collective-permute-start(f32[2,128]{1,0:T(2,128)S(1)} %get-tuple-element.14), channel_id=1, source_target_pairs={{0,8},{8,0},{16,24},{24,16},{1,9},{9,1},{17,25},{25,17},{2,10},{10... | collective-permute-start | bytes 3080 | tf_op jit(solution)/shard_map/ppermute | solution.py:24
  51.0 3.6 %collective-permute-start.9 = (f32[2,128]{1,0:T(2,128)S(1)}, f32[2,128]{1,0:T(2,128)S(1)}, u32[]{:S(2)}, u32[]{:S(2)}) collective-permute-start(f32[2,128]{1,0:T(2,128)S(1)} %add.22), channel_id=1, source_target_pairs={{0,16},{8,24},{16,0},{24,8},{1,17},{9,25},{17,1},{25,9},{2,18},{10... | collective-permute-start | bytes 3080 | tf_op jit(solution)/shard_map/ppermute | solution.py:24

commit v2 on v1

--- a/solution.py
+++ b/solution.py
@@ -24,7 +24,17 @@
     return lax.ppermute(value, axis, [(i, i ^ distance) for i in range(size)])
 
 
-def pack_kernel(peers, capacity, vis_ref, counts_ref, owner_ref, slot_ref, mine_ref, theirs_ref):
+def pack_kernel(peers, capacity, *refs):
+    sources, (mine_ref, theirs_ref), held, sems = refs[:4], refs[4:6], refs[6:10], refs[10]
+    copies = [
+        pltpu.make_async_copy(source, target, sems.at[i])
+        for i, (source, target) in enumerate(zip(sources, held))
+    ]
+    for copy in copies:
+        copy.start()
+    for copy in copies:
+        copy.wait()
+    vis_ref, counts_ref, owner_ref, slot_ref = held
     rows, columns = vis_ref.shape
     first, size = block_rows(capacity)
     padded = round_up(size, 16)
@@ -73,9 +83,12 @@
     )
 
 
-def load_kernel(chunk, beam_ref, after_ref, high_ref, low_ref, buffer, sems):
+def load_kernel(peers, chunk, beam_ref, after_ref, *refs):
+    outs, buffer, sems = (refs[:2], refs[2:4]), refs[4], refs[5]
     steps = beam_ref.shape[0] // chunk
     slots = buffer.shape[0]
+    width = beam_ref.shape[1] // peers
+    me = lax.axis_index("pair")
 
     def copy(step):
         return pltpu.make_async_copy(
@@ -92,23 +105,26 @@
         @pl.loop(0, chunk // 32)
         def _(i):
             at = pl.multiple_of(i * 32, 32)
-            value = buffer[step % slots, pl.ds(at, 32)]
-            high = value.astype(jnp.bfloat16)
-            high_ref[pl.ds(step * chunk + at, 32)] = high
-            low_ref[pl.ds(step * chunk + at, 32)] = (value - high.astype(jnp.float32)).astype(
-                jnp.bfloat16
-            )
+            for j in range(peers):
+                lane = pl.multiple_of((me ^ j) * width, width)
+                value = buffer[step % slots, pl.ds(at, 32), pl.ds(lane, width)]
+                high = value.astype(jnp.bfloat16)
+                low = (value - high.astype(jnp.float32)).astype(jnp.bfloat16)
+                high_ref, low_ref = outs[1 - j % 2]
+                to = (pl.ds(step * chunk + at, 32), slice(j // 2 * width, (j // 2 + 1) * width))
+                high_ref[to] = high
+                low_ref[to] = low
 
         if step + slots < steps:
             copy(step + slots).start()
 
 
-def project_kernel(peers, capacity, mwin, *refs):
+def stack_kernel(peers, capacity, mwin, *refs):
     pieces = refs[: peers // 2]
-    high_ref, low_ref, keep_ref, send_ref, left_ref, total_ref = refs[peers // 2 :]
+    high_ref, low_ref, left_ref, send_ref = refs[peers // 2 :]
     first, size = block_rows(capacity)
     columns = pieces[0].shape[1]
-    base_dev, modes = high_ref.shape[1:]
+    base_dev = left_ref.shape[3]
     half = columns // (2 * mwin)
     tile = 512 if base_dev % 512 == 0 else base_dev
     rows, slots, weights = [], [], []
@@ -141,25 +157,31 @@
                 low = (value - high.astype(jnp.float32)).astype(jnp.bfloat16)
                 left_ref[m, r, : 2 * half, at_n] = high
                 left_ref[m, r, 2 * half :, at_n] = low
+    project(left_ref, high_ref, low_ref, send_ref)
+
+
+def project(left_ref, high_ref, low_ref, out_ref):
+    mwin, _, rows, base_dev = left_ref.shape
+    half = rows // 2
+    chips, _, width = out_ref.shape
     for m in range(mwin):
         total = None
         for r in range(2):
+            plane = slice((2 * m + r) * base_dev, (2 * m + r + 1) * base_dev)
             both = jnp.dot(
-                left_ref[m, r], high_ref[2 * m + r], preferred_element_type=jnp.float32
+                left_ref[m, r], high_ref[plane], preferred_element_type=jnp.float32
             )
             rest = jnp.dot(
-                left_ref[m, r, : 2 * half], low_ref[2 * m + r], preferred_element_type=jnp.float32
+                left_ref[m, r, :half], low_ref[plane], preferred_element_type=jnp.float32
             )
-            term = both[: 2 * half] + (both[2 * half :] + rest)
+            term = both[:half] + (both[half:] + rest)
             total = term if total is None else total + term
-        total_ref[2 * half * m : 2 * half * (m + 1)] = total
-    me = lax.axis_index("pair")
-    width = modes // peers
-    for k in range(peers // 2):
-        at = pl.multiple_of((me ^ (2 * k)) * width, width)
-        keep_ref[k] = total_ref[:, pl.ds(at, width)]
-        at = pl.multiple_of((me ^ (2 * k + 1)) * width, width)
-        send_ref[k] = total_ref[:, pl.ds(at, width)]
+        for k in range(chips):
+            out_ref[k, m * half : (m + 1) * half] = total[:, k * width : (k + 1) * width]
+
+
+def keep_kernel(left_ref, high_ref, low_ref, keep_ref):
+    project(left_ref, high_ref, low_ref, keep_ref)
 
 
 def staged(visibility, pair_counts, owner_ids, slot_ids, beam):
@@ -173,29 +195,31 @@
     vmem = pl.BlockSpec(memory_space=pltpu.VMEM)
     anywhere = pl.BlockSpec(memory_space=pl.ANY)
     block = jax.ShapeDtypeStruct((chips, size, columns), jnp.bfloat16)
+    facts = [value.reshape(1, rows) for value in (pair_counts, owner_ids, slot_ids)]
     mine, theirs = pl.pallas_call(
         functools.partial(pack_kernel, peers, capacity),
         out_shape=(block, block),
-        in_specs=[vmem] * 4,
+        in_specs=[anywhere] * 4,
         out_specs=(vmem, vmem),
+        scratch_shapes=[pltpu.VMEM((rows, columns), jnp.bfloat16)]
+        + [pltpu.VMEM((1, rows), jnp.int32)] * 3
+        + [pltpu.SemaphoreType.DMA((4,))],
         compiler_params=pltpu.CompilerParams(vmem_limit_bytes=8 * MIB),
         name="pack",
-    )(
-        visibility[0],
-        pair_counts.reshape(1, rows),
-        owner_ids.reshape(1, rows),
-        slot_ids.reshape(1, rows),
-    )
+    )(*[pltpu.with_memory_space_constraint(value, pltpu.HBM) for value in (visibility[0], *facts)])
     got = swap(theirs, "pair", 1)
     pieces = [jnp.concatenate([mine[k], got[k]], axis=0) for k in range(chips)]
-    moved = {k: swap(pieces[k], "pair", 2 * k) for k in reversed(range(1, chips))}
+    order = [k for k in range(1, chips) if k & (chips // 2)] + [
+        k for k in range(1, chips) if not k & (chips // 2)
+    ]
+    moved = {k: swap(pieces[k], "pair", 2 * k) for k in order}
     chunk = 512
     planes = beam.reshape(mwin * 2 * base_dev, modes)
     held = pl.pallas_call(
-        functools.partial(load_kernel, chunk),
-        out_shape=(pltpu.VMEM(planes.shape, jnp.bfloat16),) * 2,
+        functools.partial(load_kernel, peers, chunk),
+        out_shape=(pltpu.VMEM((planes.shape[0], modes // 2), jnp.bfloat16),) * 4,
         in_specs=[anywhere, anywhere],
-        out_specs=(vmem, vmem),
+        out_specs=(vmem,) * 4,
         scratch_shapes=[
             pltpu.VMEM((4, chunk, modes), jnp.float32),
             pltpu.SemaphoreType.DMA((4,)),
@@ -206,30 +230,34 @@
         ),
         name="load",
     )(planes, pieces[0])
-    held = [
-        pltpu.with_memory_space_constraint(
-            part.reshape(mwin * 2, base_dev, modes), pltpu.VMEM
-        )
-        for part in held
-    ]
-    keep, send = pl.pallas_call(
-        functools.partial(project_kernel, peers, capacity, mwin),
+    held = [pltpu.with_memory_space_constraint(part, pltpu.VMEM) for part in held]
+    products = jax.ShapeDtypeStruct((chips, columns, width), jnp.float32)
+    flops = 6 * mwin * 2 * (columns // mwin) * base_dev * modes // 2
+    left, send = pl.pallas_call(
+        functools.partial(stack_kernel, peers, capacity, mwin),
         out_shape=(
-            jax.ShapeDtypeStruct((chips, columns, width), jnp.float32),
-            jax.ShapeDtypeStruct((chips, columns, width), jnp.float32),
+            pltpu.VMEM((mwin, 2, 2 * columns // mwin, base_dev), jnp.bfloat16),
+            products,
         ),
         in_specs=[vmem] * (chips + 2),
         out_specs=(vmem, vmem),
-        scratch_shapes=[
-            pltpu.VMEM((mwin, 2, 2 * columns // mwin, base_dev), jnp.bfloat16),
-            pltpu.VMEM((columns, modes), jnp.float32),
-        ],
-        compiler_params=pltpu.CompilerParams(vmem_limit_bytes=14 * MIB),
-        name="project",
-    )(pieces[0], *[moved[k] for k in range(1, chips)], *held)
-    summed = keep + swap(send, "pair", 1)
+        compiler_params=pltpu.CompilerParams(vmem_limit_bytes=12 * MIB),
+        cost_estimate=pl.CostEstimate(flops=flops, bytes_accessed=0, transcendentals=0),
+        name="stack",
+    )(pieces[0], *[moved[k] for k in order], *held[:2])
+    got = swap(send, "pair", 1)
+    keep = pl.pallas_call(
+        keep_kernel,
+        out_shape=products,
+        in_specs=[vmem] * 3,
+        out_specs=vmem,
+        compiler_params=pltpu.CompilerParams(vmem_limit_bytes=12 * MIB),
+        cost_estimate=pl.CostEstimate(flops=flops, bytes_accessed=0, transcendentals=0),
+        name="keep",
+    )(pltpu.with_memory_space_constraint(left, pltpu.VMEM), *held[2:])
+    summed = keep + got
     amplitudes = summed[0]
-    for k in reversed(range(1, chips)):
+    for k in order:
         value = summed[k] if k == 1 else summed[k].astype(jnp.bfloat16)
         amplitudes = amplitudes + swap(value, "pair", 2 * k).astype(jnp.float32)
     sets = columns // (2 * mwin)

time: 55.4 us -> 51.4 us (0.928)
  local copies, waits for them, and re-layouts: 3.04 us -> 0.06 us
  waiting for transfers between devices: 14.2 us -> 11.9 us
  Pallas kernels: 21.9 us -> 23.3 us
    unnamed x8 -> x0, local copies, waits for them, and re-layouts: 2.99 us -> none
    ppermute x10, waiting for transfers between devices: 14.2 us -> 11.9 us  [swap(): return lax.ppermute(value, axis, [(i, i ^ distance) for i in range(size)])]
    pallas_call x1, Pallas kernels: 1.2 us -> 2.2 us  [staged(): pl.pallas_call(functools.partial(pack_kernel, peers, capacity), out_shape...]
    pallas_call x2 -> x3, Pallas kernels: 20.6 us -> 21.1 us  [the longest x1 11.3 us: staged(): pl.pallas_call(functools.partial(load_kernel, peers, chunk), out_shape=(p...]
  transfers between devices with their start and end apart: 10 -> 10, of which waited for: 6 -> 5; matrix products, arithmetic and copies ran while one was open for 0% -> 0% of each run, Pallas kernels for 20% -> 29%
where the time goes in v2:
time: 51.4 us; the launch traced here: 51.2 us
  Pallas kernels  23.3 us (45%)
  starting transfers between devices  13.9 us (27%)
  waiting for transfers between devices  11.9 us (23%)
  other arithmetic  1.38 us (3%)
  between operations  0.75 us (1%)
    ppermute x10, starting transfers between devices, swap(): return lax.ppermute(value, axis, [(i, i ^ distance) for i in range(size)])  13.9 us
    ppermute x10, waiting for transfers between devices, swap(): return lax.ppermute(value, axis, [(i, i ^ distance) for i in range(size)])  11.9 us
    pallas_call x1, Pallas kernels, staged(): pl.pallas_call(functools.partial(load_kernel, peers, chunk), out_shape=(p...  11.3 us
    pallas_call x1, Pallas kernels, staged(): pl.pallas_call(functools.partial(stack_kernel, peers, capacity, mwin), ou...  6.38 us
    pallas_call x1, Pallas kernels, staged(): pl.pallas_call(keep_kernel, out_shape=products, in_specs=[vmem] * 3, out_...  3.39 us
    pallas_call x1, Pallas kernels, staged(): pl.pallas_call(functools.partial(pack_kernel, peers, capacity), out_shape...  2.2 us
  transfers between devices with their start and end apart: 10, of which 5 were waited for; matrix products, arithmetic and copies ran while one was open for 0% of the time, Pallas kernels for 29%

profile of v2, /device:TPU:0, one launch (start us, length us, event | category | flops | bytes accessed | tf_op | source)
XLA Modules:
  0.0 51.2 jit_solution(12074423840422587530)
XLA Ops:
  0.6 2.2 %pack.1 = (bf16[4,136,256]{2,1,0:T(8,128)(2,1)S(1)}, bf16[4,136,256]{2,1,0:T(8,128)(2,1)S(1)}) custom-call(bf16[512,256]{1,0:T(8,128)(2,1)} %bitcast.46, s32[1,512]{1,0:T(1,128)} %bitcast.48, s32[1,512]{1,0:T(1,128)} %bitcast.49, s32[1,512]{1,0:T(1,128)} %bitcast.50), custom_call_target="tpu_custom_call" | custom-call | tf_op jit(solution)/shard_map/pack/pallas_call | solution.py:199
  2.8 0.5 %collective-permute-start = (bf16[4,136,256]{2,1,0:T(8,128)(2,1)S(1)}, bf16[4,136,256]{2,1,0:T(8,128)(2,1)S(1)}, u32[]{:S(2)}, u32[]{:S(2)}) collective-permute-start(bf16[4,136,256]{2,1,0:T(8,128)(2,1)S(1)} %get-tuple-element.11), channel_id=1, source_target_pairs={{0,1},{1,0},{2,3},{3,2},{4,5},{5,4},{6,7},{7,6},{8,9},{9,8},{10,11... | collective-permute-start | bytes 835592 | tf_op jit(solution)/shard_map/ppermute | solution.py:24
  3.4 1.2 %collective-permute-done = bf16[4,136,256]{2,1,0:T(8,128)(2,1)S(1)} collective-permute-done((bf16[4,136,256]{2,1,0:T(8,128)(2,1)S(1)}, bf16[4,136,256]{2,1,0:T(8,128)(2,1)S(1)}, u32[]{:S(2)}, u32[]{:S(2)}) %collective-permute-start) | collective-permute-done | bytes 278560 | tf_op jit(solution)/shard_map/ppermute | solution.py:24
  4.6 4.0 %collective-permute-start.1 = (bf16[272,256]{1,0:T(8,128)(2,1)S(1)}, bf16[272,256]{1,0:T(8,128)(2,1)S(1)}, u32[]{:S(2)}, u32[]{:S(2)}) collective-permute-start(bf16[272,256]{1,0:T(8,128)(2,1)S(1)} %pad_maximum_fusion.1), channel_id=1, source_target_pairs={{0,4},{1,5},{2,6},{3,7},{4,0},{5,1},{6,2},{7,3},{8,12},{9,13},{10,... | collective-permute-start | bytes 417800 | tf_op jit(solution)/shard_map/ppermute | solution.py:24
  8.6 1.4 %collective-permute-start.2 = (bf16[272,256]{1,0:T(8,128)(2,1)S(1)}, bf16[272,256]{1,0:T(8,128)(2,1)S(1)}, u32[]{:S(2)}, u32[]{:S(2)}) collective-permute-start(bf16[272,256]{1,0:T(8,128)(2,1)S(1)} %pad_maximum_fusion.2), channel_id=1, source_target_pairs={{0,6},{1,7},{2,4},{3,5},{4,2},{5,3},{6,0},{7,1},{8,14},{9,15},{10,... | collective-permute-start | bytes 417800 | tf_op jit(solution)/shard_map/ppermute | solution.py:24
  10.1 0.3 collective-permute-start.3
  10.4 11.3 %load.1 = (bf16[8192,512]{1,0:T(8,128)(2,1)S(1)}, bf16[8192,512]{1,0:T(8,128)(2,1)S(1)}, bf16[8192,512]{1,0:T(8,128)(2,1)S(1)}, bf16[8192,512]{1,0:T(8,128)(2,1)S(1)}) custom-call(f32[8192,1024]{1,0:T(8,128)} %bitcast.45, bf16[272,256]{1,0:T(8,128)(2,1)S(1)} %pad_maximum_fusion.after_ref.refs_0_), custom_call_target="tpu_custom_call" | custom-call | bytes 67108864 | tf_op jit(solution)/shard_map/load/pallas_call | solution.py:218
  21.7 0.0 collective-permute-done.1.refs_1_
  21.7 0.0 collective-permute-done.2.refs_2_
  21.7 0.0 collective-permute-done.3.refs_3_
  21.7 6.4 %stack.1 = (bf16[2,2,256,2048]{3,2,1,0:T(8,128)(2,1)S(1)}, f32[4,256,128]{2,1,0:T(8,128)S(1)}) custom-call(bf16[272,256]{1,0:T(8,128)(2,1)S(1)} %pad_maximum_fusion.after_ref.refs_0_, bf16[272,256]{1,0:T(8,128)(2,1)S(1)} %collective-permute-done.1.refs_1_, bf16[272,256]{1,0:T(8,128)(2,1)S(1)} %collective-permute-done.2.refs_2_, ...), custom_call_target="tpu_custom_call" | custom-call | flops 3221225472 | tf_op jit(solution)/shard_map/stack/pallas_call | solution.py:236
  28.1 0.1 collective-permute-start.4
  28.2 3.4 %keep.1 = f32[4,256,128]{2,1,0:T(8,128)S(1)} custom-call(bf16[2,2,256,2048]{3,2,1,0:T(8,128)(2,1)S(1)} %get-tuple-element.14.left_ref, bf16[8192,512]{1,0:T(8,128)(2,1)S(1)} %get-tuple-element.15.high_ref, bf16[8192,512]{1,0:T(8,128)(2,1)S(1)} %get-tuple-element.16.low_ref), custom_call_target="tpu_custom_call" | custom-call | flops 3221225472 | tf_op jit(solution)/shard_map/keep/pallas_call | solution.py:249
  31.6 0.0 collective-permute-done.4
  31.6 0.1 fusion.4
  31.7 1.8 %collective-permute-start.7 = (f32[256,128]{1,0:T(8,128)S(1)}, f32[256,128]{1,0:T(8,128)S(1)}, u32[]{:S(2)}, u32[]{:S(2)}) collective-permute-start(f32[256,128]{1,0:T(8,128)S(1)} %slice_bitcast_fusion), channel_id=1, source_target_pairs={{0,2},{1,3},{2,0},{3,1},{4,6},{5,7},{6,4},{7,5},{8,10},{9,11},{10,... | collective-permute-start | bytes 393224 | tf_op jit(solution)/shard_map/ppermute | solution.py:24
  33.6 1.8 %collective-permute-start.5 = (bf16[256,128]{1,0:T(8,128)(2,1)S(1)}, bf16[256,128]{1,0:T(8,128)(2,1)S(1)}, u32[]{:S(2)}, u32[]{:S(2)}) collective-permute-start(bf16[256,128]{1,0:T(8,128)(2,1)S(1)} %get-tuple-element.30), channel_id=1, source_target_pairs={{0,4},{1,5},{2,6},{3,7},{4,0},{5,1},{6,2},{7,3},{8,12},{9,13},{10,... | collective-permute-start | bytes 196616 | tf_op jit(solution)/shard_map/ppermute | solution.py:24
  35.3 0.9 %collective-permute-start.6 = (bf16[256,128]{1,0:T(8,128)(2,1)S(1)}, bf16[256,128]{1,0:T(8,128)(2,1)S(1)}, u32[]{:S(2)}, u32[]{:S(2)}) collective-permute-start(bf16[256,128]{1,0:T(8,128)(2,1)S(1)} %get-tuple-element.31), channel_id=1, source_target_pairs={{0,6},{1,7},{2,4},{3,5},{4,2},{5,3},{6,0},{7,1},{8,14},{9,15},{10,... | collective-permute-start | bytes 196616 | tf_op jit(solution)/shard_map/ppermute | solution.py:24
  36.3 2.8 %collective-permute-done.5 = bf16[256,128]{1,0:T(8,128)(2,1)S(1)} collective-permute-done((bf16[256,128]{1,0:T(8,128)(2,1)S(1)}, bf16[256,128]{1,0:T(8,128)(2,1)S(1)}, u32[]{:S(2)}, u32[]{:S(2)}) %collective-permute-start.5) | collective-permute-done | bytes 65568 | tf_op jit(solution)/shard_map/ppermute | solution.py:24
  39.0 3.8 %collective-permute-done.6 = bf16[256,128]{1,0:T(8,128)(2,1)S(1)} collective-permute-done((bf16[256,128]{1,0:T(8,128)(2,1)S(1)}, bf16[256,128]{1,0:T(8,128)(2,1)S(1)}, u32[]{:S(2)}, u32[]{:S(2)}) %collective-permute-start.6) | collective-permute-done | bytes 65568 | tf_op jit(solution)/shard_map/ppermute | solution.py:24
  42.8 0.0 collective-permute-done.7
  42.8 0.7 %bitcast_reduce_fusion = (f32[2,128]{1,0:T(2,128)S(1)}, f32[256,128]{1,0:T(8,128)}) fusion(f32[256,128]{1,0:T(8,128)S(1)} %collective-permute-done.7, bf16[256,128]{1,0:T(8,128)(2,1)S(1)} %collective-permute-done.6, bf16[256,128]{1,0:T(8,128)(2,1)S(1)} %collective-permute-done.5, f32[4,256,128]{2,1,0:T(8,128)S(1)} %get-tuple-element.21), kind=kLoop, calls=%fused_computation.9 | loop fusion | flops 229120 | bytes 525312 | tf_op jit(solution)/shard_map/reduce_sum | solution.py:264
  43.5 1.5 %collective-permute-start.8 = (f32[2,128]{1,0:T(2,128)S(1)}, f32[2,128]{1,0:T(2,128)S(1)}, u32[]{:S(2)}, u32[]{:S(2)}) collective-permute-start(f32[2,128]{1,0:T(2,128)S(1)} %get-tuple-element.18), channel_id=1, source_target_pairs={{0,8},{8,0},{16,24},{24,16},{1,9},{9,1},{17,25},{25,17},{2,10},{10... | collective-permute-start | bytes 3080 | tf_op jit(solution)/shard_map/ppermute | solution.py:24
  45.0 2.1 %collective-permute-done.8 = f32[2,128]{1,0:T(2,128)S(1)} collective-permute-done((f32[2,128]{1,0:T(2,128)S(1)}, f32[2,128]{1,0:T(2,128)S(1)}, u32[]{:S(2)}, u32[]{:S(2)}) %collective-permute-start.8) | collective-permute-done | bytes 1056 | tf_op jit(solution)/shard_map/ppermute | solution.py:24
  47.1 1.5 %collective-permute-start.9 = (f32[2,128]{1,0:T(2,128)S(1)}, f32[2,128]{1,0:T(2,128)S(1)}, u32[]{:S(2)}, u32[]{:S(2)}) collective-permute-start(f32[2,128]{1,0:T(2,128)S(1)} %add.22), channel_id=1, source_target_pairs={{0,16},{8,24},{16,0},{24,8},{1,17},{9,25},{17,1},{25,9},{2,18},{10... | collective-permute-start | bytes 3080 | tf_op jit(solution)/shard_map/ppermute | solution.py:24
  48.6 2.0 %collective-permute-done.9 = f32[2,128]{1,0:T(2,128)S(1)} collective-permute-done((f32[2,128]{1,0:T(2,128)S(1)}, f32[2,128]{1,0:T(2,128)S(1)}, u32[]{:S(2)}, u32[]{:S(2)}) %collective-permute-start.9) | collective-permute-done | bytes 1056 | tf_op jit(solution)/shard_map/ppermute | solution.py:24
  50.7 0.6 %multiply_bitcast_fusion = f32[128,2]{0,1:T(2,128)} fusion(f32[2,128]{1,0:T(2,128)S(1)} %add.22, f32[2,128]{1,0:T(2,128)S(1)} %collective-permute-done.9), kind=kLoop, calls=%fused_computation.20 | loop fusion | flops 512 | bytes 3072 | tf_op jit(solution)/shard_map/transpose | solution.py:271
  (9 shorter events, 0.1 us)
Async XLA Ops:
  2.8 1.7 %collective-permute-start = (bf16[4,136,256]{2,1,0:T(8,128)(2,1)S(1)}, bf16[4,136,256]{2,1,0:T(8,128)(2,1)S(1)}, u32[]{:S(2)}, u32[]{:S(2)}) collective-permute-start(bf16[4,136,256]{2,1,0:T(8,128)(2,1)S(1)} %get-tuple-element.11), channel_id=1, source_target_pairs={{0,1},{1,0},{2,3},{3,2},{4,5},{5,4},{6,7},{7,6},{8,9},{9,8},{10,11... | collective-permute-start | bytes 835592 | tf_op jit(solution)/shard_map/ppermute | solution.py:24
  4.6 17.1 %collective-permute-start.1 = (bf16[272,256]{1,0:T(8,128)(2,1)S(1)}, bf16[272,256]{1,0:T(8,128)(2,1)S(1)}, u32[]{:S(2)}, u32[]{:S(2)}) collective-permute-start(bf16[272,256]{1,0:T(8,128)(2,1)S(1)} %pad_maximum_fusion.1), channel_id=1, source_target_pairs={{0,4},{1,5},{2,6},{3,7},{4,0},{5,1},{6,2},{7,3},{8,12},{9,13},{10,... | collective-permute-start | bytes 417800 | tf_op jit(solution)/shard_map/ppermute | solution.py:24
  8.6 13.1 %collective-permute-start.2 = (bf16[272,256]{1,0:T(8,128)(2,1)S(1)}, bf16[272,256]{1,0:T(8,128)(2,1)S(1)}, u32[]{:S(2)}, u32[]{:S(2)}) collective-permute-start(bf16[272,256]{1,0:T(8,128)(2,1)S(1)} %pad_maximum_fusion.2), channel_id=1, source_target_pairs={{0,6},{1,7},{2,4},{3,5},{4,2},{5,3},{6,0},{7,1},{8,14},{9,15},{10,... | collective-permute-start | bytes 417800 | tf_op jit(solution)/shard_map/ppermute | solution.py:24
  10.1 11.7 %collective-permute-start.3 = (bf16[272,256]{1,0:T(8,128)(2,1)S(1)}, bf16[272,256]{1,0:T(8,128)(2,1)S(1)}, u32[]{:S(2)}, u32[]{:S(2)}) collective-permute-start(bf16[272,256]{1,0:T(8,128)(2,1)S(1)} %pad_maximum_fusion.3), channel_id=1, source_target_pairs={{0,2},{1,3},{2,0},{3,1},{4,6},{5,7},{6,4},{7,5},{8,10},{9,11},{10,... | collective-permute-start | bytes 417800 | tf_op jit(solution)/shard_map/ppermute | solution.py:24
  28.1 3.5 %collective-permute-start.4 = (f32[4,256,128]{2,1,0:T(8,128)S(1)}, f32[4,256,128]{2,1,0:T(8,128)S(1)}, u32[]{:S(2)}, u32[]{:S(2)}) collective-permute-start(f32[4,256,128]{2,1,0:T(8,128)S(1)} %get-tuple-element.17), channel_id=1, source_target_pairs={{0,1},{1,0},{2,3},{3,2},{4,5},{5,4},{6,7},{7,6},{8,9},{9,8},{10,11... | collective-permute-start | bytes 1572872 | tf_op jit(solution)/shard_map/ppermute | solution.py:24
  31.7 11.1 %collective-permute-start.7 = (f32[256,128]{1,0:T(8,128)S(1)}, f32[256,128]{1,0:T(8,128)S(1)}, u32[]{:S(2)}, u32[]{:S(2)}) collective-permute-start(f32[256,128]{1,0:T(8,128)S(1)} %slice_bitcast_fusion), channel_id=1, source_target_pairs={{0,2},{1,3},{2,0},{3,1},{4,6},{5,7},{6,4},{7,5},{8,10},{9,11},{10,... | collective-permute-start | bytes 393224 | tf_op jit(solution)/shard_map/ppermute | solution.py:24
  33.6 5.5 %collective-permute-start.5 = (bf16[256,128]{1,0:T(8,128)(2,1)S(1)}, bf16[256,128]{1,0:T(8,128)(2,1)S(1)}, u32[]{:S(2)}, u32[]{:S(2)}) collective-permute-start(bf16[256,128]{1,0:T(8,128)(2,1)S(1)} %get-tuple-element.30), channel_id=1, source_target_pairs={{0,4},{1,5},{2,6},{3,7},{4,0},{5,1},{6,2},{7,3},{8,12},{9,13},{10,... | collective-permute-start | bytes 196616 | tf_op jit(solution)/shard_map/ppermute | solution.py:24
  35.3 7.5 %collective-permute-start.6 = (bf16[256,128]{1,0:T(8,128)(2,1)S(1)}, bf16[256,128]{1,0:T(8,128)(2,1)S(1)}, u32[]{:S(2)}, u32[]{:S(2)}) collective-permute-start(bf16[256,128]{1,0:T(8,128)(2,1)S(1)} %get-tuple-element.31), channel_id=1, source_target_pairs={{0,6},{1,7},{2,4},{3,5},{4,2},{5,3},{6,0},{7,1},{8,14},{9,15},{10,... | collective-permute-start | bytes 196616 | tf_op jit(solution)/shard_map/ppermute | solution.py:24
  43.5 3.6 %collective-permute-start.8 = (f32[2,128]{1,0:T(2,128)S(1)}, f32[2,128]{1,0:T(2,128)S(1)}, u32[]{:S(2)}, u32[]{:S(2)}) collective-permute-start(f32[2,128]{1,0:T(2,128)S(1)} %get-tuple-element.18), channel_id=1, source_target_pairs={{0,8},{8,0},{16,24},{24,16},{1,9},{9,1},{17,25},{25,17},{2,10},{10... | collective-permute-start | bytes 3080 | tf_op jit(solution)/shard_map/ppermute | solution.py:24
  47.1 3.6 %collective-permute-start.9 = (f32[2,128]{1,0:T(2,128)S(1)}, f32[2,128]{1,0:T(2,128)S(1)}, u32[]{:S(2)}, u32[]{:S(2)}) collective-permute-start(f32[2,128]{1,0:T(2,128)S(1)} %add.22), channel_id=1, source_target_pairs={{0,16},{8,24},{16,0},{24,8},{1,17},{9,25},{17,1},{25,9},{2,18},{10... | collective-permute-start | bytes 3080 | tf_op jit(solution)/shard_map/ppermute | solution.py:24

commit v3 on v2

--- a/solution.py
+++ b/solution.py
@@ -83,8 +83,17 @@
     )
 
 
+def groups(peers):
+    chips = peers // 2
+    return (
+        [2 * k + 1 for k in range(chips)],
+        [2 * k for k in range(chips) if k & (chips // 2)],
+        [2 * k for k in range(chips) if not k & (chips // 2)],
+    )
+
+
 def load_kernel(peers, chunk, beam_ref, after_ref, *refs):
-    outs, buffer, sems = (refs[:2], refs[2:4]), refs[4], refs[5]
+    outs, buffer, sems = (refs[:2], refs[2:4], refs[4:6]), refs[6], refs[7]
     steps = beam_ref.shape[0] // chunk
     slots = buffer.shape[0]
     width = beam_ref.shape[1] // peers
@@ -103,17 +112,17 @@
         copy(step).wait()
 
         @pl.loop(0, chunk // 32)
-        def _(i):
-            at = pl.multiple_of(i * 32, 32)
-            for j in range(peers):
-                lane = pl.multiple_of((me ^ j) * width, width)
-                value = buffer[step % slots, pl.ds(at, 32), pl.ds(lane, width)]
-                high = value.astype(jnp.bfloat16)
-                low = (value - high.astype(jnp.float32)).astype(jnp.bfloat16)
-                high_ref, low_ref = outs[1 - j % 2]
-                to = (pl.ds(step * chunk + at, 32), slice(j // 2 * width, (j // 2 + 1) * width))
-                high_ref[to] = high
-                low_ref[to] = low
+        def _(line):
+            at = pl.multiple_of(line * 32, 32)
+            for (high_ref, low_ref), owners in zip(outs, groups(peers)):
+                for i, j in enumerate(owners):
+                    lane = pl.multiple_of((me ^ j) * width, width)
+                    value = buffer[step % slots, pl.ds(at, 32), pl.ds(lane, width)]
+                    high = value.astype(jnp.bfloat16)
+                    low = (value - high.astype(jnp.float32)).astype(jnp.bfloat16)
+                    to = (pl.ds(step * chunk + at, 32), slice(i * width, (i + 1) * width))
+                    high_ref[to] = high
+                    low_ref[to] = low
 
         if step + slots < steps:
             copy(step + slots).start()
@@ -180,7 +189,8 @@
             out_ref[k, m * half : (m + 1) * half] = total[:, k * width : (k + 1) * width]
 
 
-def keep_kernel(left_ref, high_ref, low_ref, keep_ref):
+def keep_kernel(left_ref, high_ref, low_ref, *refs):
+    keep_ref = refs[-1]
     project(left_ref, high_ref, low_ref, keep_ref)
 
 
@@ -217,9 +227,13 @@
     planes = beam.reshape(mwin * 2 * base_dev, modes)
     held = pl.pallas_call(
         functools.partial(load_kernel, peers, chunk),
-        out_shape=(pltpu.VMEM((planes.shape[0], modes // 2), jnp.bfloat16),) * 4,
+        out_shape=tuple(
+            pltpu.VMEM((planes.shape[0], len(owners) * width), jnp.bfloat16)
+            for owners in groups(peers)
+            for _ in range(2)
+        ),
         in_specs=[anywhere, anywhere],
-        out_specs=(vmem,) * 4,
+        out_specs=(vmem,) * 6,
         scratch_shapes=[
             pltpu.VMEM((4, chunk, modes), jnp.float32),
             pltpu.SemaphoreType.DMA((4,)),
@@ -231,35 +245,50 @@
         name="load",
     )(planes, pieces[0])
     held = [pltpu.with_memory_space_constraint(part, pltpu.VMEM) for part in held]
-    products = jax.ShapeDtypeStruct((chips, columns, width), jnp.float32)
-    flops = 6 * mwin * 2 * (columns // mwin) * base_dev * modes // 2
+    def products(count):
+        return jax.ShapeDtypeStruct((count, columns, width), jnp.float32)
+
+    def cost(count):
+        flops = 6 * mwin * 2 * (columns // mwin) * base_dev * count * width
+        return pl.CostEstimate(flops=flops, bytes_accessed=0, transcendentals=0)
+
     left, send = pl.pallas_call(
         functools.partial(stack_kernel, peers, capacity, mwin),
         out_shape=(
             pltpu.VMEM((mwin, 2, 2 * columns // mwin, base_dev), jnp.bfloat16),
-            products,
+            products(chips),
         ),
         in_specs=[vmem] * (chips + 2),
         out_specs=(vmem, vmem),
         compiler_params=pltpu.CompilerParams(vmem_limit_bytes=12 * MIB),
-        cost_estimate=pl.CostEstimate(flops=flops, bytes_accessed=0, transcendentals=0),
+        cost_estimate=cost(chips),
         name="stack",
     )(pieces[0], *[moved[k] for k in order], *held[:2])
     got = swap(send, "pair", 1)
-    keep = pl.pallas_call(
-        keep_kernel,
-        out_shape=products,
-        in_specs=[vmem] * 3,
-        out_specs=vmem,
-        compiler_params=pltpu.CompilerParams(vmem_limit_bytes=12 * MIB),
-        cost_estimate=pl.CostEstimate(flops=flops, bytes_accessed=0, transcendentals=0),
-        name="keep",
-    )(pltpu.with_memory_space_constraint(left, pltpu.VMEM), *held[2:])
-    summed = keep + got
+    left = pltpu.with_memory_space_constraint(left, pltpu.VMEM)
+    summed, after = {}, []
+    for name, parts, owners in zip(("far", "near"), (held[2:4], held[4:6]), groups(peers)[1:]):
+        keep = pl.pallas_call(
+            keep_kernel,
+            out_shape=products(len(owners)),
+            in_specs=[vmem] * 3 + [anywhere] * len(after),
+            out_specs=vmem,
+            compiler_params=pltpu.CompilerParams(vmem_limit_bytes=12 * MIB),
+            cost_estimate=cost(len(owners)),
+            name=name,
+        )(left, *parts, *after)
+        for i, j in enumerate(owners):
+            k = j // 2
+            summed[k] = keep[i] + got[k]
+            if k:
+                summed[k] = summed[k].astype(jnp.bfloat16)
+            if k & (chips // 2):
+                after.append(summed[k])
     amplitudes = summed[0]
     for k in order:
-        value = summed[k] if k == 1 else summed[k].astype(jnp.bfloat16)
-        amplitudes = amplitudes + swap(value, "pair", 2 * k).astype(jnp.float32)
+        if not k & (chips // 2):
+            amplitudes = lax.optimization_barrier(amplitudes)
+        amplitudes = amplitudes + swap(summed[k], "pair", 2 * k).astype(jnp.float32)
     sets = columns // (2 * mwin)
     power = jnp.sum((amplitudes * amplitudes).reshape(mwin, 2 * sets, width), axis=1)
     distance = 1

time: 51.4 us -> 49.6 us (0.965)
  waiting for transfers between devices: 11.9 us -> 9.46 us
  Pallas kernels: 23.3 us -> 23.9 us
    ppermute x10, waiting for transfers between devices: 11.9 us -> 9.46 us  [swap(): return lax.ppermute(value, axis, [(i, i ^ distance) for i in range(size)])]
    pallas_call x2 -> x3, Pallas kernels: 14.7 us -> 15.3 us  [the longest x1 11.3 us: staged(): pl.pallas_call(functools.partial(load_kernel, peers, chunk), out_shape=tu...]
  transfers between devices with their start and end apart: 10 -> 10, of which waited for: 5 -> 5; matrix products, arithmetic and copies ran while one was open for 0% -> 0% of each run, Pallas kernels for 29% -> 31%
where the time goes in v3:
time: 49.6 us; the launch traced here: 49.4 us
  Pallas kernels  23.9 us (48%)
  starting transfers between devices  13.9 us (28%)
  waiting for transfers between devices  9.46 us (19%)
  other arithmetic  1.38 us (3%)
  between operations  0.75 us (2%)
    ppermute x10, starting transfers between devices, swap(): return lax.ppermute(value, axis, [(i, i ^ distance) for i in range(size)])  13.9 us
    pallas_call x1, Pallas kernels, staged(): pl.pallas_call(functools.partial(load_kernel, peers, chunk), out_shape=tu...  11.3 us
    ppermute x10, waiting for transfers between devices, swap(): return lax.ppermute(value, axis, [(i, i ^ distance) for i in range(size)])  9.46 us
    pallas_call x1, Pallas kernels, staged(): pl.pallas_call(functools.partial(stack_kernel, peers, capacity, mwin), ou...  6.37 us
    pallas_call x2, Pallas kernels, staged(): pl.pallas_call(keep_kernel, out_shape=products(len(owners)), in_specs=[vm...  4.01 us
    pallas_call x1, Pallas kernels, staged(): pl.pallas_call(functools.partial(pack_kernel, peers, capacity), out_shape...  2.2 us
  transfers between devices with their start and end apart: 10, of which 5 were waited for; matrix products, arithmetic and copies ran while one was open for 0% of the time, Pallas kernels for 31%

profile of v3, /device:TPU:0, one launch (start us, length us, event | category | flops | bytes accessed | tf_op | source)
XLA Modules:
  0.0 49.4 jit_solution(7917053560980318572)
XLA Ops:
  0.6 2.2 %pack.1 = (bf16[4,136,256]{2,1,0:T(8,128)(2,1)S(1)}, bf16[4,136,256]{2,1,0:T(8,128)(2,1)S(1)}) custom-call(bf16[512,256]{1,0:T(8,128)(2,1)} %bitcast.43, s32[1,512]{1,0:T(1,128)} %bitcast.45, s32[1,512]{1,0:T(1,128)} %bitcast.46, s32[1,512]{1,0:T(1,128)} %bitcast.47), custom_call_target="tpu_custom_call" | custom-call | tf_op jit(solution)/shard_map/pack/pallas_call | solution.py:209
  2.8 0.5 %collective-permute-start = (bf16[4,136,256]{2,1,0:T(8,128)(2,1)S(1)}, bf16[4,136,256]{2,1,0:T(8,128)(2,1)S(1)}, u32[]{:S(2)}, u32[]{:S(2)}) collective-permute-start(bf16[4,136,256]{2,1,0:T(8,128)(2,1)S(1)} %get-tuple-element.13), channel_id=1, source_target_pairs={{0,1},{1,0},{2,3},{3,2},{4,5},{5,4},{6,7},{7,6},{8,9},{9,8},{10,11... | collective-permute-start | bytes 835592 | tf_op jit(solution)/shard_map/ppermute | solution.py:24
  3.4 1.2 %collective-permute-done = bf16[4,136,256]{2,1,0:T(8,128)(2,1)S(1)} collective-permute-done((bf16[4,136,256]{2,1,0:T(8,128)(2,1)S(1)}, bf16[4,136,256]{2,1,0:T(8,128)(2,1)S(1)}, u32[]{:S(2)}, u32[]{:S(2)}) %collective-permute-start) | collective-permute-done | bytes 278560 | tf_op jit(solution)/shard_map/ppermute | solution.py:24
  4.6 4.0 %collective-permute-start.1 = (bf16[272,256]{1,0:T(8,128)(2,1)S(1)}, bf16[272,256]{1,0:T(8,128)(2,1)S(1)}, u32[]{:S(2)}, u32[]{:S(2)}) collective-permute-start(bf16[272,256]{1,0:T(8,128)(2,1)S(1)} %pad_maximum_fusion.1), channel_id=1, source_target_pairs={{0,4},{1,5},{2,6},{3,7},{4,0},{5,1},{6,2},{7,3},{8,12},{9,13},{10,... | collective-permute-start | bytes 417800 | tf_op jit(solution)/shard_map/ppermute | solution.py:24
  8.6 1.4 %collective-permute-start.2 = (bf16[272,256]{1,0:T(8,128)(2,1)S(1)}, bf16[272,256]{1,0:T(8,128)(2,1)S(1)}, u32[]{:S(2)}, u32[]{:S(2)}) collective-permute-start(bf16[272,256]{1,0:T(8,128)(2,1)S(1)} %pad_maximum_fusion.2), channel_id=1, source_target_pairs={{0,6},{1,7},{2,4},{3,5},{4,2},{5,3},{6,0},{7,1},{8,14},{9,15},{10,... | collective-permute-start | bytes 417800 | tf_op jit(solution)/shard_map/ppermute | solution.py:24
  10.1 0.3 collective-permute-start.3
  10.4 11.3 %load.1 = (bf16[8192,512]{1,0:T(8,128)(2,1)S(1)}, bf16[8192,512]{1,0:T(8,128)(2,1)S(1)}, bf16[8192,256]{1,0:T(8,128)(2,1)S(1)}, bf16[8192,256]{1,0:T(8,128)(2,1)...) custom-call(f32[8192,1024]{1,0:T(8,128)} %bitcast.42, ...), custom_call_target="tpu_custom_call" | custom-call | bytes 67108864 | tf_op jit(solution)/shard_map/load/pallas_call | solution.py:228
  21.7 0.0 collective-permute-done.1.refs_1_
  21.7 0.0 collective-permute-done.2.refs_2_
  21.7 0.0 collective-permute-done.3.refs_3_
  21.8 6.4 %stack.1 = (bf16[2,2,256,2048]{3,2,1,0:T(8,128)(2,1)S(1)}, f32[4,256,128]{2,1,0:T(8,128)S(1)}) custom-call(bf16[272,256]{1,0:T(8,128)(2,1)S(1)} %pad_maximum_fusion.after_ref.refs_0_, bf16[272,256]{1,0:T(8,128)(2,1)S(1)} %collective-permute-done.1.refs_1_, bf16[272,256]{1,0:T(8,128)(2,1)S(1)} %collective-permute-done.2.refs_2_, ...), custom_call_target="tpu_custom_call" | custom-call | flops 3221225472 | tf_op jit(solution)/shard_map/stack/pallas_call | solution.py:255
  28.1 0.1 collective-permute-start.4
  28.2 2.0 %far.1 = f32[2,256,128]{2,1,0:T(8,128)S(1)} custom-call(bf16[2,2,256,2048]{3,2,1,0:T(8,128)(2,1)S(1)} %get-tuple-element.16.left_ref, bf16[8192,256]{1,0:T(8,128)(2,1)S(1)} %get-tuple-element.19.high_ref, bf16[8192,256]{1,0:T(8,128)(2,1)S(1)} %get-tuple-element.20.low_ref), custom_call_target="tpu_custom_call" | custom-call | flops 1610612736 | tf_op jit(solution)/shard_map/far/pallas_call | solution.py:271
  30.2 0.0 collective-permute-done.4
  30.3 3.0 %collective-permute-start.6 = (bf16[256,128]{1,0:T(8,128)(2,1)S(1)}, bf16[256,128]{1,0:T(8,128)(2,1)S(1)}, u32[]{:S(2)}, u32[]{:S(2)}) collective-permute-start(bf16[256,128]{1,0:T(8,128)(2,1)S(1)} %get-tuple-element.24.refs_1_), channel_id=1, source_target_pairs={{0,6},{1,7},{2,4},{3,5},{4,2},{5,3},{6,0},{7,1},{8,14},{9,15},{10,... | collective-permute-start | bytes 196616 | tf_op jit(solution)/shard_map/ppermute | solution.py:24
  33.3 0.3 collective-permute-start.5
  33.6 2.0 %near.1 = f32[2,256,128]{2,1,0:T(8,128)S(1)} custom-call(bf16[2,2,256,2048]{3,2,1,0:T(8,128)(2,1)S(1)} %get-tuple-element.16.left_ref, bf16[8192,256]{1,0:T(8,128)(2,1)S(1)} %get-tuple-element.17.high_ref, bf16[8192,256]{1,0:T(8,128)(2,1)S(1)} %get-tuple-element.18.low_ref, bf16[256,128]{1,0:T(8,128)(2,1)S(1)} %get-tuple-element.25.refs_0_, ...), custom_call_target="tpu_custom_call" | custom-call | flops 1610612736 | tf_op jit(solution)/shard_map/near/pallas_call | solution.py:271
  35.6 1.2 %collective-permute-start.7 = (bf16[256,128]{1,0:T(8,128)(2,1)S(1)}, bf16[256,128]{1,0:T(8,128)(2,1)S(1)}, u32[]{:S(2)}, u32[]{:S(2)}) collective-permute-start(bf16[256,128]{1,0:T(8,128)(2,1)S(1)} %fusion.8), channel_id=1, source_target_pairs={{0,2},{1,3},{2,0},{3,1},{4,6},{5,7},{6,4},{7,5},{8,10},{9,11},{10,... | collective-permute-start | bytes 196616 | tf_op jit(solution)/shard_map/ppermute | solution.py:24
  36.8 0.0 collective-permute-done.6
  36.8 3.5 %collective-permute-done.5 = bf16[256,128]{1,0:T(8,128)(2,1)S(1)} collective-permute-done((bf16[256,128]{1,0:T(8,128)(2,1)S(1)}, bf16[256,128]{1,0:T(8,128)(2,1)S(1)}, u32[]{:S(2)}, u32[]{:S(2)}) %collective-permute-start.5) | collective-permute-done | bytes 65568 | tf_op jit(solution)/shard_map/ppermute | solution.py:24
  40.4 0.6 %collective-permute-done.7 = bf16[256,128]{1,0:T(8,128)(2,1)S(1)} collective-permute-done((bf16[256,128]{1,0:T(8,128)(2,1)S(1)}, bf16[256,128]{1,0:T(8,128)(2,1)S(1)}, u32[]{:S(2)}, u32[]{:S(2)}) %collective-permute-start.7) | collective-permute-done | bytes 65568 | tf_op jit(solution)/shard_map/ppermute | solution.py:24
  41.0 0.7 %bitcast_reduce_fusion = (f32[2,128]{1,0:T(2,128)S(1)}, f32[256,128]{1,0:T(8,128)}) fusion(f32[256,128]{1,0:T(8,128)S(1)} %fusion.3, bf16[256,128]{1,0:T(8,128)(2,1)S(1)} %collective-permute-done.7), kind=kLoop, calls=%fused_computation.14 | loop fusion | flops 130816 | bytes 328704 | tf_op jit(solution)/shard_map/reduce_sum | solution.py:293
  41.7 1.5 %collective-permute-start.8 = (f32[2,128]{1,0:T(2,128)S(1)}, f32[2,128]{1,0:T(2,128)S(1)}, u32[]{:S(2)}, u32[]{:S(2)}) collective-permute-start(f32[2,128]{1,0:T(2,128)S(1)} %get-tuple-element.22), channel_id=1, source_target_pairs={{0,8},{8,0},{16,24},{24,16},{1,9},{9,1},{17,25},{25,17},{2,10},{10... | collective-permute-start | bytes 3080 | tf_op jit(solution)/shard_map/ppermute | solution.py:24
  43.2 2.1 %collective-permute-done.8 = f32[2,128]{1,0:T(2,128)S(1)} collective-permute-done((f32[2,128]{1,0:T(2,128)S(1)}, f32[2,128]{1,0:T(2,128)S(1)}, u32[]{:S(2)}, u32[]{:S(2)}) %collective-permute-start.8) | collective-permute-done | bytes 1056 | tf_op jit(solution)/shard_map/ppermute | solution.py:24
  45.3 1.5 %collective-permute-start.9 = (f32[2,128]{1,0:T(2,128)S(1)}, f32[2,128]{1,0:T(2,128)S(1)}, u32[]{:S(2)}, u32[]{:S(2)}) collective-permute-start(f32[2,128]{1,0:T(2,128)S(1)} %add.41), channel_id=1, source_target_pairs={{0,16},{8,24},{16,0},{24,8},{1,17},{9,25},{17,1},{25,9},{2,18},{10... | collective-permute-start | bytes 3080 | tf_op jit(solution)/shard_map/ppermute | solution.py:24
  46.8 2.0 %collective-permute-done.9 = f32[2,128]{1,0:T(2,128)S(1)} collective-permute-done((f32[2,128]{1,0:T(2,128)S(1)}, f32[2,128]{1,0:T(2,128)S(1)}, u32[]{:S(2)}, u32[]{:S(2)}) %collective-permute-start.9) | collective-permute-done | bytes 1056 | tf_op jit(solution)/shard_map/ppermute | solution.py:24
  48.9 0.6 %multiply_bitcast_fusion = f32[128,2]{0,1:T(2,128)} fusion(f32[2,128]{1,0:T(2,128)S(1)} %add.41, f32[2,128]{1,0:T(2,128)S(1)} %collective-permute-done.9), kind=kLoop, calls=%fused_computation.27 | loop fusion | flops 512 | bytes 3072 | tf_op jit(solution)/shard_map/transpose | solution.py:300
  (10 shorter events, 0.2 us)
Async XLA Ops:
  2.8 1.7 %collective-permute-start = (bf16[4,136,256]{2,1,0:T(8,128)(2,1)S(1)}, bf16[4,136,256]{2,1,0:T(8,128)(2,1)S(1)}, u32[]{:S(2)}, u32[]{:S(2)}) collective-permute-start(bf16[4,136,256]{2,1,0:T(8,128)(2,1)S(1)} %get-tuple-element.13), channel_id=1, source_target_pairs={{0,1},{1,0},{2,3},{3,2},{4,5},{5,4},{6,7},{7,6},{8,9},{9,8},{10,11... | collective-permute-start | bytes 835592 | tf_op jit(solution)/shard_map/ppermute | solution.py:24
  4.6 17.1 %collective-permute-start.1 = (bf16[272,256]{1,0:T(8,128)(2,1)S(1)}, bf16[272,256]{1,0:T(8,128)(2,1)S(1)}, u32[]{:S(2)}, u32[]{:S(2)}) collective-permute-start(bf16[272,256]{1,0:T(8,128)(2,1)S(1)} %pad_maximum_fusion.1), channel_id=1, source_target_pairs={{0,4},{1,5},{2,6},{3,7},{4,0},{5,1},{6,2},{7,3},{8,12},{9,13},{10,... | collective-permute-start | bytes 417800 | tf_op jit(solution)/shard_map/ppermute | solution.py:24
  8.6 13.1 %collective-permute-start.2 = (bf16[272,256]{1,0:T(8,128)(2,1)S(1)}, bf16[272,256]{1,0:T(8,128)(2,1)S(1)}, u32[]{:S(2)}, u32[]{:S(2)}) collective-permute-start(bf16[272,256]{1,0:T(8,128)(2,1)S(1)} %pad_maximum_fusion.2), channel_id=1, source_target_pairs={{0,6},{1,7},{2,4},{3,5},{4,2},{5,3},{6,0},{7,1},{8,14},{9,15},{10,... | collective-permute-start | bytes 417800 | tf_op jit(solution)/shard_map/ppermute | solution.py:24
  10.1 11.7 %collective-permute-start.3 = (bf16[272,256]{1,0:T(8,128)(2,1)S(1)}, bf16[272,256]{1,0:T(8,128)(2,1)S(1)}, u32[]{:S(2)}, u32[]{:S(2)}) collective-permute-start(bf16[272,256]{1,0:T(8,128)(2,1)S(1)} %pad_maximum_fusion.3), channel_id=1, source_target_pairs={{0,2},{1,3},{2,0},{3,1},{4,6},{5,7},{6,4},{7,5},{8,10},{9,11},{10,... | collective-permute-start | bytes 417800 | tf_op jit(solution)/shard_map/ppermute | solution.py:24
  28.1 2.1 %collective-permute-start.4 = (f32[4,256,128]{2,1,0:T(8,128)S(1)}, f32[4,256,128]{2,1,0:T(8,128)S(1)}, u32[]{:S(2)}, u32[]{:S(2)}) collective-permute-start(f32[4,256,128]{2,1,0:T(8,128)S(1)} %get-tuple-element.21), channel_id=1, source_target_pairs={{0,1},{1,0},{2,3},{3,2},{4,5},{5,4},{6,7},{7,6},{8,9},{9,8},{10,11... | collective-permute-start | bytes 1572872 | tf_op jit(solution)/shard_map/ppermute | solution.py:24
  30.3 6.6 %collective-permute-start.6 = (bf16[256,128]{1,0:T(8,128)(2,1)S(1)}, bf16[256,128]{1,0:T(8,128)(2,1)S(1)}, u32[]{:S(2)}, u32[]{:S(2)}) collective-permute-start(bf16[256,128]{1,0:T(8,128)(2,1)S(1)} %get-tuple-element.24.refs_1_), channel_id=1, source_target_pairs={{0,6},{1,7},{2,4},{3,5},{4,2},{5,3},{6,0},{7,1},{8,14},{9,15},{10,... | collective-permute-start | bytes 196616 | tf_op jit(solution)/shard_map/ppermute | solution.py:24
  33.3 7.1 %collective-permute-start.5 = (bf16[256,128]{1,0:T(8,128)(2,1)S(1)}, bf16[256,128]{1,0:T(8,128)(2,1)S(1)}, u32[]{:S(2)}, u32[]{:S(2)}) collective-permute-start(bf16[256,128]{1,0:T(8,128)(2,1)S(1)} %get-tuple-element.25.refs_0_), channel_id=1, source_target_pairs={{0,4},{1,5},{2,6},{3,7},{4,0},{5,1},{6,2},{7,3},{8,12},{9,13},{10,... | collective-permute-start | bytes 196616 | tf_op jit(solution)/shard_map/ppermute | solution.py:24
  35.6 5.4 %collective-permute-start.7 = (bf16[256,128]{1,0:T(8,128)(2,1)S(1)}, bf16[256,128]{1,0:T(8,128)(2,1)S(1)}, u32[]{:S(2)}, u32[]{:S(2)}) collective-permute-start(bf16[256,128]{1,0:T(8,128)(2,1)S(1)} %fusion.8), channel_id=1, source_target_pairs={{0,2},{1,3},{2,0},{3,1},{4,6},{5,7},{6,4},{7,5},{8,10},{9,11},{10,... | collective-permute-start | bytes 196616 | tf_op jit(solution)/shard_map/ppermute | solution.py:24
  41.7 3.6 %collective-permute-start.8 = (f32[2,128]{1,0:T(2,128)S(1)}, f32[2,128]{1,0:T(2,128)S(1)}, u32[]{:S(2)}, u32[]{:S(2)}) collective-permute-start(f32[2,128]{1,0:T(2,128)S(1)} %get-tuple-element.22), channel_id=1, source_target_pairs={{0,8},{8,0},{16,24},{24,16},{1,9},{9,1},{17,25},{25,17},{2,10},{10... | collective-permute-start | bytes 3080 | tf_op jit(solution)/shard_map/ppermute | solution.py:24
  45.3 3.6 %collective-permute-start.9 = (f32[2,128]{1,0:T(2,128)S(1)}, f32[2,128]{1,0:T(2,128)S(1)}, u32[]{:S(2)}, u32[]{:S(2)}) collective-permute-start(f32[2,128]{1,0:T(2,128)S(1)} %add.41), channel_id=1, source_target_pairs={{0,16},{8,24},{16,0},{24,8},{1,17},{9,25},{17,1},{25,9},{2,18},{10... | collective-permute-start | bytes 3080 | tf_op jit(solution)/shard_map/ppermute | solution.py:24

commit v4 on v3

--- a/solution.py
+++ b/solution.py
@@ -8,6 +8,9 @@
 from jax.sharding import PartitionSpec as P
 
 MIB = 1 << 20
+SMALL = jnp.float8_e5m2
+AHEAD = 2
+BEAM, BEAM_REST, STACK, STACK_REST = 2.0**18, 2.0**27, 2.0**12, 2.0**21
 
 
 def round_up(value, unit):
@@ -25,13 +28,16 @@
 
 
 def pack_kernel(peers, capacity, *refs):
-    sources, (mine_ref, theirs_ref), held, sems = refs[:4], refs[4:6], refs[6:10], refs[10]
+    sources, beam_ref, (mine_ref, theirs_ref, start_ref) = refs[:4], refs[4], refs[5:8]
+    held, sems = refs[8:12], refs[12]
     copies = [
         pltpu.make_async_copy(source, target, sems.at[i])
         for i, (source, target) in enumerate(zip(sources, held))
     ]
     for copy in copies:
         copy.start()
+    ahead = pltpu.make_async_copy(beam_ref.at[pl.ds(0, start_ref.shape[0])], start_ref, sems.at[4])
+    ahead.start()
     for copy in copies:
         copy.wait()
     vis_ref, counts_ref, owner_ref, slot_ref = held
@@ -75,6 +81,7 @@
         block = jnp.concatenate([body[: size - 8], body[size - 8 : size] + named], axis=0)
         out_ref = theirs_ref if j % 2 else mine_ref
         out_ref[j // 2] = block.astype(jnp.bfloat16)
+    ahead.wait()
 
 
 def dot_rows(left, right):
@@ -92,9 +99,10 @@
     )
 
 
-def load_kernel(peers, chunk, beam_ref, after_ref, *refs):
-    outs, buffer, sems = (refs[:2], refs[2:4], refs[4:6]), refs[6], refs[7]
+def load_kernel(peers, chunk, beam_ref, start_ref, after_ref, *refs):
+    outs, buffer, sems = (refs[:3], refs[3:6], refs[6:9]), refs[9], refs[10]
     steps = beam_ref.shape[0] // chunk
+    ahead = start_ref.shape[0] // chunk
     slots = buffer.shape[0]
     width = beam_ref.shape[1] // peers
     me = lax.axis_index("pair")
@@ -106,34 +114,39 @@
             sems.at[step % slots],
         )
 
-    for step in range(min(slots, steps)):
+    for step in range(ahead, min(ahead + slots, steps)):
         copy(step).start()
     for step in range(steps):
-        copy(step).wait()
+        if step < ahead:
+            source = start_ref.at[pl.ds(step * chunk, chunk)]
+        else:
+            copy(step).wait()
+            source = buffer.at[step % slots]
 
         @pl.loop(0, chunk // 32)
         def _(line):
             at = pl.multiple_of(line * 32, 32)
-            for (high_ref, low_ref), owners in zip(outs, groups(peers)):
+            for (high_ref, again_ref, rest_ref), owners in zip(outs, groups(peers)):
                 for i, j in enumerate(owners):
                     lane = pl.multiple_of((me ^ j) * width, width)
-                    value = buffer[step % slots, pl.ds(at, 32), pl.ds(lane, width)]
+                    value = source[pl.ds(at, 32), pl.ds(lane, width)]
                     high = value.astype(jnp.bfloat16)
-                    low = (value - high.astype(jnp.float32)).astype(jnp.bfloat16)
+                    rest = value - high.astype(jnp.float32)
                     to = (pl.ds(step * chunk + at, 32), slice(i * width, (i + 1) * width))
                     high_ref[to] = high
-                    low_ref[to] = low
-
-        if step + slots < steps:
+                    again_ref[to] = (high * BEAM).astype(SMALL)
+                    rest_ref[to] = (rest * BEAM_REST).astype(SMALL)
+
+        if ahead <= step < steps - slots:
             copy(step + slots).start()
 
 
 def stack_kernel(peers, capacity, mwin, *refs):
     pieces = refs[: peers // 2]
-    high_ref, low_ref, left_ref, send_ref = refs[peers // 2 :]
+    held, (left_ref, small_ref, *send_refs) = refs[peers // 2 : -4], refs[-4:]
     first, size = block_rows(capacity)
     columns = pieces[0].shape[1]
-    base_dev = left_ref.shape[3]
+    base_dev = left_ref.shape[2] // 2
     half = columns // (2 * mwin)
     tile = 512 if base_dev % 512 == 0 else base_dev
     rows, slots, weights = [], [], []
@@ -154,44 +167,45 @@
     for n in range(base_dev // tile):
         match = jnp.where(places == slots - n * tile, 1.0, 0.0).astype(jnp.bfloat16)
         sums = jnp.dot(left, match, preferred_element_type=jnp.float32)
-        stacked = sums[:columns] / jnp.maximum(sums[columns : columns + 1], 1.0)
-        at_n = slice(n * tile, (n + 1) * tile)
+        stacked = sums[:columns] * (1.0 / jnp.maximum(sums[columns : columns + 1], 1.0))
+        high = stacked.astype(jnp.bfloat16)
+        rest = (stacked - high.astype(jnp.float32)) * STACK_REST
+        again = stacked * STACK
+        straight = slice(n * tile, (n + 1) * tile)
+        crossed = slice(base_dev + n * tile, base_dev + (n + 1) * tile)
         for m in range(mwin):
             at = 2 * half * m
-            real, imag = stacked[at : at + half], stacked[at + half : at + 2 * half]
-            for r, value in enumerate((stacked[at : at + 2 * half], (imag, -real))):
-                if r:
-                    value = jnp.concatenate(value, axis=0)
-                high = value.astype(jnp.bfloat16)
-                low = (value - high.astype(jnp.float32)).astype(jnp.bfloat16)
-                left_ref[m, r, : 2 * half, at_n] = high
-                left_ref[m, r, 2 * half :, at_n] = low
-    project(left_ref, high_ref, low_ref, send_ref)
-
-
-def project(left_ref, high_ref, low_ref, out_ref):
-    mwin, _, rows, base_dev = left_ref.shape
-    half = rows // 2
-    chips, _, width = out_ref.shape
+            real, imag = slice(at, at + half), slice(at + half, at + 2 * half)
+            upper, lower = slice(0, half), slice(half, 2 * half)
+            for value, to in (
+                (high, left_ref.at[m]),
+                (rest, small_ref.at[m, 0]),
+                (again, small_ref.at[m, 1]),
+            ):
+                to[upper, straight] = value[real].astype(to.dtype)
+                to[lower, straight] = value[imag].astype(to.dtype)
+                to[upper, crossed] = value[imag].astype(to.dtype)
+                to[lower, crossed] = (-value[real]).astype(to.dtype)
+    project(left_ref, small_ref, *held, *send_refs)
+
+
+def project(left_ref, small_ref, high_ref, again_ref, rest_ref, *out_refs):
+    mwin, half, depth = left_ref.shape
+    width = out_refs[0].shape[2]
     for m in range(mwin):
-        total = None
-        for r in range(2):
-            plane = slice((2 * m + r) * base_dev, (2 * m + r + 1) * base_dev)
-            both = jnp.dot(
-                left_ref[m, r], high_ref[plane], preferred_element_type=jnp.float32
-            )
-            rest = jnp.dot(
-                left_ref[m, r, :half], low_ref[plane], preferred_element_type=jnp.float32
-            )
-            term = both[:half] + (both[half:] + rest)
-            total = term if total is None else total + term
-        for k in range(chips):
-            out_ref[k, m * half : (m + 1) * half] = total[:, k * width : (k + 1) * width]
-
-
-def keep_kernel(left_ref, high_ref, low_ref, *refs):
-    keep_ref = refs[-1]
-    project(left_ref, high_ref, low_ref, keep_ref)
+        planes = slice(m * depth, (m + 1) * depth)
+        rough = jnp.dot(left_ref[m], high_ref[planes], preferred_element_type=jnp.float32)
+        fine = jnp.dot(
+            small_ref[m, 0], again_ref[planes], preferred_element_type=jnp.float32
+        ) + jnp.dot(small_ref[m, 1], rest_ref[planes], preferred_element_type=jnp.float32)
+        total = rough + fine * (1.0 / (BEAM * STACK_REST))
+        blocks = [out_ref.at[i] for out_ref in out_refs for i in range(out_ref.shape[0])]
+        for i, block_ref in enumerate(blocks):
+            block_ref[m * half : (m + 1) * half] = total[:, i * width : (i + 1) * width]
+
+
+def keep_kernel(*refs):
+    project(*refs[:5], refs[-1])
 
 
 def staged(visibility, pair_counts, owner_ids, slot_ids, beam):
@@ -206,34 +220,39 @@
     anywhere = pl.BlockSpec(memory_space=pl.ANY)
     block = jax.ShapeDtypeStruct((chips, size, columns), jnp.bfloat16)
     facts = [value.reshape(1, rows) for value in (pair_counts, owner_ids, slot_ids)]
-    mine, theirs = pl.pallas_call(
+    chunk = 512
+    planes = beam.reshape(mwin * 2 * base_dev, modes)
+    mine, theirs, start = pl.pallas_call(
         functools.partial(pack_kernel, peers, capacity),
-        out_shape=(block, block),
-        in_specs=[anywhere] * 4,
-        out_specs=(vmem, vmem),
+        out_shape=(block, block, pltpu.VMEM((AHEAD * chunk, modes), jnp.float32)),
+        in_specs=[anywhere] * 5,
+        out_specs=(vmem,) * 3,
         scratch_shapes=[pltpu.VMEM((rows, columns), jnp.bfloat16)]
         + [pltpu.VMEM((1, rows), jnp.int32)] * 3
-        + [pltpu.SemaphoreType.DMA((4,))],
+        + [pltpu.SemaphoreType.DMA((5,))],
         compiler_params=pltpu.CompilerParams(vmem_limit_bytes=8 * MIB),
         name="pack",
-    )(*[pltpu.with_memory_space_constraint(value, pltpu.HBM) for value in (visibility[0], *facts)])
+    )(
+        *[
+            pltpu.with_memory_space_constraint(value, pltpu.HBM)
+            for value in (visibility[0], *facts, planes)
+        ]
+    )
     got = swap(theirs, "pair", 1)
     pieces = [jnp.concatenate([mine[k], got[k]], axis=0) for k in range(chips)]
     order = [k for k in range(1, chips) if k & (chips // 2)] + [
         k for k in range(1, chips) if not k & (chips // 2)
     ]
     moved = {k: swap(pieces[k], "pair", 2 * k) for k in order}
-    chunk = 512
-    planes = beam.reshape(mwin * 2 * base_dev, modes)
     held = pl.pallas_call(
         functools.partial(load_kernel, peers, chunk),
         out_shape=tuple(
-            pltpu.VMEM((planes.shape[0], len(owners) * width), jnp.bfloat16)
+            pltpu.VMEM((planes.shape[0], len(owners) * width), dtype)
             for owners in groups(peers)
-            for _ in range(2)
+            for dtype in (jnp.bfloat16, SMALL, SMALL)
         ),
-        in_specs=[anywhere, anywhere],
-        out_specs=(vmem,) * 6,
+        in_specs=[anywhere, vmem, anywhere],
+        out_specs=(vmem,) * 9,
         scratch_shapes=[
             pltpu.VMEM((4, chunk, modes), jnp.float32),
             pltpu.SemaphoreType.DMA((4,)),
@@ -243,7 +262,7 @@
             flops=0, bytes_accessed=8 * planes.size, transcendentals=0
         ),
         name="load",
-    )(planes, pieces[0])
+    )(planes, pltpu.with_memory_space_constraint(start, pltpu.VMEM), pieces[0])
     held = [pltpu.with_memory_space_constraint(part, pltpu.VMEM) for part in held]
     def products(count):
         return jax.ShapeDtypeStruct((count, columns, width), jnp.float32)
@@ -252,34 +271,38 @@
         flops = 6 * mwin * 2 * (columns // mwin) * base_dev * count * width
         return pl.CostEstimate(flops=flops, bytes_accessed=0, transcendentals=0)
 
-    left, send = pl.pallas_call(
+    left, small, near_send, far_send = pl.pallas_call(
         functools.partial(stack_kernel, peers, capacity, mwin),
         out_shape=(
-            pltpu.VMEM((mwin, 2, 2 * columns // mwin, base_dev), jnp.bfloat16),
-            products(chips),
+            pltpu.VMEM((mwin, columns // mwin, 2 * base_dev), jnp.bfloat16),
+            pltpu.VMEM((mwin, 2, columns // mwin, 2 * base_dev), SMALL),
+            products(chips // 2),
+            products(chips // 2),
         ),
-        in_specs=[vmem] * (chips + 2),
-        out_specs=(vmem, vmem),
+        in_specs=[vmem] * (chips + 3),
+        out_specs=(vmem,) * 4,
         compiler_params=pltpu.CompilerParams(vmem_limit_bytes=12 * MIB),
         cost_estimate=cost(chips),
         name="stack",
-    )(pieces[0], *[moved[k] for k in order], *held[:2])
-    got = swap(send, "pair", 1)
-    left = pltpu.with_memory_space_constraint(left, pltpu.VMEM)
+    )(pieces[0], *[moved[k] for k in order], *held[:3])
+    far_got, near_got = swap(far_send, "pair", 1), swap(near_send, "pair", 1)
+    left, small = [pltpu.with_memory_space_constraint(part, pltpu.VMEM) for part in (left, small)]
     summed, after = {}, []
-    for name, parts, owners in zip(("far", "near"), (held[2:4], held[4:6]), groups(peers)[1:]):
+    for name, got, parts, owners in zip(
+        ("far", "near"), (far_got, near_got), (held[3:6], held[6:9]), groups(peers)[1:]
+    ):
         keep = pl.pallas_call(
             keep_kernel,
             out_shape=products(len(owners)),
-            in_specs=[vmem] * 3 + [anywhere] * len(after),
+            in_specs=[vmem] * 5 + [anywhere] * len(after),
             out_specs=vmem,
             compiler_params=pltpu.CompilerParams(vmem_limit_bytes=12 * MIB),
             cost_estimate=cost(len(owners)),
             name=name,
-        )(left, *parts, *after)
+        )(left, small, *parts, *after)
         for i, j in enumerate(owners):
             k = j // 2
-            summed[k] = keep[i] + got[k]
+            summed[k] = keep[i] + got[i]
             if k:
                 summed[k] = summed[k].astype(jnp.bfloat16)
             if k & (chips // 2):
@@ -288,15 +311,19 @@
     for k in order:
         if not k & (chips // 2):
             amplitudes = lax.optimization_barrier(amplitudes)
-        amplitudes = amplitudes + swap(summed[k], "pair", 2 * k).astype(jnp.float32)
+        partial = amplitudes
+        last = swap(summed[k], "pair", 2 * k)
+        amplitudes = partial + last.astype(jnp.float32)
+    partial, last = lax.optimization_barrier((partial, last))
+    modes_out = partial + last.astype(jnp.float32)
     sets = columns // (2 * mwin)
     power = jnp.sum((amplitudes * amplitudes).reshape(mwin, 2 * sets, width), axis=1)
-    distance = 1
-    while distance < lax.axis_size("chan"):
-        power = power + swap(power, "chan", distance)
-        distance *= 2
+    terms = [power] + [swap(power, "chan", d) for d in range(1, lax.axis_size("chan"))]
+    while len(terms) > 1:
+        terms = [one + other for one, other in zip(terms[::2], terms[1::2])]
+    power = terms[0]
     power = power / (lax.axis_size("chan") * sets)
-    shaped = amplitudes.reshape(mwin, 2, sets, width).transpose(3, 0, 1, 2)
+    shaped = modes_out.reshape(mwin, 2, sets, width).transpose(3, 0, 1, 2)
     return shaped[None], power.T
 
 

time: 49.6 us -> 46.8 us (0.944)
  Pallas kernels: 23.9 us -> 21.2 us
  waiting for transfers between devices: 9.46 us -> 8.35 us
  starting transfers between devices: 13.9 us -> 14.9 us
    ppermute x10 -> x12, waiting for transfers between devices: 9.46 us -> 8.35 us  [swap(): return lax.ppermute(value, axis, [(i, i ^ distance) for i in range(size)])]
    pallas_call x2, Pallas kernels: 4.01 us -> 2.91 us  [staged(): pl.pallas_call(keep_kernel, out_shape=products(len(owners)), in_specs=[vm...]
    pallas_call x1, Pallas kernels: 11.3 us -> 10.3 us  [staged(): pl.pallas_call(functools.partial(load_kernel, peers, chunk), out_shape=tu...]
    ppermute x10 -> x12, starting transfers between devices: 13.9 us -> 14.9 us  [swap(): return lax.ppermute(value, axis, [(i, i ^ distance) for i in range(size)])]
    pallas_call x1, Pallas kernels: 6.37 us -> 5.59 us  [staged(): pl.pallas_call(functools.partial(stack_kernel, peers, capacity, mwin), ou...]
    add x2, other arithmetic: 0.04 us -> 0.7 us  [the longest x1 0.67 us: staged(): modes_out = partial + last.astype(jnp.float32)]
    reduce_sum x1, other arithmetic: 0.67 us -> 0.04 us  [staged(): jnp.sum((amplitudes * amplitudes).reshape(mwin, 2 * sets, width), axis=1)]
  transfers between devices with their start and end apart: 10 -> 12, of which waited for: 5 -> 7; matrix products, arithmetic and copies ran while one was open for 0% -> 2% of each run, Pallas kernels for 31% -> 28%
where the time goes in v4:
time: 46.8 us; the launch traced here: 46.6 us
  Pallas kernels  21.2 us (45%)
  starting transfers between devices  14.9 us (32%)
  waiting for transfers between devices  8.35 us (18%)
  other arithmetic  1.4 us (3%)
  between operations  0.76 us (2%)
    ppermute x12, starting transfers between devices, swap(): return lax.ppermute(value, axis, [(i, i ^ distance) for i in range(size)])  14.9 us
    pallas_call x1, Pallas kernels, staged(): pl.pallas_call(functools.partial(load_kernel, peers, chunk), out_shape=tu...  10.3 us
    ppermute x12, waiting for transfers between devices, swap(): return lax.ppermute(value, axis, [(i, i ^ distance) for i in range(size)])  8.35 us
    pallas_call x1, Pallas kernels, staged(): pl.pallas_call(functools.partial(stack_kernel, peers, capacity, mwin), ou...  5.59 us
    pallas_call x2, Pallas kernels, staged(): pl.pallas_call(keep_kernel, out_shape=products(len(owners)), in_specs=[vm...  2.91 us
    pallas_call x1, Pallas kernels, staged(): pl.pallas_call(functools.partial(pack_kernel, peers, capacity), out_shape...  2.37 us
  transfers between devices with their start and end apart: 12, of which 7 were waited for; matrix products, arithmetic and copies ran while one was open for 2% of the time, Pallas kernels for 28%

profile of v4, /device:TPU:0, one launch (start us, length us, event | category | flops | bytes accessed | tf_op | source)
XLA Modules:
  0.0 46.6 jit_solution(15559202382754568353)
XLA Ops:
  0.6 2.4 %pack.1 = (bf16[4,136,256]{2,1,0:T(8,128)(2,1)S(1)}, bf16[4,136,256]{2,1,0:T(8,128)(2,1)S(1)}, f32[1024,1024]{1,0:T(8,128)S(1)}) custom-call(bf16[512,256]{1,0:T(8,128)(2,1)} %bitcast.44, s32[1,512]{1,0:T(1,128)} %bitcast.46, s32[1,512]{1,0:T(1,128)} %bitcast.47, s32[1,512]{1,0:T(1,128)} %bitcast.48, f32[8192,1024]{1,0:T(8,128)} %bitcast.42), custom_call_target="tpu_custom_call" | custom-call | tf_op jit(solution)/shard_map/pack/pallas_call | solution.py:225
  3.0 0.5 %collective-permute-start = (bf16[4,136,256]{2,1,0:T(8,128)(2,1)S(1)}, bf16[4,136,256]{2,1,0:T(8,128)(2,1)S(1)}, u32[]{:S(2)}, u32[]{:S(2)}) collective-permute-start(bf16[4,136,256]{2,1,0:T(8,128)(2,1)S(1)} %get-tuple-element.21), channel_id=1, source_target_pairs={{0,1},{1,0},{2,3},{3,2},{4,5},{5,4},{6,7},{7,6},{8,9},{9,8},{10,11... | collective-permute-start | bytes 835592 | tf_op jit(solution)/shard_map/ppermute | solution.py:27
  3.6 1.2 %collective-permute-done = bf16[4,136,256]{2,1,0:T(8,128)(2,1)S(1)} collective-permute-done((bf16[4,136,256]{2,1,0:T(8,128)(2,1)S(1)}, bf16[4,136,256]{2,1,0:T(8,128)(2,1)S(1)}, u32[]{:S(2)}, u32[]{:S(2)}) %collective-permute-start) | collective-permute-done | bytes 278560 | tf_op jit(solution)/shard_map/ppermute | solution.py:27
  4.8 4.0 %collective-permute-start.1 = (bf16[272,256]{1,0:T(8,128)(2,1)S(1)}, bf16[272,256]{1,0:T(8,128)(2,1)S(1)}, u32[]{:S(2)}, u32[]{:S(2)}) collective-permute-start(bf16[272,256]{1,0:T(8,128)(2,1)S(1)} %pad_maximum_fusion.1), channel_id=1, source_target_pairs={{0,4},{1,5},{2,6},{3,7},{4,0},{5,1},{6,2},{7,3},{8,12},{9,13},{10,... | collective-permute-start | bytes 417800 | tf_op jit(solution)/shard_map/ppermute | solution.py:27
  8.8 1.4 %collective-permute-start.2 = (bf16[272,256]{1,0:T(8,128)(2,1)S(1)}, bf16[272,256]{1,0:T(8,128)(2,1)S(1)}, u32[]{:S(2)}, u32[]{:S(2)}) collective-permute-start(bf16[272,256]{1,0:T(8,128)(2,1)S(1)} %pad_maximum_fusion.2), channel_id=1, source_target_pairs={{0,6},{1,7},{2,4},{3,5},{4,2},{5,3},{6,0},{7,1},{8,14},{9,15},{10,... | collective-permute-start | bytes 417800 | tf_op jit(solution)/shard_map/ppermute | solution.py:27
  10.2 0.3 collective-permute-start.3
  10.5 10.3 %load.1 = (bf16[8192,512]{1,0:T(8,128)(2,1)S(1)}, f8e5m2[8192,512]{1,0:T(32,128)(4,1)S(1)}, f8e5m2[8192,512]{1,0:T(32,128)(4,1)S(1)}, bf16[8192,256]{1,0:T(8,128...) custom-call(f32[8192,1024]{1,0:T(8,128)} %bitcast.43, ...), custom_call_target="tpu_custom_call" | custom-call | bytes 67108864 | tf_op jit(solution)/shard_map/load/pallas_call | solution.py:247
  20.8 0.0 collective-permute-done.1.refs_1_
  20.9 0.0 collective-permute-done.2.refs_2_
  20.9 0.0 collective-permute-done.3.refs_3_
  20.9 5.6 %stack.1 = (bf16[2,128,4096]{2,1,0:T(8,128)(2,1)S(1)}, f8e5m2[2,2,128,4096]{3,2,1,0:T(32,128)(4,1)S(1)}, f32[2,256,128]{2,1,0:T(8,128)S(1)}, f32[2,256,128]{2,1,0:T(8,128)S(1)}) custom-call(bf16[272,256]{1,0:T(8,128)(2,1)S(1)} %pad_maximum_fusion.after_ref.refs_0_, bf16[272,256]{1,0:T(8,128)(2,1)S(1)} %collective-permute-done.1.refs_1_, ...), custom_call_target="tpu_custom_call" | custom-call | flops 3221225472 | tf_op jit(solution)/shard_map/stack/pallas_call | solution.py:274
  26.5 0.1 collective-permute-start.4
  26.6 0.5 %collective-permute-start.5 = (f32[2,256,128]{2,1,0:T(8,128)S(1)}, f32[2,256,128]{2,1,0:T(8,128)S(1)}, u32[]{:S(2)}, u32[]{:S(2)}) collective-permute-start(f32[2,256,128]{2,1,0:T(8,128)S(1)} %get-tuple-element.35), channel_id=1, source_target_pairs={{0,1},{1,0},{2,3},{3,2},{4,5},{5,4},{6,7},{7,6},{8,9},{9,8},{10,11... | collective-permute-start | bytes 786440 | tf_op jit(solution)/shard_map/ppermute | solution.py:27
  27.1 1.5 %far.1 = f32[2,256,128]{2,1,0:T(8,128)S(1)} custom-call(bf16[2,128,4096]{2,1,0:T(8,128)(2,1)S(1)} %get-tuple-element.26.refs_0_, f8e5m2[2,2,128,4096]{3,2,1,0:T(32,128)(4,1)S(1)} %get-tuple-element.27.refs_1_, bf16[8192,256]{1,0:T(8,128)(2,1)S(1)} %get-tuple-element.31.refs_2_, f8e5m2[8192,256]{1,0:T(32,128)(4,1)S(1)} %get-tuple-element.32.refs_3_, ...), custom_call_target="tpu_custom_call" | custom-call | flops 1610612736 | tf_op jit(solution)/shard_map/far/pallas_call | solution.py:294
  28.6 0.0 collective-permute-done.4
  28.6 3.0 %collective-permute-start.7 = (bf16[256,128]{1,0:T(8,128)(2,1)S(1)}, bf16[256,128]{1,0:T(8,128)(2,1)S(1)}, u32[]{:S(2)}, u32[]{:S(2)}) collective-permute-start(bf16[256,128]{1,0:T(8,128)(2,1)S(1)} %get-tuple-element.38.refs_6_), channel_id=1, source_target_pairs={{0,6},{1,7},{2,4},{3,5},{4,2},{5,3},{6,0},{7,1},{8,14},{9,15},{10,... | collective-permute-start | bytes 196616 | tf_op jit(solution)/shard_map/ppermute | solution.py:27
  31.6 0.7 %collective-permute-start.6 = (bf16[256,128]{1,0:T(8,128)(2,1)S(1)}, bf16[256,128]{1,0:T(8,128)(2,1)S(1)}, u32[]{:S(2)}, u32[]{:S(2)}) collective-permute-start(bf16[256,128]{1,0:T(8,128)(2,1)S(1)} %get-tuple-element.39.refs_5_), channel_id=1, source_target_pairs={{0,4},{1,5},{2,6},{3,7},{4,0},{5,1},{6,2},{7,3},{8,12},{9,13},{10,... | collective-permute-start | bytes 196616 | tf_op jit(solution)/shard_map/ppermute | solution.py:27
  32.3 1.4 %near.1 = f32[2,256,128]{2,1,0:T(8,128)S(1)} custom-call(bf16[2,128,4096]{2,1,0:T(8,128)(2,1)S(1)} %get-tuple-element.26.refs_0_, f8e5m2[2,2,128,4096]{3,2,1,0:T(32,128)(4,1)S(1)} %get-tuple-element.27.refs_1_, bf16[8192,256]{1,0:T(8,128)(2,1)S(1)} %get-tuple-element.28.refs_2_, f8e5m2[8192,256]{1,0:T(32,128)(4,1)S(1)} %get-tuple-element.29.refs_3_, ...), custom_call_target="tpu_custom_call" | custom-call | flops 1610612736 | tf_op jit(solution)/shard_map/near/pallas_call | solution.py:294
  33.7 0.0 collective-permute-done.5
  33.7 0.8 %collective-permute-start.8 = (bf16[256,128]{1,0:T(8,128)(2,1)S(1)}, bf16[256,128]{1,0:T(8,128)(2,1)S(1)}, u32[]{:S(2)}, u32[]{:S(2)}) collective-permute-start(bf16[256,128]{1,0:T(8,128)(2,1)S(1)} %fusion.8), channel_id=1, source_target_pairs={{0,2},{1,3},{2,0},{3,1},{4,6},{5,7},{6,4},{7,5},{8,10},{9,11},{10,... | collective-permute-start | bytes 196616 | tf_op jit(solution)/shard_map/ppermute | solution.py:27
  34.6 0.2 collective-permute-done.7
  34.8 4.1 %collective-permute-done.6 = bf16[256,128]{1,0:T(8,128)(2,1)S(1)} collective-permute-done((bf16[256,128]{1,0:T(8,128)(2,1)S(1)}, bf16[256,128]{1,0:T(8,128)(2,1)S(1)}, u32[]{:S(2)}, u32[]{:S(2)}) %collective-permute-start.6) | collective-permute-done | bytes 65568 | tf_op jit(solution)/shard_map/ppermute | solution.py:27
  38.9 0.5 %collective-permute-done.8 = bf16[256,128]{1,0:T(8,128)(2,1)S(1)} collective-permute-done((bf16[256,128]{1,0:T(8,128)(2,1)S(1)}, bf16[256,128]{1,0:T(8,128)(2,1)S(1)}, u32[]{:S(2)}, u32[]{:S(2)}) %collective-permute-start.8) | collective-permute-done | bytes 65568 | tf_op jit(solution)/shard_map/ppermute | solution.py:27
  39.4 2.5 %collective-permute-start.11 = (f32[2,128]{1,0:T(2,128)S(1)}, f32[2,128]{1,0:T(2,128)S(1)}, u32[]{:S(2)}, u32[]{:S(2)}) collective-permute-start(f32[2,128]{1,0:T(2,128)S(1)} %bitcast_reduce_fusion), channel_id=1, source_target_pairs={{0,24},{8,16},{16,8},{24,0},{1,25},{9,17},{17,9},{25,1},{2,26},{10... | collective-permute-start | bytes 3080 | tf_op jit(solution)/shard_map/ppermute | solution.py:27
  41.9 0.5 %collective-permute-start.10 = (f32[2,128]{1,0:T(2,128)S(1)}, f32[2,128]{1,0:T(2,128)S(1)}, u32[]{:S(2)}, u32[]{:S(2)}) collective-permute-start(f32[2,128]{1,0:T(2,128)S(1)} %bitcast_reduce_fusion), channel_id=1, source_target_pairs={{0,16},{8,24},{16,0},{24,8},{1,17},{9,25},{17,1},{25,9},{2,18},{10... | collective-permute-start | bytes 3080 | tf_op jit(solution)/shard_map/ppermute | solution.py:27
  42.5 0.5 %collective-permute-start.9 = (f32[2,128]{1,0:T(2,128)S(1)}, f32[2,128]{1,0:T(2,128)S(1)}, u32[]{:S(2)}, u32[]{:S(2)}) collective-permute-start(f32[2,128]{1,0:T(2,128)S(1)} %bitcast_reduce_fusion), channel_id=1, source_target_pairs={{0,8},{8,0},{16,24},{24,16},{1,9},{9,1},{17,25},{25,17},{2,10},{10... | collective-permute-start | bytes 3080 | tf_op jit(solution)/shard_map/ppermute | solution.py:27
  43.0 0.7 %convert_add_fusion = f32[256,128]{1,0:T(8,128)} fusion(f32[256,128]{1,0:T(8,128)S(1)} %fusion.3, bf16[256,128]{1,0:T(8,128)(2,1)S(1)} %collective-permute-done.8), kind=kLoop, calls=%fused_computation.16 | loop fusion | flops 65536 | bytes 327680 | tf_op jit(solution)/shard_map/add | solution.py:318
  43.7 0.3 collective-permute-done.11
  44.0 1.5 %collective-permute-done.10 = f32[2,128]{1,0:T(2,128)S(1)} collective-permute-done((f32[2,128]{1,0:T(2,128)S(1)}, f32[2,128]{1,0:T(2,128)S(1)}, u32[]{:S(2)}, u32[]{:S(2)}) %collective-permute-start.10) | collective-permute-done | bytes 1056 | tf_op jit(solution)/shard_map/ppermute | solution.py:27
  45.5 0.5 %collective-permute-done.9 = f32[2,128]{1,0:T(2,128)S(1)} collective-permute-done((f32[2,128]{1,0:T(2,128)S(1)}, f32[2,128]{1,0:T(2,128)S(1)}, u32[]{:S(2)}, u32[]{:S(2)}) %collective-permute-start.9) | collective-permute-done | bytes 1056 | tf_op jit(solution)/shard_map/ppermute | solution.py:27
  46.0 0.6 %multiply_bitcast_fusion = f32[128,2]{0,1:T(2,128)} fusion(f32[2,128]{1,0:T(2,128)S(1)} %collective-permute-done.10, f32[2,128]{1,0:T(2,128)S(1)} %collective-permute-done.11, f32[2,128]{1,0:T(2,128)S(1)} %bitcast_reduce_fusion, f32[2,128]{1,0:T(2,128)S(1)} %collective-permute-done.9), kind=kLoop, calls=%fused_computation.28 | loop fusion | flops 1024 | bytes 5120 | tf_op jit(solution)/shard_map/transpose | solution.py:327
  (10 shorter events, 0.2 us)
Async XLA Ops:
  3.0 1.7 %collective-permute-start = (bf16[4,136,256]{2,1,0:T(8,128)(2,1)S(1)}, bf16[4,136,256]{2,1,0:T(8,128)(2,1)S(1)}, u32[]{:S(2)}, u32[]{:S(2)}) collective-permute-start(bf16[4,136,256]{2,1,0:T(8,128)(2,1)S(1)} %get-tuple-element.21), channel_id=1, source_target_pairs={{0,1},{1,0},{2,3},{3,2},{4,5},{5,4},{6,7},{7,6},{8,9},{9,8},{10,11... | collective-permute-start | bytes 835592 | tf_op jit(solution)/shard_map/ppermute | solution.py:27
  4.8 16.1 %collective-permute-start.1 = (bf16[272,256]{1,0:T(8,128)(2,1)S(1)}, bf16[272,256]{1,0:T(8,128)(2,1)S(1)}, u32[]{:S(2)}, u32[]{:S(2)}) collective-permute-start(bf16[272,256]{1,0:T(8,128)(2,1)S(1)} %pad_maximum_fusion.1), channel_id=1, source_target_pairs={{0,4},{1,5},{2,6},{3,7},{4,0},{5,1},{6,2},{7,3},{8,12},{9,13},{10,... | collective-permute-start | bytes 417800 | tf_op jit(solution)/shard_map/ppermute | solution.py:27
  8.8 12.1 %collective-permute-start.2 = (bf16[272,256]{1,0:T(8,128)(2,1)S(1)}, bf16[272,256]{1,0:T(8,128)(2,1)S(1)}, u32[]{:S(2)}, u32[]{:S(2)}) collective-permute-start(bf16[272,256]{1,0:T(8,128)(2,1)S(1)} %pad_maximum_fusion.2), channel_id=1, source_target_pairs={{0,6},{1,7},{2,4},{3,5},{4,2},{5,3},{6,0},{7,1},{8,14},{9,15},{10,... | collective-permute-start | bytes 417800 | tf_op jit(solution)/shard_map/ppermute | solution.py:27
  10.2 10.6 %collective-permute-start.3 = (bf16[272,256]{1,0:T(8,128)(2,1)S(1)}, bf16[272,256]{1,0:T(8,128)(2,1)S(1)}, u32[]{:S(2)}, u32[]{:S(2)}) collective-permute-start(bf16[272,256]{1,0:T(8,128)(2,1)S(1)} %pad_maximum_fusion.3), channel_id=1, source_target_pairs={{0,2},{1,3},{2,0},{3,1},{4,6},{5,7},{6,4},{7,5},{8,10},{9,11},{10,... | collective-permute-start | bytes 417800 | tf_op jit(solution)/shard_map/ppermute | solution.py:27
  26.5 2.1 %collective-permute-start.4 = (f32[2,256,128]{2,1,0:T(8,128)S(1)}, f32[2,256,128]{2,1,0:T(8,128)S(1)}, u32[]{:S(2)}, u32[]{:S(2)}) collective-permute-start(f32[2,256,128]{2,1,0:T(8,128)S(1)} %get-tuple-element.34), channel_id=1, source_target_pairs={{0,1},{1,0},{2,3},{3,2},{4,5},{5,4},{6,7},{7,6},{8,9},{9,8},{10,11... | collective-permute-start | bytes 786440 | tf_op jit(solution)/shard_map/ppermute | solution.py:27
  26.6 7.1 %collective-permute-start.5 = (f32[2,256,128]{2,1,0:T(8,128)S(1)}, f32[2,256,128]{2,1,0:T(8,128)S(1)}, u32[]{:S(2)}, u32[]{:S(2)}) collective-permute-start(f32[2,256,128]{2,1,0:T(8,128)S(1)} %get-tuple-element.35), channel_id=1, source_target_pairs={{0,1},{1,0},{2,3},{3,2},{4,5},{5,4},{6,7},{7,6},{8,9},{9,8},{10,11... | collective-permute-start | bytes 786440 | tf_op jit(solution)/shard_map/ppermute | solution.py:27
  28.6 6.2 %collective-permute-start.7 = (bf16[256,128]{1,0:T(8,128)(2,1)S(1)}, bf16[256,128]{1,0:T(8,128)(2,1)S(1)}, u32[]{:S(2)}, u32[]{:S(2)}) collective-permute-start(bf16[256,128]{1,0:T(8,128)(2,1)S(1)} %get-tuple-element.38.refs_6_), channel_id=1, source_target_pairs={{0,6},{1,7},{2,4},{3,5},{4,2},{5,3},{6,0},{7,1},{8,14},{9,15},{10,... | collective-permute-start | bytes 196616 | tf_op jit(solution)/shard_map/ppermute | solution.py:27
  31.6 7.3 %collective-permute-start.6 = (bf16[256,128]{1,0:T(8,128)(2,1)S(1)}, bf16[256,128]{1,0:T(8,128)(2,1)S(1)}, u32[]{:S(2)}, u32[]{:S(2)}) collective-permute-start(bf16[256,128]{1,0:T(8,128)(2,1)S(1)} %get-tuple-element.39.refs_5_), channel_id=1, source_target_pairs={{0,4},{1,5},{2,6},{3,7},{4,0},{5,1},{6,2},{7,3},{8,12},{9,13},{10,... | collective-permute-start | bytes 196616 | tf_op jit(solution)/shard_map/ppermute | solution.py:27
  33.7 5.7 %collective-permute-start.8 = (bf16[256,128]{1,0:T(8,128)(2,1)S(1)}, bf16[256,128]{1,0:T(8,128)(2,1)S(1)}, u32[]{:S(2)}, u32[]{:S(2)}) collective-permute-start(bf16[256,128]{1,0:T(8,128)(2,1)S(1)} %fusion.8), channel_id=1, source_target_pairs={{0,2},{1,3},{2,0},{3,1},{4,6},{5,7},{6,4},{7,5},{8,10},{9,11},{10,... | collective-permute-start | bytes 196616 | tf_op jit(solution)/shard_map/ppermute | solution.py:27
  39.4 4.5 %collective-permute-start.11 = (f32[2,128]{1,0:T(2,128)S(1)}, f32[2,128]{1,0:T(2,128)S(1)}, u32[]{:S(2)}, u32[]{:S(2)}) collective-permute-start(f32[2,128]{1,0:T(2,128)S(1)} %bitcast_reduce_fusion), channel_id=1, source_target_pairs={{0,24},{8,16},{16,8},{24,0},{1,25},{9,17},{17,9},{25,1},{2,26},{10... | collective-permute-start | bytes 3080 | tf_op jit(solution)/shard_map/ppermute | solution.py:27
  41.9 3.6 %collective-permute-start.10 = (f32[2,128]{1,0:T(2,128)S(1)}, f32[2,128]{1,0:T(2,128)S(1)}, u32[]{:S(2)}, u32[]{:S(2)}) collective-permute-start(f32[2,128]{1,0:T(2,128)S(1)} %bitcast_reduce_fusion), channel_id=1, source_target_pairs={{0,16},{8,24},{16,0},{24,8},{1,17},{9,25},{17,1},{25,9},{2,18},{10... | collective-permute-start | bytes 3080 | tf_op jit(solution)/shard_map/ppermute | solution.py:27
  42.5 3.6 %collective-permute-start.9 = (f32[2,128]{1,0:T(2,128)S(1)}, f32[2,128]{1,0:T(2,128)S(1)}, u32[]{:S(2)}, u32[]{:S(2)}) collective-permute-start(f32[2,128]{1,0:T(2,128)S(1)} %bitcast_reduce_fusion), channel_id=1, source_target_pairs={{0,8},{8,0},{16,24},{24,16},{1,9},{9,1},{17,25},{25,17},{2,10},{10... | collective-permute-start | bytes 3080 | tf_op jit(solution)/shard_map/ppermute | solution.py:27

commit v5 on v4

--- a/solution.py
+++ b/solution.py
@@ -28,8 +28,8 @@
 
 
 def pack_kernel(peers, capacity, *refs):
-    sources, beam_ref, (mine_ref, theirs_ref, start_ref) = refs[:4], refs[4], refs[5:8]
-    held, sems = refs[8:12], refs[12]
+    sources, beam_ref, out_refs, start_ref = refs[:4], refs[4], refs[5 : 5 + peers // 2], refs[-6]
+    held, sems = refs[-5:-1], refs[-1]
     copies = [
         pltpu.make_async_copy(source, target, sems.at[i])
         for i, (source, target) in enumerate(zip(sources, held))
@@ -68,19 +68,22 @@
             jnp.where(line == first % 8 + 2, weight, 0.0),
         ),
     ).astype(jnp.bfloat16)
-    places = lax.broadcasted_iota(jnp.int32, (columns, rows), 0)
+    places = lax.broadcasted_iota(jnp.int32, (padded, rows), 0)
     beyond = (lax.broadcasted_iota(jnp.int32, (8, columns), 0) == first % 8) & (
         lax.broadcasted_iota(jnp.int32, (8, columns), 1) >= capacity
     )
+    blocks = []
     for j in range(peers):
         match = places == jnp.where(relative == j, rank, -1)
         named = dot_rows(facts, jnp.where(match, 1.0, 0.0).astype(jnp.bfloat16))
+        named = jnp.concatenate([named, jnp.zeros((8, columns - padded), jnp.float32)], axis=1)
         named = jnp.where(beyond, 255.0, named)
-        scaled = jnp.where(match[:padded], weight, 0.0).astype(jnp.bfloat16)
+        scaled = jnp.where(match, weight, 0.0).astype(jnp.bfloat16)
         body = jnp.dot(scaled, vis_ref[...], preferred_element_type=jnp.float32)
-        block = jnp.concatenate([body[: size - 8], body[size - 8 : size] + named], axis=0)
-        out_ref = theirs_ref if j % 2 else mine_ref
-        out_ref[j // 2] = block.astype(jnp.bfloat16)
+        blocks += [body[: size - 8], body[size - 8 : size] + named]
+        if j % 2:
+            out_refs[j // 2][...] = jnp.concatenate(blocks, axis=0).astype(jnp.bfloat16)
+            blocks = []
     ahead.wait()
 
 
@@ -100,7 +103,8 @@
 
 
 def load_kernel(peers, chunk, beam_ref, start_ref, after_ref, *refs):
-    outs, buffer, sems = (refs[:3], refs[3:6], refs[6:9]), refs[9], refs[10]
+    outs, done_ref, buffer, sems = (refs[:3], refs[3:6], refs[6:9]), refs[9], refs[10], refs[11]
+    done_ref[...] = jnp.zeros(done_ref.shape, done_ref.dtype)
     steps = beam_ref.shape[0] // chunk
     ahead = start_ref.shape[0] // chunk
     slots = buffer.shape[0]
@@ -141,38 +145,58 @@
             copy(step + slots).start()
 
 
-def stack_kernel(peers, capacity, mwin, *refs):
-    pieces = refs[: peers // 2]
-    held, (left_ref, small_ref, *send_refs) = refs[peers // 2 : -4], refs[-4:]
+def add_up(capacity, blocks, base_dev, write):
     first, size = block_rows(capacity)
-    columns = pieces[0].shape[1]
-    base_dev = left_ref.shape[2] // 2
-    half = columns // (2 * mwin)
-    tile = 512 if base_dev % 512 == 0 else base_dev
-    rows, slots, weights = [], [], []
-    for piece in pieces:
-        values = piece[...].astype(jnp.float32)
-        rows.append(values)
-        for b in range(2):
-            facts = values[(b + 1) * size - 8 : (b + 1) * size].T[:size]
-            high = facts[:, first % 8 : first % 8 + 1]
-            low = facts[:, first % 8 + 1 : first % 8 + 2]
-            slots.append((high * 256.0 + low).astype(jnp.int32))
-            weights.append(jnp.broadcast_to(facts[:, first % 8 + 2 : first % 8 + 3], (size, 128)))
-    rows = jnp.concatenate(rows, axis=0).T
+    slots, weights = [], []
+    for block in blocks:
+        facts = block[size - 8 :].T[:size]
+        high = facts[:, first % 8 : first % 8 + 1]
+        low = facts[:, first % 8 + 1 : first % 8 + 2]
+        slots.append((high * 256.0 + low).astype(jnp.int32))
+        weights.append(jnp.broadcast_to(facts[:, first % 8 + 2 : first % 8 + 3], (size, 128)))
+    rows = jnp.concatenate(blocks, axis=0).T
     weights = jnp.concatenate(weights, axis=0).T[:16]
     slots = jnp.concatenate(slots, axis=0)
     left = jnp.concatenate([rows, weights], axis=0).astype(jnp.bfloat16)
+    tile = 512
     places = lax.broadcasted_iota(jnp.int32, (slots.shape[0], tile), 1)
     for n in range(base_dev // tile):
         match = jnp.where(places == slots - n * tile, 1.0, 0.0).astype(jnp.bfloat16)
-        sums = jnp.dot(left, match, preferred_element_type=jnp.float32)
+        write(n * tile, tile, jnp.dot(left, match, preferred_element_type=jnp.float32))
+
+
+def pass_kernel(capacity, *refs):
+    _, size = block_rows(capacity)
+    blocks = [piece[...].astype(jnp.float32)[size:] for piece in refs[:-2]]
+    refs[-1][...] = jnp.concatenate(blocks, axis=0).astype(jnp.bfloat16)
+
+
+def direct_kernel(capacity, *refs):
+    _, size = block_rows(capacity)
+    sums_ref = refs[-1]
+
+    def write(at, tile, sums):
+        sums_ref[:, at : at + tile] = sums
+
+    blocks = [piece[...].astype(jnp.float32)[:size] for piece in refs[:-2]]
+    add_up(capacity, blocks, sums_ref.shape[1], write)
+
+
+def stack_kernel(capacity, mwin, blocks_ref, direct_ref, *refs):
+    held, (left_ref, small_ref, *send_refs) = refs[:3], refs[3:]
+    _, size = block_rows(capacity)
+    columns = blocks_ref.shape[1]
+    base_dev = direct_ref.shape[1]
+    half = columns // (2 * mwin)
+
+    def write(at_n, tile, sums):
+        sums = sums + direct_ref[:, at_n : at_n + tile]
         stacked = sums[:columns] * (1.0 / jnp.maximum(sums[columns : columns + 1], 1.0))
         high = stacked.astype(jnp.bfloat16)
         rest = (stacked - high.astype(jnp.float32)) * STACK_REST
         again = stacked * STACK
-        straight = slice(n * tile, (n + 1) * tile)
-        crossed = slice(base_dev + n * tile, base_dev + (n + 1) * tile)
+        straight = slice(at_n, at_n + tile)
+        crossed = slice(base_dev + at_n, base_dev + at_n + tile)
         for m in range(mwin):
             at = 2 * half * m
             real, imag = slice(at, at + half), slice(at + half, at + 2 * half)
@@ -186,6 +210,10 @@
                 to[lower, straight] = value[imag].astype(to.dtype)
                 to[upper, crossed] = value[imag].astype(to.dtype)
                 to[lower, crossed] = (-value[real]).astype(to.dtype)
+
+    values = blocks_ref[...].astype(jnp.float32)
+    blocks = [values[i : i + size] for i in range(0, values.shape[0], size)]
+    add_up(capacity, blocks, base_dev, write)
     project(left_ref, small_ref, *held, *send_refs)
 
 
@@ -218,15 +246,15 @@
     _, size = block_rows(capacity)
     vmem = pl.BlockSpec(memory_space=pltpu.VMEM)
     anywhere = pl.BlockSpec(memory_space=pl.ANY)
-    block = jax.ShapeDtypeStruct((chips, size, columns), jnp.bfloat16)
+    block = jax.ShapeDtypeStruct((2 * size, columns), jnp.bfloat16)
     facts = [value.reshape(1, rows) for value in (pair_counts, owner_ids, slot_ids)]
     chunk = 512
     planes = beam.reshape(mwin * 2 * base_dev, modes)
-    mine, theirs, start = pl.pallas_call(
+    *pieces, start = pl.pallas_call(
         functools.partial(pack_kernel, peers, capacity),
-        out_shape=(block, block, pltpu.VMEM((AHEAD * chunk, modes), jnp.float32)),
+        out_shape=[block] * chips + [pltpu.VMEM((AHEAD * chunk, modes), jnp.float32)],
         in_specs=[anywhere] * 5,
-        out_specs=(vmem,) * 3,
+        out_specs=[vmem] * (chips + 1),
         scratch_shapes=[pltpu.VMEM((rows, columns), jnp.bfloat16)]
         + [pltpu.VMEM((1, rows), jnp.int32)] * 3
         + [pltpu.SemaphoreType.DMA((5,))],
@@ -238,21 +266,20 @@
             for value in (visibility[0], *facts, planes)
         ]
     )
-    got = swap(theirs, "pair", 1)
-    pieces = [jnp.concatenate([mine[k], got[k]], axis=0) for k in range(chips)]
     order = [k for k in range(1, chips) if k & (chips // 2)] + [
         k for k in range(1, chips) if not k & (chips // 2)
     ]
     moved = {k: swap(pieces[k], "pair", 2 * k) for k in order}
-    held = pl.pallas_call(
+    *held, loaded = pl.pallas_call(
         functools.partial(load_kernel, peers, chunk),
         out_shape=tuple(
             pltpu.VMEM((planes.shape[0], len(owners) * width), dtype)
             for owners in groups(peers)
             for dtype in (jnp.bfloat16, SMALL, SMALL)
-        ),
+        )
+        + (jax.ShapeDtypeStruct((8, 128), jnp.float32),),
         in_specs=[anywhere, vmem, anywhere],
-        out_specs=(vmem,) * 9,
+        out_specs=(vmem,) * 10,
         scratch_shapes=[
             pltpu.VMEM((4, chunk, modes), jnp.float32),
             pltpu.SemaphoreType.DMA((4,)),
@@ -264,6 +291,7 @@
         name="load",
     )(planes, pltpu.with_memory_space_constraint(start, pltpu.VMEM), pieces[0])
     held = [pltpu.with_memory_space_constraint(part, pltpu.VMEM) for part in held]
+
     def products(count):
         return jax.ShapeDtypeStruct((count, columns, width), jnp.float32)
 
@@ -271,20 +299,39 @@
         flops = 6 * mwin * 2 * (columns // mwin) * base_dev * count * width
         return pl.CostEstimate(flops=flops, bytes_accessed=0, transcendentals=0)
 
+    received = [pieces[0]] + [moved[k] for k in order]
+    passed = pl.pallas_call(
+        functools.partial(pass_kernel, capacity),
+        out_shape=jax.ShapeDtypeStruct((chips * size, columns), jnp.bfloat16),
+        in_specs=[vmem] * chips + [anywhere],
+        out_specs=vmem,
+        compiler_params=pltpu.CompilerParams(vmem_limit_bytes=8 * MIB),
+        name="pass",
+    )(*received, loaded)
+    got = swap(passed, "pair", 1)
+    direct = pl.pallas_call(
+        functools.partial(direct_kernel, capacity),
+        out_shape=pltpu.VMEM((columns + 16, base_dev), jnp.float32),
+        in_specs=[vmem] * chips + [anywhere],
+        out_specs=vmem,
+        compiler_params=pltpu.CompilerParams(vmem_limit_bytes=12 * MIB),
+        cost_estimate=cost(1),
+        name="direct",
+    )(*received, loaded)
     left, small, near_send, far_send = pl.pallas_call(
-        functools.partial(stack_kernel, peers, capacity, mwin),
+        functools.partial(stack_kernel, capacity, mwin),
         out_shape=(
             pltpu.VMEM((mwin, columns // mwin, 2 * base_dev), jnp.bfloat16),
             pltpu.VMEM((mwin, 2, columns // mwin, 2 * base_dev), SMALL),
             products(chips // 2),
             products(chips // 2),
         ),
-        in_specs=[vmem] * (chips + 3),
+        in_specs=[vmem] * 5,
         out_specs=(vmem,) * 4,
         compiler_params=pltpu.CompilerParams(vmem_limit_bytes=12 * MIB),
         cost_estimate=cost(chips),
         name="stack",
-    )(pieces[0], *[moved[k] for k in order], *held[:3])
+    )(got, pltpu.with_memory_space_constraint(direct, pltpu.VMEM), *held[:3])
     far_got, near_got = swap(far_send, "pair", 1), swap(near_send, "pair", 1)
     left, small = [pltpu.with_memory_space_constraint(part, pltpu.VMEM) for part in (left, small)]
     summed, after = {}, []

time: 46.8 us -> 45.9 us (0.981)
  waiting for transfers between devices: 8.35 us -> 7.12 us
  Pallas kernels: 21.2 us -> 22.1 us
    ppermute x12, waiting for transfers between devices: 8.35 us -> 7.12 us  [swap(): return lax.ppermute(value, axis, [(i, i ^ distance) for i in range(size)])]
    pallas_call x1 -> x3, Pallas kernels: 5.59 us -> 6.62 us  [the longest x1 4.83 us: staged(): pl.pallas_call(functools.partial(stack_kernel, capacity, mwin), out_shape...]
  transfers between devices with their start and end apart: 12 -> 12, of which waited for: 7 -> 6; matrix products, arithmetic and copies ran while one was open for 2% -> 2% of each run, Pallas kernels for 28% -> 32%
where the time goes in v5:
time: 45.9 us; the launch traced here: 45.8 us
  Pallas kernels  22.1 us (48%)
  starting transfers between devices  14.5 us (32%)
  waiting for transfers between devices  7.12 us (16%)
  other arithmetic  1.34 us (3%)
  between operations  0.77 us (2%)
    ppermute x12, starting transfers between devices, swap(): return lax.ppermute(value, axis, [(i, i ^ distance) for i in range(size)])  14.5 us
    pallas_call x1, Pallas kernels, staged(): pl.pallas_call(functools.partial(load_kernel, peers, chunk), out_shape=tu...  10.3 us
    ppermute x12, waiting for transfers between devices, swap(): return lax.ppermute(value, axis, [(i, i ^ distance) for i in range(size)])  7.12 us
    pallas_call x1, Pallas kernels, staged(): pl.pallas_call(functools.partial(stack_kernel, capacity, mwin), out_shape...  4.83 us
    pallas_call x2, Pallas kernels, staged(): pl.pallas_call(keep_kernel, out_shape=products(len(owners)), in_specs=[vm...  2.8 us
    pallas_call x1, Pallas kernels, staged(): pl.pallas_call(functools.partial(pack_kernel, peers, capacity), out_shape...  2.37 us
    pallas_call x1, Pallas kernels, staged(): pl.pallas_call(functools.partial(direct_kernel, capacity), out_shape=pltp...  1.78 us
  transfers between devices with their start and end apart: 12, of which 6 were waited for; matrix products, arithmetic and copies ran while one was open for 2% of the time, Pallas kernels for 32%

profile of v5, /device:TPU:0, one launch (start us, length us, event | category | flops | bytes accessed | tf_op | source)
XLA Modules:
  0.0 45.8 jit_solution(17902286558021041087)
XLA Ops:
  0.6 2.4 %pack.1 = (bf16[272,256]{1,0:T(8,128)(2,1)S(1)}, bf16[272,256]{1,0:T(8,128)(2,1)S(1)}, bf16[272,256]{1,0:T(8,128)(2,1)S(1)}, bf16[272,256]{1,0:T(8,128)(2,1)S(1)}, f32[1024,1024]{1,0:T(8,128)S(1)}) custom-call(bf16[512,256]{1,0:T(8,128)(2,1)} %bitcast.28, s32[1,512]{1,0:T(1,128)} %bitcast.30, s32[1,512]{1,0:T(1,128)} %bitcast.31, s32[1,512]{1,0:T(1,128)} %bitcast.32, ...), custom_call_target="tpu_custom_call" | custom-call | tf_op jit(solution)/shard_map/pack/pallas_call | solution.py:253
  3.0 4.1 %collective-permute-start = (bf16[272,256]{1,0:T(8,128)(2,1)S(1)}, bf16[272,256]{1,0:T(8,128)(2,1)S(1)}, u32[]{:S(2)}, u32[]{:S(2)}) collective-permute-start(bf16[272,256]{1,0:T(8,128)(2,1)S(1)} %get-tuple-element.24), channel_id=1, source_target_pairs={{0,4},{1,5},{2,6},{3,7},{4,0},{5,1},{6,2},{7,3},{8,12},{9,13},{10,... | collective-permute-start | bytes 417800 | tf_op jit(solution)/shard_map/ppermute | solution.py:27
  7.1 1.3 %collective-permute-start.1 = (bf16[272,256]{1,0:T(8,128)(2,1)S(1)}, bf16[272,256]{1,0:T(8,128)(2,1)S(1)}, u32[]{:S(2)}, u32[]{:S(2)}) collective-permute-start(bf16[272,256]{1,0:T(8,128)(2,1)S(1)} %get-tuple-element.25), channel_id=1, source_target_pairs={{0,6},{1,7},{2,4},{3,5},{4,2},{5,3},{6,0},{7,1},{8,14},{9,15},{10,... | collective-permute-start | bytes 417800 | tf_op jit(solution)/shard_map/ppermute | solution.py:27
  8.5 0.2 collective-permute-start.2
  8.7 10.3 %load.1 = (bf16[8192,512]{1,0:T(8,128)(2,1)S(1)}, f8e5m2[8192,512]{1,0:T(32,128)(4,1)S(1)}, f8e5m2[8192,512]{1,0:T(32,128)(4,1)S(1)}, bf16[8192,256]{1,0:T(8,128...) custom-call(f32[8192,1024]{1,0:T(8,128)} %bitcast.27, ...), custom_call_target="tpu_custom_call" | custom-call | bytes 67108864 | tf_op jit(solution)/shard_map/load/pallas_call | solution.py:273
  19.0 0.0 collective-permute-done.refs_1_
  19.0 0.0 collective-permute-done.1.refs_2_
  19.0 0.0 collective-permute-done.2.refs_3_
  19.0 0.1 collective-permute-start.3
  19.1 1.8 %direct.1.direct_ref = f32[272,2048]{1,0:T(8,128)S(1)} custom-call(bf16[272,256]{1,0:T(8,128)(2,1)S(1)} %get-tuple-element.23.after_ref.refs_0_, bf16[272,256]{1,0:T(8,128)(2,1)S(1)} %collective-permute-done.refs_1_, bf16[272,256]{1,0:T(8,128)(2,1)S(1)} %collective-permute-done.1.refs_2_, bf16[272,256]{1,0:T(8,128)(2,1)S(1)} %collective-permute-done.2.refs_3_, ...), custom_call_target="tpu_custom_call" | custom-call | flops 805306368 | tf_op jit(solution)/shard_map/direct/pallas_call | solution.py:312
  20.9 0.0 collective-permute-done.3.blocks_ref
  20.9 4.8 %stack.1 = (bf16[2,128,4096]{2,1,0:T(8,128)(2,1)S(1)}, f8e5m2[2,2,128,4096]{3,2,1,0:T(32,128)(4,1)S(1)}, f32[2,256,128]{2,1,0:T(8,128)S(1)}, f32[2,256,128]{2,1,0:T(8,128)S(1)}) custom-call(bf16[544,256]{1,0:T(8,128)(2,1)S(1)} %collective-permute-done.3.blocks_ref, f32[272,2048]{1,0:T(8,128)S(1)} %direct.1.direct_ref, ...), custom_call_target="tpu_custom_call" | custom-call | flops 3221225472 | tf_op jit(solution)/shard_map/stack/pallas_call | solution.py:321
  25.7 0.6 %collective-permute-start.4 = (f32[2,256,128]{2,1,0:T(8,128)S(1)}, f32[2,256,128]{2,1,0:T(8,128)S(1)}, u32[]{:S(2)}, u32[]{:S(2)}) collective-permute-start(f32[2,256,128]{2,1,0:T(8,128)S(1)} %get-tuple-element.40), channel_id=1, source_target_pairs={{0,1},{1,0},{2,3},{3,2},{4,5},{5,4},{6,7},{7,6},{8,9},{9,8},{10,11... | collective-permute-start | bytes 786440 | tf_op jit(solution)/shard_map/ppermute | solution.py:27
  26.3 0.1 collective-permute-start.5
  26.4 1.4 %far.1 = f32[2,256,128]{2,1,0:T(8,128)S(1)} custom-call(bf16[2,128,4096]{2,1,0:T(8,128)(2,1)S(1)} %get-tuple-element.32.refs_0_, f8e5m2[2,2,128,4096]{3,2,1,0:T(32,128)(4,1)S(1)} %get-tuple-element.33.refs_1_, bf16[8192,256]{1,0:T(8,128)(2,1)S(1)} %get-tuple-element.37.refs_2_, f8e5m2[8192,256]{1,0:T(32,128)(4,1)S(1)} %get-tuple-element.38.refs_3_, ...), custom_call_target="tpu_custom_call" | custom-call | flops 1610612736 | tf_op jit(solution)/shard_map/far/pallas_call | solution.py:341
  27.8 0.0 collective-permute-done.4
  27.8 3.0 %collective-permute-start.7 = (bf16[256,128]{1,0:T(8,128)(2,1)S(1)}, bf16[256,128]{1,0:T(8,128)(2,1)S(1)}, u32[]{:S(2)}, u32[]{:S(2)}) collective-permute-start(bf16[256,128]{1,0:T(8,128)(2,1)S(1)} %get-tuple-element.44.refs_6_), channel_id=1, source_target_pairs={{0,6},{1,7},{2,4},{3,5},{4,2},{5,3},{6,0},{7,1},{8,14},{9,15},{10,... | collective-permute-start | bytes 196616 | tf_op jit(solution)/shard_map/ppermute | solution.py:27
  30.8 0.6 %collective-permute-start.6 = (bf16[256,128]{1,0:T(8,128)(2,1)S(1)}, bf16[256,128]{1,0:T(8,128)(2,1)S(1)}, u32[]{:S(2)}, u32[]{:S(2)}) collective-permute-start(bf16[256,128]{1,0:T(8,128)(2,1)S(1)} %get-tuple-element.45.refs_5_), channel_id=1, source_target_pairs={{0,4},{1,5},{2,6},{3,7},{4,0},{5,1},{6,2},{7,3},{8,12},{9,13},{10,... | collective-permute-start | bytes 196616 | tf_op jit(solution)/shard_map/ppermute | solution.py:27
  31.4 1.4 %near.1 = f32[2,256,128]{2,1,0:T(8,128)S(1)} custom-call(bf16[2,128,4096]{2,1,0:T(8,128)(2,1)S(1)} %get-tuple-element.32.refs_0_, f8e5m2[2,2,128,4096]{3,2,1,0:T(32,128)(4,1)S(1)} %get-tuple-element.33.refs_1_, bf16[8192,256]{1,0:T(8,128)(2,1)S(1)} %get-tuple-element.34.refs_2_, f8e5m2[8192,256]{1,0:T(32,128)(4,1)S(1)} %get-tuple-element.35.refs_3_, ...), custom_call_target="tpu_custom_call" | custom-call | flops 1610612736 | tf_op jit(solution)/shard_map/near/pallas_call | solution.py:341
  32.8 0.0 collective-permute-done.5
  32.9 1.0 %collective-permute-start.8 = (bf16[256,128]{1,0:T(8,128)(2,1)S(1)}, bf16[256,128]{1,0:T(8,128)(2,1)S(1)}, u32[]{:S(2)}, u32[]{:S(2)}) collective-permute-start(bf16[256,128]{1,0:T(8,128)(2,1)S(1)} %fusion.8), channel_id=1, source_target_pairs={{0,2},{1,3},{2,0},{3,1},{4,6},{5,7},{6,4},{7,5},{8,10},{9,11},{10,... | collective-permute-start | bytes 196616 | tf_op jit(solution)/shard_map/ppermute | solution.py:27
  33.8 0.4 collective-permute-done.7
  34.3 4.1 %collective-permute-done.6 = bf16[256,128]{1,0:T(8,128)(2,1)S(1)} collective-permute-done((bf16[256,128]{1,0:T(8,128)(2,1)S(1)}, bf16[256,128]{1,0:T(8,128)(2,1)S(1)}, u32[]{:S(2)}, u32[]{:S(2)}) %collective-permute-start.6) | collective-permute-done | bytes 65568 | tf_op jit(solution)/shard_map/ppermute | solution.py:27
  38.4 0.2 collective-permute-done.8
  38.6 2.5 %collective-permute-start.11 = (f32[2,128]{1,0:T(2,128)S(1)}, f32[2,128]{1,0:T(2,128)S(1)}, u32[]{:S(2)}, u32[]{:S(2)}) collective-permute-start(f32[2,128]{1,0:T(2,128)S(1)} %bitcast_reduce_fusion), channel_id=1, source_target_pairs={{0,24},{8,16},{16,8},{24,0},{1,25},{9,17},{17,9},{25,1},{2,26},{10... | collective-permute-start | bytes 3080 | tf_op jit(solution)/shard_map/ppermute | solution.py:27
  41.1 0.5 %collective-permute-start.10 = (f32[2,128]{1,0:T(2,128)S(1)}, f32[2,128]{1,0:T(2,128)S(1)}, u32[]{:S(2)}, u32[]{:S(2)}) collective-permute-start(f32[2,128]{1,0:T(2,128)S(1)} %bitcast_reduce_fusion), channel_id=1, source_target_pairs={{0,16},{8,24},{16,0},{24,8},{1,17},{9,25},{17,1},{25,9},{2,18},{10... | collective-permute-start | bytes 3080 | tf_op jit(solution)/shard_map/ppermute | solution.py:27
  41.6 0.5 %collective-permute-start.9 = (f32[2,128]{1,0:T(2,128)S(1)}, f32[2,128]{1,0:T(2,128)S(1)}, u32[]{:S(2)}, u32[]{:S(2)}) collective-permute-start(f32[2,128]{1,0:T(2,128)S(1)} %bitcast_reduce_fusion), channel_id=1, source_target_pairs={{0,8},{8,0},{16,24},{24,16},{1,9},{9,1},{17,25},{25,17},{2,10},{10... | collective-permute-start | bytes 3080 | tf_op jit(solution)/shard_map/ppermute | solution.py:27
  42.2 0.7 %convert_add_fusion = f32[256,128]{1,0:T(8,128)} fusion(f32[256,128]{1,0:T(8,128)S(1)} %fusion.3, bf16[256,128]{1,0:T(8,128)(2,1)S(1)} %collective-permute-done.8), kind=kLoop, calls=%fused_computation.12 | loop fusion | flops 65536 | bytes 327680 | tf_op jit(solution)/shard_map/add | solution.py:365
  42.8 0.3 collective-permute-done.11
  43.2 1.5 %collective-permute-done.10 = f32[2,128]{1,0:T(2,128)S(1)} collective-permute-done((f32[2,128]{1,0:T(2,128)S(1)}, f32[2,128]{1,0:T(2,128)S(1)}, u32[]{:S(2)}, u32[]{:S(2)}) %collective-permute-start.10) | collective-permute-done | bytes 1056 | tf_op jit(solution)/shard_map/ppermute | solution.py:27
  44.7 0.5 %collective-permute-done.9 = f32[2,128]{1,0:T(2,128)S(1)} collective-permute-done((f32[2,128]{1,0:T(2,128)S(1)}, f32[2,128]{1,0:T(2,128)S(1)}, u32[]{:S(2)}, u32[]{:S(2)}) %collective-permute-start.9) | collective-permute-done | bytes 1056 | tf_op jit(solution)/shard_map/ppermute | solution.py:27
  45.2 0.6 %multiply_bitcast_fusion = f32[128,2]{0,1:T(2,128)} fusion(f32[2,128]{1,0:T(2,128)S(1)} %collective-permute-done.10, f32[2,128]{1,0:T(2,128)S(1)} %collective-permute-done.11, f32[2,128]{1,0:T(2,128)S(1)} %bitcast_reduce_fusion, f32[2,128]{1,0:T(2,128)S(1)} %collective-permute-done.9), kind=kLoop, calls=%fused_computation.16 | loop fusion | flops 1024 | bytes 5120 | tf_op jit(solution)/shard_map/transpose | solution.py:374
  (5 shorter events, 0.1 us)
Async XLA Ops:
  3.0 16.0 %collective-permute-start = (bf16[272,256]{1,0:T(8,128)(2,1)S(1)}, bf16[272,256]{1,0:T(8,128)(2,1)S(1)}, u32[]{:S(2)}, u32[]{:S(2)}) collective-permute-start(bf16[272,256]{1,0:T(8,128)(2,1)S(1)} %get-tuple-element.24), channel_id=1, source_target_pairs={{0,4},{1,5},{2,6},{3,7},{4,0},{5,1},{6,2},{7,3},{8,12},{9,13},{10,... | collective-permute-start | bytes 417800 | tf_op jit(solution)/shard_map/ppermute | solution.py:27
  7.1 11.9 %collective-permute-start.1 = (bf16[272,256]{1,0:T(8,128)(2,1)S(1)}, bf16[272,256]{1,0:T(8,128)(2,1)S(1)}, u32[]{:S(2)}, u32[]{:S(2)}) collective-permute-start(bf16[272,256]{1,0:T(8,128)(2,1)S(1)} %get-tuple-element.25), channel_id=1, source_target_pairs={{0,6},{1,7},{2,4},{3,5},{4,2},{5,3},{6,0},{7,1},{8,14},{9,15},{10,... | collective-permute-start | bytes 417800 | tf_op jit(solution)/shard_map/ppermute | solution.py:27
  8.5 10.5 %collective-permute-start.2 = (bf16[272,256]{1,0:T(8,128)(2,1)S(1)}, bf16[272,256]{1,0:T(8,128)(2,1)S(1)}, u32[]{:S(2)}, u32[]{:S(2)}) collective-permute-start(bf16[272,256]{1,0:T(8,128)(2,1)S(1)} %get-tuple-element.26), channel_id=1, source_target_pairs={{0,2},{1,3},{2,0},{3,1},{4,6},{5,7},{6,4},{7,5},{8,10},{9,11},{10,... | collective-permute-start | bytes 417800 | tf_op jit(solution)/shard_map/ppermute | solution.py:27
  19.0 1.9 %collective-permute-start.3 = (bf16[544,256]{1,0:T(8,128)(2,1)S(1)}, bf16[544,256]{1,0:T(8,128)(2,1)S(1)}, u32[]{:S(2)}, u32[]{:S(2)}) collective-permute-start(bf16[544,256]{1,0:T(8,128)(2,1)S(1)} %pass.1), channel_id=1, source_target_pairs={{0,1},{1,0},{2,3},{3,2},{4,5},{5,4},{6,7},{7,6},{8,9},{9,8},{10,11... | collective-permute-start | bytes 835592 | tf_op jit(solution)/shard_map/ppermute | solution.py:27
  25.7 2.1 %collective-permute-start.4 = (f32[2,256,128]{2,1,0:T(8,128)S(1)}, f32[2,256,128]{2,1,0:T(8,128)S(1)}, u32[]{:S(2)}, u32[]{:S(2)}) collective-permute-start(f32[2,256,128]{2,1,0:T(8,128)S(1)} %get-tuple-element.40), channel_id=1, source_target_pairs={{0,1},{1,0},{2,3},{3,2},{4,5},{5,4},{6,7},{7,6},{8,9},{9,8},{10,11... | collective-permute-start | bytes 786440 | tf_op jit(solution)/shard_map/ppermute | solution.py:27
  26.3 6.5 %collective-permute-start.5 = (f32[2,256,128]{2,1,0:T(8,128)S(1)}, f32[2,256,128]{2,1,0:T(8,128)S(1)}, u32[]{:S(2)}, u32[]{:S(2)}) collective-permute-start(f32[2,256,128]{2,1,0:T(8,128)S(1)} %get-tuple-element.41), channel_id=1, source_target_pairs={{0,1},{1,0},{2,3},{3,2},{4,5},{5,4},{6,7},{7,6},{8,9},{9,8},{10,11... | collective-permute-start | bytes 786440 | tf_op jit(solution)/shard_map/ppermute | solution.py:27
  27.8 6.4 %collective-permute-start.7 = (bf16[256,128]{1,0:T(8,128)(2,1)S(1)}, bf16[256,128]{1,0:T(8,128)(2,1)S(1)}, u32[]{:S(2)}, u32[]{:S(2)}) collective-permute-start(bf16[256,128]{1,0:T(8,128)(2,1)S(1)} %get-tuple-element.44.refs_6_), channel_id=1, source_target_pairs={{0,6},{1,7},{2,4},{3,5},{4,2},{5,3},{6,0},{7,1},{8,14},{9,15},{10,... | collective-permute-start | bytes 196616 | tf_op jit(solution)/shard_map/ppermute | solution.py:27
  30.8 7.5 %collective-permute-start.6 = (bf16[256,128]{1,0:T(8,128)(2,1)S(1)}, bf16[256,128]{1,0:T(8,128)(2,1)S(1)}, u32[]{:S(2)}, u32[]{:S(2)}) collective-permute-start(bf16[256,128]{1,0:T(8,128)(2,1)S(1)} %get-tuple-element.45.refs_5_), channel_id=1, source_target_pairs={{0,4},{1,5},{2,6},{3,7},{4,0},{5,1},{6,2},{7,3},{8,12},{9,13},{10,... | collective-permute-start | bytes 196616 | tf_op jit(solution)/shard_map/ppermute | solution.py:27
  32.9 5.7 %collective-permute-start.8 = (bf16[256,128]{1,0:T(8,128)(2,1)S(1)}, bf16[256,128]{1,0:T(8,128)(2,1)S(1)}, u32[]{:S(2)}, u32[]{:S(2)}) collective-permute-start(bf16[256,128]{1,0:T(8,128)(2,1)S(1)} %fusion.8), channel_id=1, source_target_pairs={{0,2},{1,3},{2,0},{3,1},{4,6},{5,7},{6,4},{7,5},{8,10},{9,11},{10,... | collective-permute-start | bytes 196616 | tf_op jit(solution)/shard_map/ppermute | solution.py:27
  38.6 4.5 %collective-permute-start.11 = (f32[2,128]{1,0:T(2,128)S(1)}, f32[2,128]{1,0:T(2,128)S(1)}, u32[]{:S(2)}, u32[]{:S(2)}) collective-permute-start(f32[2,128]{1,0:T(2,128)S(1)} %bitcast_reduce_fusion), channel_id=1, source_target_pairs={{0,24},{8,16},{16,8},{24,0},{1,25},{9,17},{17,9},{25,1},{2,26},{10... | collective-permute-start | bytes 3080 | tf_op jit(solution)/shard_map/ppermute | solution.py:27
  41.1 3.6 %collective-permute-start.10 = (f32[2,128]{1,0:T(2,128)S(1)}, f32[2,128]{1,0:T(2,128)S(1)}, u32[]{:S(2)}, u32[]{:S(2)}) collective-permute-start(f32[2,128]{1,0:T(2,128)S(1)} %bitcast_reduce_fusion), channel_id=1, source_target_pairs={{0,16},{8,24},{16,0},{24,8},{1,17},{9,25},{17,1},{25,9},{2,18},{10... | collective-permute-start | bytes 3080 | tf_op jit(solution)/shard_map/ppermute | solution.py:27
  41.6 3.6 %collective-permute-start.9 = (f32[2,128]{1,0:T(2,128)S(1)}, f32[2,128]{1,0:T(2,128)S(1)}, u32[]{:S(2)}, u32[]{:S(2)}) collective-permute-start(f32[2,128]{1,0:T(2,128)S(1)} %bitcast_reduce_fusion), channel_id=1, source_target_pairs={{0,8},{8,0},{16,24},{24,16},{1,9},{9,1},{17,25},{25,17},{2,10},{10... | collective-permute-start | bytes 3080 | tf_op jit(solution)/shard_map/ppermute | solution.py:27

commit v6 on v5

--- a/solution.py
+++ b/solution.py
@@ -9,7 +9,7 @@
 
 MIB = 1 << 20
 SMALL = jnp.float8_e5m2
-AHEAD = 2
+AHEAD = 4
 BEAM, BEAM_REST, STACK, STACK_REST = 2.0**18, 2.0**27, 2.0**12, 2.0**21
 
 
@@ -248,7 +248,7 @@
     anywhere = pl.BlockSpec(memory_space=pl.ANY)
     block = jax.ShapeDtypeStruct((2 * size, columns), jnp.bfloat16)
     facts = [value.reshape(1, rows) for value in (pair_counts, owner_ids, slot_ids)]
-    chunk = 512
+    chunk = 128
     planes = beam.reshape(mwin * 2 * base_dev, modes)
     *pieces, start = pl.pallas_call(
         functools.partial(pack_kernel, peers, capacity),
@@ -281,8 +281,8 @@
         in_specs=[anywhere, vmem, anywhere],
         out_specs=(vmem,) * 10,
         scratch_shapes=[
-            pltpu.VMEM((4, chunk, modes), jnp.float32),
-            pltpu.SemaphoreType.DMA((4,)),
+            pltpu.VMEM((16, chunk, modes), jnp.float32),
+            pltpu.SemaphoreType.DMA((16,)),
         ],
         compiler_params=pltpu.CompilerParams(vmem_limit_bytes=12 * MIB),
         cost_estimate=pl.CostEstimate(

time: 45.9 us -> 45.4 us (0.989)
  transfers between devices with their start and end apart: 12 -> 12, of which waited for: 6 -> 6; matrix products, arithmetic and copies ran while one was open for 2% -> 2% of each run, Pallas kernels for 32% -> 33%
where the time goes in v6:
time: 45.4 us; the launch traced here: 45.3 us
  Pallas kernels  21.7 us (48%)
  starting transfers between devices  14.5 us (32%)
  waiting for transfers between devices  6.99 us (15%)
  other arithmetic  1.34 us (3%)
  between operations  0.77 us (2%)
    ppermute x12, starting transfers between devices, swap(): return lax.ppermute(value, axis, [(i, i ^ distance) for i in range(size)])  14.5 us
    pallas_call x1, Pallas kernels, staged(): pl.pallas_call(functools.partial(load_kernel, peers, chunk), out_shape=tu...  10.4 us
    ppermute x12, waiting for transfers between devices, swap(): return lax.ppermute(value, axis, [(i, i ^ distance) for i in range(size)])  6.99 us
    pallas_call x1, Pallas kernels, staged(): pl.pallas_call(functools.partial(stack_kernel, capacity, mwin), out_shape...  4.8 us
    pallas_call x2, Pallas kernels, staged(): pl.pallas_call(keep_kernel, out_shape=products(len(owners)), in_specs=[vm...  2.8 us
    pallas_call x1, Pallas kernels, staged(): pl.pallas_call(functools.partial(pack_kernel, peers, capacity), out_shape...  1.94 us
    pallas_call x1, Pallas kernels, staged(): pl.pallas_call(functools.partial(direct_kernel, capacity), out_shape=pltp...  1.78 us
  transfers between devices with their start and end apart: 12, of which 6 were waited for; matrix products, arithmetic and copies ran while one was open for 2% of the time, Pallas kernels for 33%

profile of v6, /device:TPU:0, one launch (start us, length us, event | category | flops | bytes accessed | tf_op | source)
XLA Modules:
  0.0 45.3 jit_solution(2943268307837919702)
XLA Ops:
  0.6 1.9 %pack.1 = (bf16[272,256]{1,0:T(8,128)(2,1)S(1)}, bf16[272,256]{1,0:T(8,128)(2,1)S(1)}, bf16[272,256]{1,0:T(8,128)(2,1)S(1)}, bf16[272,256]{1,0:T(8,128)(2,1)S(1)}, f32[512,1024]{1,0:T(8,128)S(1)}) custom-call(bf16[512,256]{1,0:T(8,128)(2,1)} %bitcast.28, s32[1,512]{1,0:T(1,128)} %bitcast.30, s32[1,512]{1,0:T(1,128)} %bitcast.31, s32[1,512]{1,0:T(1,128)} %bitcast.32, ...), custom_call_target="tpu_custom_call" | custom-call | tf_op jit(solution)/shard_map/pack/pallas_call | solution.py:253
  2.6 4.1 %collective-permute-start = (bf16[272,256]{1,0:T(8,128)(2,1)S(1)}, bf16[272,256]{1,0:T(8,128)(2,1)S(1)}, u32[]{:S(2)}, u32[]{:S(2)}) collective-permute-start(bf16[272,256]{1,0:T(8,128)(2,1)S(1)} %get-tuple-element.24), channel_id=1, source_target_pairs={{0,4},{1,5},{2,6},{3,7},{4,0},{5,1},{6,2},{7,3},{8,12},{9,13},{10,... | collective-permute-start | bytes 417800 | tf_op jit(solution)/shard_map/ppermute | solution.py:27
  6.7 1.3 %collective-permute-start.1 = (bf16[272,256]{1,0:T(8,128)(2,1)S(1)}, bf16[272,256]{1,0:T(8,128)(2,1)S(1)}, u32[]{:S(2)}, u32[]{:S(2)}) collective-permute-start(bf16[272,256]{1,0:T(8,128)(2,1)S(1)} %get-tuple-element.25), channel_id=1, source_target_pairs={{0,6},{1,7},{2,4},{3,5},{4,2},{5,3},{6,0},{7,1},{8,14},{9,15},{10,... | collective-permute-start | bytes 417800 | tf_op jit(solution)/shard_map/ppermute | solution.py:27
  8.0 0.2 collective-permute-start.2
  8.3 10.4 %load.1 = (bf16[8192,512]{1,0:T(8,128)(2,1)S(1)}, f8e5m2[8192,512]{1,0:T(32,128)(4,1)S(1)}, f8e5m2[8192,512]{1,0:T(32,128)(4,1)S(1)}, bf16[8192,256]{1,0:T(8,128...) custom-call(f32[8192,1024]{1,0:T(8,128)} %bitcast.27, ...), custom_call_target="tpu_custom_call" | custom-call | bytes 67108864 | tf_op jit(solution)/shard_map/load/pallas_call | solution.py:273
  18.7 0.0 collective-permute-done.refs_1_
  18.7 0.0 collective-permute-done.1.refs_2_
  18.7 0.0 collective-permute-done.2.refs_3_
  18.7 0.1 collective-permute-start.3
  18.8 1.8 %direct.1.direct_ref = f32[272,2048]{1,0:T(8,128)S(1)} custom-call(bf16[272,256]{1,0:T(8,128)(2,1)S(1)} %get-tuple-element.23.after_ref.refs_0_, bf16[272,256]{1,0:T(8,128)(2,1)S(1)} %collective-permute-done.refs_1_, bf16[272,256]{1,0:T(8,128)(2,1)S(1)} %collective-permute-done.1.refs_2_, bf16[272,256]{1,0:T(8,128)(2,1)S(1)} %collective-permute-done.2.refs_3_, ...), custom_call_target="tpu_custom_call" | custom-call | flops 805306368 | tf_op jit(solution)/shard_map/direct/pallas_call | solution.py:312
  20.6 0.0 collective-permute-done.3.blocks_ref
  20.6 4.8 %stack.1 = (bf16[2,128,4096]{2,1,0:T(8,128)(2,1)S(1)}, f8e5m2[2,2,128,4096]{3,2,1,0:T(32,128)(4,1)S(1)}, f32[2,256,128]{2,1,0:T(8,128)S(1)}, f32[2,256,128]{2,1,0:T(8,128)S(1)}) custom-call(bf16[544,256]{1,0:T(8,128)(2,1)S(1)} %collective-permute-done.3.blocks_ref, f32[272,2048]{1,0:T(8,128)S(1)} %direct.1.direct_ref, ...), custom_call_target="tpu_custom_call" | custom-call | flops 3221225472 | tf_op jit(solution)/shard_map/stack/pallas_call | solution.py:321
  25.4 0.6 %collective-permute-start.4 = (f32[2,256,128]{2,1,0:T(8,128)S(1)}, f32[2,256,128]{2,1,0:T(8,128)S(1)}, u32[]{:S(2)}, u32[]{:S(2)}) collective-permute-start(f32[2,256,128]{2,1,0:T(8,128)S(1)} %get-tuple-element.40), channel_id=1, source_target_pairs={{0,1},{1,0},{2,3},{3,2},{4,5},{5,4},{6,7},{7,6},{8,9},{9,8},{10,11... | collective-permute-start | bytes 786440 | tf_op jit(solution)/shard_map/ppermute | solution.py:27
  26.0 0.1 collective-permute-start.5
  26.1 1.4 %far.1 = f32[2,256,128]{2,1,0:T(8,128)S(1)} custom-call(bf16[2,128,4096]{2,1,0:T(8,128)(2,1)S(1)} %get-tuple-element.32.refs_0_, f8e5m2[2,2,128,4096]{3,2,1,0:T(32,128)(4,1)S(1)} %get-tuple-element.33.refs_1_, bf16[8192,256]{1,0:T(8,128)(2,1)S(1)} %get-tuple-element.37.refs_2_, f8e5m2[8192,256]{1,0:T(32,128)(4,1)S(1)} %get-tuple-element.38.refs_3_, ...), custom_call_target="tpu_custom_call" | custom-call | flops 1610612736 | tf_op jit(solution)/shard_map/far/pallas_call | solution.py:341
  27.5 0.0 collective-permute-done.4
  27.5 3.0 %collective-permute-start.7 = (bf16[256,128]{1,0:T(8,128)(2,1)S(1)}, bf16[256,128]{1,0:T(8,128)(2,1)S(1)}, u32[]{:S(2)}, u32[]{:S(2)}) collective-permute-start(bf16[256,128]{1,0:T(8,128)(2,1)S(1)} %get-tuple-element.44.refs_6_), channel_id=1, source_target_pairs={{0,6},{1,7},{2,4},{3,5},{4,2},{5,3},{6,0},{7,1},{8,14},{9,15},{10,... | collective-permute-start | bytes 196616 | tf_op jit(solution)/shard_map/ppermute | solution.py:27
  30.5 0.4 collective-permute-start.6
  30.9 1.4 %near.1 = f32[2,256,128]{2,1,0:T(8,128)S(1)} custom-call(bf16[2,128,4096]{2,1,0:T(8,128)(2,1)S(1)} %get-tuple-element.32.refs_0_, f8e5m2[2,2,128,4096]{3,2,1,0:T(32,128)(4,1)S(1)} %get-tuple-element.33.refs_1_, bf16[8192,256]{1,0:T(8,128)(2,1)S(1)} %get-tuple-element.34.refs_2_, f8e5m2[8192,256]{1,0:T(32,128)(4,1)S(1)} %get-tuple-element.35.refs_3_, ...), custom_call_target="tpu_custom_call" | custom-call | flops 1610612736 | tf_op jit(solution)/shard_map/near/pallas_call | solution.py:341
  32.3 0.0 collective-permute-done.5
  32.4 1.1 %collective-permute-start.8 = (bf16[256,128]{1,0:T(8,128)(2,1)S(1)}, bf16[256,128]{1,0:T(8,128)(2,1)S(1)}, u32[]{:S(2)}, u32[]{:S(2)}) collective-permute-start(bf16[256,128]{1,0:T(8,128)(2,1)S(1)} %fusion.8), channel_id=1, source_target_pairs={{0,2},{1,3},{2,0},{3,1},{4,6},{5,7},{6,4},{7,5},{8,10},{9,11},{10,... | collective-permute-start | bytes 196616 | tf_op jit(solution)/shard_map/ppermute | solution.py:27
  33.5 0.4 collective-permute-done.7
  33.9 3.9 %collective-permute-done.6 = bf16[256,128]{1,0:T(8,128)(2,1)S(1)} collective-permute-done((bf16[256,128]{1,0:T(8,128)(2,1)S(1)}, bf16[256,128]{1,0:T(8,128)(2,1)S(1)}, u32[]{:S(2)}, u32[]{:S(2)}) %collective-permute-start.6) | collective-permute-done | bytes 65568 | tf_op jit(solution)/shard_map/ppermute | solution.py:27
  37.9 0.2 collective-permute-done.8
  38.1 2.5 %collective-permute-start.11 = (f32[2,128]{1,0:T(2,128)S(1)}, f32[2,128]{1,0:T(2,128)S(1)}, u32[]{:S(2)}, u32[]{:S(2)}) collective-permute-start(f32[2,128]{1,0:T(2,128)S(1)} %bitcast_reduce_fusion), channel_id=1, source_target_pairs={{0,24},{8,16},{16,8},{24,0},{1,25},{9,17},{17,9},{25,1},{2,26},{10... | collective-permute-start | bytes 3080 | tf_op jit(solution)/shard_map/ppermute | solution.py:27
  40.7 0.5 %collective-permute-start.10 = (f32[2,128]{1,0:T(2,128)S(1)}, f32[2,128]{1,0:T(2,128)S(1)}, u32[]{:S(2)}, u32[]{:S(2)}) collective-permute-start(f32[2,128]{1,0:T(2,128)S(1)} %bitcast_reduce_fusion), channel_id=1, source_target_pairs={{0,16},{8,24},{16,0},{24,8},{1,17},{9,25},{17,1},{25,9},{2,18},{10... | collective-permute-start | bytes 3080 | tf_op jit(solution)/shard_map/ppermute | solution.py:27
  41.2 0.5 %collective-permute-start.9 = (f32[2,128]{1,0:T(2,128)S(1)}, f32[2,128]{1,0:T(2,128)S(1)}, u32[]{:S(2)}, u32[]{:S(2)}) collective-permute-start(f32[2,128]{1,0:T(2,128)S(1)} %bitcast_reduce_fusion), channel_id=1, source_target_pairs={{0,8},{8,0},{16,24},{24,16},{1,9},{9,1},{17,25},{25,17},{2,10},{10... | collective-permute-start | bytes 3080 | tf_op jit(solution)/shard_map/ppermute | solution.py:27
  41.7 0.7 %convert_add_fusion = f32[256,128]{1,0:T(8,128)} fusion(f32[256,128]{1,0:T(8,128)S(1)} %fusion.3, bf16[256,128]{1,0:T(8,128)(2,1)S(1)} %collective-permute-done.8), kind=kLoop, calls=%fused_computation.12 | loop fusion | flops 65536 | bytes 327680 | tf_op jit(solution)/shard_map/add | solution.py:365
  42.4 0.3 collective-permute-done.11
  42.7 1.6 %collective-permute-done.10 = f32[2,128]{1,0:T(2,128)S(1)} collective-permute-done((f32[2,128]{1,0:T(2,128)S(1)}, f32[2,128]{1,0:T(2,128)S(1)}, u32[]{:S(2)}, u32[]{:S(2)}) %collective-permute-start.10) | collective-permute-done | bytes 1056 | tf_op jit(solution)/shard_map/ppermute | solution.py:27
  44.2 0.5 %collective-permute-done.9 = f32[2,128]{1,0:T(2,128)S(1)} collective-permute-done((f32[2,128]{1,0:T(2,128)S(1)}, f32[2,128]{1,0:T(2,128)S(1)}, u32[]{:S(2)}, u32[]{:S(2)}) %collective-permute-start.9) | collective-permute-done | bytes 1056 | tf_op jit(solution)/shard_map/ppermute | solution.py:27
  44.7 0.6 %multiply_bitcast_fusion = f32[128,2]{0,1:T(2,128)} fusion(f32[2,128]{1,0:T(2,128)S(1)} %collective-permute-done.10, f32[2,128]{1,0:T(2,128)S(1)} %collective-permute-done.11, f32[2,128]{1,0:T(2,128)S(1)} %bitcast_reduce_fusion, f32[2,128]{1,0:T(2,128)S(1)} %collective-permute-done.9), kind=kLoop, calls=%fused_computation.16 | loop fusion | flops 1024 | bytes 5120 | tf_op jit(solution)/shard_map/transpose | solution.py:374
  (5 shorter events, 0.1 us)
Async XLA Ops:
  2.6 16.1 %collective-permute-start = (bf16[272,256]{1,0:T(8,128)(2,1)S(1)}, bf16[272,256]{1,0:T(8,128)(2,1)S(1)}, u32[]{:S(2)}, u32[]{:S(2)}) collective-permute-start(bf16[272,256]{1,0:T(8,128)(2,1)S(1)} %get-tuple-element.24), channel_id=1, source_target_pairs={{0,4},{1,5},{2,6},{3,7},{4,0},{5,1},{6,2},{7,3},{8,12},{9,13},{10,... | collective-permute-start | bytes 417800 | tf_op jit(solution)/shard_map/ppermute | solution.py:27
  6.7 12.0 %collective-permute-start.1 = (bf16[272,256]{1,0:T(8,128)(2,1)S(1)}, bf16[272,256]{1,0:T(8,128)(2,1)S(1)}, u32[]{:S(2)}, u32[]{:S(2)}) collective-permute-start(bf16[272,256]{1,0:T(8,128)(2,1)S(1)} %get-tuple-element.25), channel_id=1, source_target_pairs={{0,6},{1,7},{2,4},{3,5},{4,2},{5,3},{6,0},{7,1},{8,14},{9,15},{10,... | collective-permute-start | bytes 417800 | tf_op jit(solution)/shard_map/ppermute | solution.py:27
  8.0 10.7 %collective-permute-start.2 = (bf16[272,256]{1,0:T(8,128)(2,1)S(1)}, bf16[272,256]{1,0:T(8,128)(2,1)S(1)}, u32[]{:S(2)}, u32[]{:S(2)}) collective-permute-start(bf16[272,256]{1,0:T(8,128)(2,1)S(1)} %get-tuple-element.26), channel_id=1, source_target_pairs={{0,2},{1,3},{2,0},{3,1},{4,6},{5,7},{6,4},{7,5},{8,10},{9,11},{10,... | collective-permute-start | bytes 417800 | tf_op jit(solution)/shard_map/ppermute | solution.py:27
  18.7 1.9 %collective-permute-start.3 = (bf16[544,256]{1,0:T(8,128)(2,1)S(1)}, bf16[544,256]{1,0:T(8,128)(2,1)S(1)}, u32[]{:S(2)}, u32[]{:S(2)}) collective-permute-start(bf16[544,256]{1,0:T(8,128)(2,1)S(1)} %pass.1), channel_id=1, source_target_pairs={{0,1},{1,0},{2,3},{3,2},{4,5},{5,4},{6,7},{7,6},{8,9},{9,8},{10,11... | collective-permute-start | bytes 835592 | tf_op jit(solution)/shard_map/ppermute | solution.py:27
  25.4 2.0 %collective-permute-start.4 = (f32[2,256,128]{2,1,0:T(8,128)S(1)}, f32[2,256,128]{2,1,0:T(8,128)S(1)}, u32[]{:S(2)}, u32[]{:S(2)}) collective-permute-start(f32[2,256,128]{2,1,0:T(8,128)S(1)} %get-tuple-element.40), channel_id=1, source_target_pairs={{0,1},{1,0},{2,3},{3,2},{4,5},{5,4},{6,7},{7,6},{8,9},{9,8},{10,11... | collective-permute-start | bytes 786440 | tf_op jit(solution)/shard_map/ppermute | solution.py:27
  26.0 6.4 %collective-permute-start.5 = (f32[2,256,128]{2,1,0:T(8,128)S(1)}, f32[2,256,128]{2,1,0:T(8,128)S(1)}, u32[]{:S(2)}, u32[]{:S(2)}) collective-permute-start(f32[2,256,128]{2,1,0:T(8,128)S(1)} %get-tuple-element.41), channel_id=1, source_target_pairs={{0,1},{1,0},{2,3},{3,2},{4,5},{5,4},{6,7},{7,6},{8,9},{9,8},{10,11... | collective-permute-start | bytes 786440 | tf_op jit(solution)/shard_map/ppermute | solution.py:27
  27.5 6.4 %collective-permute-start.7 = (bf16[256,128]{1,0:T(8,128)(2,1)S(1)}, bf16[256,128]{1,0:T(8,128)(2,1)S(1)}, u32[]{:S(2)}, u32[]{:S(2)}) collective-permute-start(bf16[256,128]{1,0:T(8,128)(2,1)S(1)} %get-tuple-element.44.refs_6_), channel_id=1, source_target_pairs={{0,6},{1,7},{2,4},{3,5},{4,2},{5,3},{6,0},{7,1},{8,14},{9,15},{10,... | collective-permute-start | bytes 196616 | tf_op jit(solution)/shard_map/ppermute | solution.py:27
  30.5 7.4 %collective-permute-start.6 = (bf16[256,128]{1,0:T(8,128)(2,1)S(1)}, bf16[256,128]{1,0:T(8,128)(2,1)S(1)}, u32[]{:S(2)}, u32[]{:S(2)}) collective-permute-start(bf16[256,128]{1,0:T(8,128)(2,1)S(1)} %get-tuple-element.45.refs_5_), channel_id=1, source_target_pairs={{0,4},{1,5},{2,6},{3,7},{4,0},{5,1},{6,2},{7,3},{8,12},{9,13},{10,... | collective-permute-start | bytes 196616 | tf_op jit(solution)/shard_map/ppermute | solution.py:27
  32.4 5.7 %collective-permute-start.8 = (bf16[256,128]{1,0:T(8,128)(2,1)S(1)}, bf16[256,128]{1,0:T(8,128)(2,1)S(1)}, u32[]{:S(2)}, u32[]{:S(2)}) collective-permute-start(bf16[256,128]{1,0:T(8,128)(2,1)S(1)} %fusion.8), channel_id=1, source_target_pairs={{0,2},{1,3},{2,0},{3,1},{4,6},{5,7},{6,4},{7,5},{8,10},{9,11},{10,... | collective-permute-start | bytes 196616 | tf_op jit(solution)/shard_map/ppermute | solution.py:27
  38.1 4.5 %collective-permute-start.11 = (f32[2,128]{1,0:T(2,128)S(1)}, f32[2,128]{1,0:T(2,128)S(1)}, u32[]{:S(2)}, u32[]{:S(2)}) collective-permute-start(f32[2,128]{1,0:T(2,128)S(1)} %bitcast_reduce_fusion), channel_id=1, source_target_pairs={{0,24},{8,16},{16,8},{24,0},{1,25},{9,17},{17,9},{25,1},{2,26},{10... | collective-permute-start | bytes 3080 | tf_op jit(solution)/shard_map/ppermute | solution.py:27
  40.7 3.6 %collective-permute-start.10 = (f32[2,128]{1,0:T(2,128)S(1)}, f32[2,128]{1,0:T(2,128)S(1)}, u32[]{:S(2)}, u32[]{:S(2)}) collective-permute-start(f32[2,128]{1,0:T(2,128)S(1)} %bitcast_reduce_fusion), channel_id=1, source_target_pairs={{0,16},{8,24},{16,0},{24,8},{1,17},{9,25},{17,1},{25,9},{2,18},{10... | collective-permute-start | bytes 3080 | tf_op jit(solution)/shard_map/ppermute | solution.py:27
  41.2 3.6 %collective-permute-start.9 = (f32[2,128]{1,0:T(2,128)S(1)}, f32[2,128]{1,0:T(2,128)S(1)}, u32[]{:S(2)}, u32[]{:S(2)}) collective-permute-start(f32[2,128]{1,0:T(2,128)S(1)} %bitcast_reduce_fusion), channel_id=1, source_target_pairs={{0,8},{8,0},{16,24},{24,16},{1,9},{9,1},{17,25},{25,17},{2,10},{10... | collective-permute-start | bytes 3080 | tf_op jit(solution)/shard_map/ppermute | solution.py:27

commit v7 on v6

--- a/solution.py
+++ b/solution.py
@@ -355,7 +355,7 @@
             if k & (chips // 2):
                 after.append(summed[k])
     amplitudes = summed[0]
-    for k in order:
+    for k in order[-2::-1] + order[-1:]:
         if not k & (chips // 2):
             amplitudes = lax.optimization_barrier(amplitudes)
         partial = amplitudes

time: 45.4 us -> 45.4 us (level)
  no operation moved by 1% of the time
where the time goes in v7:
time: 45.4 us; the launch traced here: 45.3 us
  Pallas kernels  21.7 us (48%)
  starting transfers between devices  14.5 us (32%)
  waiting for transfers between devices  6.99 us (15%)
  other arithmetic  1.34 us (3%)
  between operations  0.77 us (2%)
    ppermute x12, starting transfers between devices, swap(): return lax.ppermute(value, axis, [(i, i ^ distance) for i in range(size)])  14.5 us
    pallas_call x1, Pallas kernels, staged(): pl.pallas_call(functools.partial(load_kernel, peers, chunk), out_shape=tu...  10.4 us
    ppermute x12, waiting for transfers between devices, swap(): return lax.ppermute(value, axis, [(i, i ^ distance) for i in range(size)])  6.99 us
    pallas_call x1, Pallas kernels, staged(): pl.pallas_call(functools.partial(stack_kernel, capacity, mwin), out_shape...  4.8 us
    pallas_call x2, Pallas kernels, staged(): pl.pallas_call(keep_kernel, out_shape=products(len(owners)), in_specs=[vm...  2.8 us
    pallas_call x1, Pallas kernels, staged(): pl.pallas_call(functools.partial(pack_kernel, peers, capacity), out_shape...  1.94 us
    pallas_call x1, Pallas kernels, staged(): pl.pallas_call(functools.partial(direct_kernel, capacity), out_shape=pltp...  1.78 us
  transfers between devices with their start and end apart: 12, of which 6 were waited for; matrix products, arithmetic and copies ran while one was open for 2% of the time, Pallas kernels for 33%

profile of v7, /device:TPU:0, one launch (start us, length us, event | category | flops | bytes accessed | tf_op | source)
XLA Modules:
  0.0 45.3 jit_solution(17656338871379720330)
XLA Ops:
  0.6 1.9 %pack.1 = (bf16[272,256]{1,0:T(8,128)(2,1)S(1)}, bf16[272,256]{1,0:T(8,128)(2,1)S(1)}, bf16[272,256]{1,0:T(8,128)(2,1)S(1)}, bf16[272,256]{1,0:T(8,128)(2,1)S(1)}, f32[512,1024]{1,0:T(8,128)S(1)}) custom-call(bf16[512,256]{1,0:T(8,128)(2,1)} %bitcast.28, s32[1,512]{1,0:T(1,128)} %bitcast.30, s32[1,512]{1,0:T(1,128)} %bitcast.31, s32[1,512]{1,0:T(1,128)} %bitcast.32, ...), custom_call_target="tpu_custom_call" | custom-call | tf_op jit(solution)/shard_map/pack/pallas_call | solution.py:253
  2.6 4.1 %collective-permute-start = (bf16[272,256]{1,0:T(8,128)(2,1)S(1)}, bf16[272,256]{1,0:T(8,128)(2,1)S(1)}, u32[]{:S(2)}, u32[]{:S(2)}) collective-permute-start(bf16[272,256]{1,0:T(8,128)(2,1)S(1)} %get-tuple-element.24), channel_id=1, source_target_pairs={{0,4},{1,5},{2,6},{3,7},{4,0},{5,1},{6,2},{7,3},{8,12},{9,13},{10,... | collective-permute-start | bytes 417800 | tf_op jit(solution)/shard_map/ppermute | solution.py:27
  6.7 1.3 %collective-permute-start.1 = (bf16[272,256]{1,0:T(8,128)(2,1)S(1)}, bf16[272,256]{1,0:T(8,128)(2,1)S(1)}, u32[]{:S(2)}, u32[]{:S(2)}) collective-permute-start(bf16[272,256]{1,0:T(8,128)(2,1)S(1)} %get-tuple-element.25), channel_id=1, source_target_pairs={{0,6},{1,7},{2,4},{3,5},{4,2},{5,3},{6,0},{7,1},{8,14},{9,15},{10,... | collective-permute-start | bytes 417800 | tf_op jit(solution)/shard_map/ppermute | solution.py:27
  8.0 0.2 collective-permute-start.2
  8.3 10.4 %load.1 = (bf16[8192,512]{1,0:T(8,128)(2,1)S(1)}, f8e5m2[8192,512]{1,0:T(32,128)(4,1)S(1)}, f8e5m2[8192,512]{1,0:T(32,128)(4,1)S(1)}, bf16[8192,256]{1,0:T(8,128...) custom-call(f32[8192,1024]{1,0:T(8,128)} %bitcast.27, ...), custom_call_target="tpu_custom_call" | custom-call | bytes 67108864 | tf_op jit(solution)/shard_map/load/pallas_call | solution.py:273
  18.7 0.0 collective-permute-done.refs_1_
  18.7 0.0 collective-permute-done.1.refs_2_
  18.7 0.0 collective-permute-done.2.refs_3_
  18.7 0.1 collective-permute-start.3
  18.8 1.8 %direct.1.direct_ref = f32[272,2048]{1,0:T(8,128)S(1)} custom-call(bf16[272,256]{1,0:T(8,128)(2,1)S(1)} %get-tuple-element.23.after_ref.refs_0_, bf16[272,256]{1,0:T(8,128)(2,1)S(1)} %collective-permute-done.refs_1_, bf16[272,256]{1,0:T(8,128)(2,1)S(1)} %collective-permute-done.1.refs_2_, bf16[272,256]{1,0:T(8,128)(2,1)S(1)} %collective-permute-done.2.refs_3_, ...), custom_call_target="tpu_custom_call" | custom-call | flops 805306368 | tf_op jit(solution)/shard_map/direct/pallas_call | solution.py:312
  20.6 0.0 collective-permute-done.3.blocks_ref
  20.6 4.8 %stack.1 = (bf16[2,128,4096]{2,1,0:T(8,128)(2,1)S(1)}, f8e5m2[2,2,128,4096]{3,2,1,0:T(32,128)(4,1)S(1)}, f32[2,256,128]{2,1,0:T(8,128)S(1)}, f32[2,256,128]{2,1,0:T(8,128)S(1)}) custom-call(bf16[544,256]{1,0:T(8,128)(2,1)S(1)} %collective-permute-done.3.blocks_ref, f32[272,2048]{1,0:T(8,128)S(1)} %direct.1.direct_ref, ...), custom_call_target="tpu_custom_call" | custom-call | flops 3221225472 | tf_op jit(solution)/shard_map/stack/pallas_call | solution.py:321
  25.4 0.6 %collective-permute-start.4 = (f32[2,256,128]{2,1,0:T(8,128)S(1)}, f32[2,256,128]{2,1,0:T(8,128)S(1)}, u32[]{:S(2)}, u32[]{:S(2)}) collective-permute-start(f32[2,256,128]{2,1,0:T(8,128)S(1)} %get-tuple-element.40), channel_id=1, source_target_pairs={{0,1},{1,0},{2,3},{3,2},{4,5},{5,4},{6,7},{7,6},{8,9},{9,8},{10,11... | collective-permute-start | bytes 786440 | tf_op jit(solution)/shard_map/ppermute | solution.py:27
  26.0 0.1 collective-permute-start.5
  26.1 1.4 %far.1 = f32[2,256,128]{2,1,0:T(8,128)S(1)} custom-call(bf16[2,128,4096]{2,1,0:T(8,128)(2,1)S(1)} %get-tuple-element.32.refs_0_, f8e5m2[2,2,128,4096]{3,2,1,0:T(32,128)(4,1)S(1)} %get-tuple-element.33.refs_1_, bf16[8192,256]{1,0:T(8,128)(2,1)S(1)} %get-tuple-element.37.refs_2_, f8e5m2[8192,256]{1,0:T(32,128)(4,1)S(1)} %get-tuple-element.38.refs_3_, ...), custom_call_target="tpu_custom_call" | custom-call | flops 1610612736 | tf_op jit(solution)/shard_map/far/pallas_call | solution.py:341
  27.5 0.0 collective-permute-done.4
  27.5 3.0 %collective-permute-start.6 = (bf16[256,128]{1,0:T(8,128)(2,1)S(1)}, bf16[256,128]{1,0:T(8,128)(2,1)S(1)}, u32[]{:S(2)}, u32[]{:S(2)}) collective-permute-start(bf16[256,128]{1,0:T(8,128)(2,1)S(1)} %get-tuple-element.44.refs_6_), channel_id=1, source_target_pairs={{0,6},{1,7},{2,4},{3,5},{4,2},{5,3},{6,0},{7,1},{8,14},{9,15},{10,... | collective-permute-start | bytes 196616 | tf_op jit(solution)/shard_map/ppermute | solution.py:27
  30.5 0.4 collective-permute-start.7
  30.9 1.4 %near.1 = f32[2,256,128]{2,1,0:T(8,128)S(1)} custom-call(bf16[2,128,4096]{2,1,0:T(8,128)(2,1)S(1)} %get-tuple-element.32.refs_0_, f8e5m2[2,2,128,4096]{3,2,1,0:T(32,128)(4,1)S(1)} %get-tuple-element.33.refs_1_, bf16[8192,256]{1,0:T(8,128)(2,1)S(1)} %get-tuple-element.34.refs_2_, f8e5m2[8192,256]{1,0:T(32,128)(4,1)S(1)} %get-tuple-element.35.refs_3_, ...), custom_call_target="tpu_custom_call" | custom-call | flops 1610612736 | tf_op jit(solution)/shard_map/near/pallas_call | solution.py:341
  32.3 0.0 collective-permute-done.5
  32.4 1.1 %collective-permute-start.8 = (bf16[256,128]{1,0:T(8,128)(2,1)S(1)}, bf16[256,128]{1,0:T(8,128)(2,1)S(1)}, u32[]{:S(2)}, u32[]{:S(2)}) collective-permute-start(bf16[256,128]{1,0:T(8,128)(2,1)S(1)} %fusion.8), channel_id=1, source_target_pairs={{0,2},{1,3},{2,0},{3,1},{4,6},{5,7},{6,4},{7,5},{8,10},{9,11},{10,... | collective-permute-start | bytes 196616 | tf_op jit(solution)/shard_map/ppermute | solution.py:27
  33.5 0.4 collective-permute-done.6
  33.9 3.9 %collective-permute-done.7 = bf16[256,128]{1,0:T(8,128)(2,1)S(1)} collective-permute-done((bf16[256,128]{1,0:T(8,128)(2,1)S(1)}, bf16[256,128]{1,0:T(8,128)(2,1)S(1)}, u32[]{:S(2)}, u32[]{:S(2)}) %collective-permute-start.7) | collective-permute-done | bytes 65568 | tf_op jit(solution)/shard_map/ppermute | solution.py:27
  37.9 0.2 collective-permute-done.8
  38.1 2.5 %collective-permute-start.11 = (f32[2,128]{1,0:T(2,128)S(1)}, f32[2,128]{1,0:T(2,128)S(1)}, u32[]{:S(2)}, u32[]{:S(2)}) collective-permute-start(f32[2,128]{1,0:T(2,128)S(1)} %bitcast_reduce_fusion), channel_id=1, source_target_pairs={{0,24},{8,16},{16,8},{24,0},{1,25},{9,17},{17,9},{25,1},{2,26},{10... | collective-permute-start | bytes 3080 | tf_op jit(solution)/shard_map/ppermute | solution.py:27
  40.7 0.5 %collective-permute-start.10 = (f32[2,128]{1,0:T(2,128)S(1)}, f32[2,128]{1,0:T(2,128)S(1)}, u32[]{:S(2)}, u32[]{:S(2)}) collective-permute-start(f32[2,128]{1,0:T(2,128)S(1)} %bitcast_reduce_fusion), channel_id=1, source_target_pairs={{0,16},{8,24},{16,0},{24,8},{1,17},{9,25},{17,1},{25,9},{2,18},{10... | collective-permute-start | bytes 3080 | tf_op jit(solution)/shard_map/ppermute | solution.py:27
  41.2 0.5 %collective-permute-start.9 = (f32[2,128]{1,0:T(2,128)S(1)}, f32[2,128]{1,0:T(2,128)S(1)}, u32[]{:S(2)}, u32[]{:S(2)}) collective-permute-start(f32[2,128]{1,0:T(2,128)S(1)} %bitcast_reduce_fusion), channel_id=1, source_target_pairs={{0,8},{8,0},{16,24},{24,16},{1,9},{9,1},{17,25},{25,17},{2,10},{10... | collective-permute-start | bytes 3080 | tf_op jit(solution)/shard_map/ppermute | solution.py:27
  41.7 0.7 %convert_add_fusion = f32[256,128]{1,0:T(8,128)} fusion(f32[256,128]{1,0:T(8,128)S(1)} %fusion.3, bf16[256,128]{1,0:T(8,128)(2,1)S(1)} %collective-permute-done.8), kind=kLoop, calls=%fused_computation.12 | loop fusion | flops 65536 | bytes 327680 | tf_op jit(solution)/shard_map/add | solution.py:365
  42.4 0.3 collective-permute-done.11
  42.7 1.6 %collective-permute-done.10 = f32[2,128]{1,0:T(2,128)S(1)} collective-permute-done((f32[2,128]{1,0:T(2,128)S(1)}, f32[2,128]{1,0:T(2,128)S(1)}, u32[]{:S(2)}, u32[]{:S(2)}) %collective-permute-start.10) | collective-permute-done | bytes 1056 | tf_op jit(solution)/shard_map/ppermute | solution.py:27
  44.2 0.5 %collective-permute-done.9 = f32[2,128]{1,0:T(2,128)S(1)} collective-permute-done((f32[2,128]{1,0:T(2,128)S(1)}, f32[2,128]{1,0:T(2,128)S(1)}, u32[]{:S(2)}, u32[]{:S(2)}) %collective-permute-start.9) | collective-permute-done | bytes 1056 | tf_op jit(solution)/shard_map/ppermute | solution.py:27
  44.7 0.6 %multiply_bitcast_fusion = f32[128,2]{0,1:T(2,128)} fusion(f32[2,128]{1,0:T(2,128)S(1)} %collective-permute-done.10, f32[2,128]{1,0:T(2,128)S(1)} %collective-permute-done.11, f32[2,128]{1,0:T(2,128)S(1)} %bitcast_reduce_fusion, f32[2,128]{1,0:T(2,128)S(1)} %collective-permute-done.9), kind=kLoop, calls=%fused_computation.16 | loop fusion | flops 1024 | bytes 5120 | tf_op jit(solution)/shard_map/transpose | solution.py:374
  (5 shorter events, 0.1 us)
Async XLA Ops:
  2.6 16.1 %collective-permute-start = (bf16[272,256]{1,0:T(8,128)(2,1)S(1)}, bf16[272,256]{1,0:T(8,128)(2,1)S(1)}, u32[]{:S(2)}, u32[]{:S(2)}) collective-permute-start(bf16[272,256]{1,0:T(8,128)(2,1)S(1)} %get-tuple-element.24), channel_id=1, source_target_pairs={{0,4},{1,5},{2,6},{3,7},{4,0},{5,1},{6,2},{7,3},{8,12},{9,13},{10,... | collective-permute-start | bytes 417800 | tf_op jit(solution)/shard_map/ppermute | solution.py:27
  6.7 12.0 %collective-permute-start.1 = (bf16[272,256]{1,0:T(8,128)(2,1)S(1)}, bf16[272,256]{1,0:T(8,128)(2,1)S(1)}, u32[]{:S(2)}, u32[]{:S(2)}) collective-permute-start(bf16[272,256]{1,0:T(8,128)(2,1)S(1)} %get-tuple-element.25), channel_id=1, source_target_pairs={{0,6},{1,7},{2,4},{3,5},{4,2},{5,3},{6,0},{7,1},{8,14},{9,15},{10,... | collective-permute-start | bytes 417800 | tf_op jit(solution)/shard_map/ppermute | solution.py:27
  8.0 10.7 %collective-permute-start.2 = (bf16[272,256]{1,0:T(8,128)(2,1)S(1)}, bf16[272,256]{1,0:T(8,128)(2,1)S(1)}, u32[]{:S(2)}, u32[]{:S(2)}) collective-permute-start(bf16[272,256]{1,0:T(8,128)(2,1)S(1)} %get-tuple-element.26), channel_id=1, source_target_pairs={{0,2},{1,3},{2,0},{3,1},{4,6},{5,7},{6,4},{7,5},{8,10},{9,11},{10,... | collective-permute-start | bytes 417800 | tf_op jit(solution)/shard_map/ppermute | solution.py:27
  18.7 1.9 %collective-permute-start.3 = (bf16[544,256]{1,0:T(8,128)(2,1)S(1)}, bf16[544,256]{1,0:T(8,128)(2,1)S(1)}, u32[]{:S(2)}, u32[]{:S(2)}) collective-permute-start(bf16[544,256]{1,0:T(8,128)(2,1)S(1)} %pass.1), channel_id=1, source_target_pairs={{0,1},{1,0},{2,3},{3,2},{4,5},{5,4},{6,7},{7,6},{8,9},{9,8},{10,11... | collective-permute-start | bytes 835592 | tf_op jit(solution)/shard_map/ppermute | solution.py:27
  25.4 2.0 %collective-permute-start.4 = (f32[2,256,128]{2,1,0:T(8,128)S(1)}, f32[2,256,128]{2,1,0:T(8,128)S(1)}, u32[]{:S(2)}, u32[]{:S(2)}) collective-permute-start(f32[2,256,128]{2,1,0:T(8,128)S(1)} %get-tuple-element.40), channel_id=1, source_target_pairs={{0,1},{1,0},{2,3},{3,2},{4,5},{5,4},{6,7},{7,6},{8,9},{9,8},{10,11... | collective-permute-start | bytes 786440 | tf_op jit(solution)/shard_map/ppermute | solution.py:27
  26.0 6.4 %collective-permute-start.5 = (f32[2,256,128]{2,1,0:T(8,128)S(1)}, f32[2,256,128]{2,1,0:T(8,128)S(1)}, u32[]{:S(2)}, u32[]{:S(2)}) collective-permute-start(f32[2,256,128]{2,1,0:T(8,128)S(1)} %get-tuple-element.41), channel_id=1, source_target_pairs={{0,1},{1,0},{2,3},{3,2},{4,5},{5,4},{6,7},{7,6},{8,9},{9,8},{10,11... | collective-permute-start | bytes 786440 | tf_op jit(solution)/shard_map/ppermute | solution.py:27
  27.5 6.4 %collective-permute-start.6 = (bf16[256,128]{1,0:T(8,128)(2,1)S(1)}, bf16[256,128]{1,0:T(8,128)(2,1)S(1)}, u32[]{:S(2)}, u32[]{:S(2)}) collective-permute-start(bf16[256,128]{1,0:T(8,128)(2,1)S(1)} %get-tuple-element.44.refs_6_), channel_id=1, source_target_pairs={{0,6},{1,7},{2,4},{3,5},{4,2},{5,3},{6,0},{7,1},{8,14},{9,15},{10,... | collective-permute-start | bytes 196616 | tf_op jit(solution)/shard_map/ppermute | solution.py:27
  30.5 7.4 %collective-permute-start.7 = (bf16[256,128]{1,0:T(8,128)(2,1)S(1)}, bf16[256,128]{1,0:T(8,128)(2,1)S(1)}, u32[]{:S(2)}, u32[]{:S(2)}) collective-permute-start(bf16[256,128]{1,0:T(8,128)(2,1)S(1)} %get-tuple-element.45.refs_5_), channel_id=1, source_target_pairs={{0,4},{1,5},{2,6},{3,7},{4,0},{5,1},{6,2},{7,3},{8,12},{9,13},{10,... | collective-permute-start | bytes 196616 | tf_op jit(solution)/shard_map/ppermute | solution.py:27
  32.4 5.7 %collective-permute-start.8 = (bf16[256,128]{1,0:T(8,128)(2,1)S(1)}, bf16[256,128]{1,0:T(8,128)(2,1)S(1)}, u32[]{:S(2)}, u32[]{:S(2)}) collective-permute-start(bf16[256,128]{1,0:T(8,128)(2,1)S(1)} %fusion.8), channel_id=1, source_target_pairs={{0,2},{1,3},{2,0},{3,1},{4,6},{5,7},{6,4},{7,5},{8,10},{9,11},{10,... | collective-permute-start | bytes 196616 | tf_op jit(solution)/shard_map/ppermute | solution.py:27
  38.1 4.5 %collective-permute-start.11 = (f32[2,128]{1,0:T(2,128)S(1)}, f32[2,128]{1,0:T(2,128)S(1)}, u32[]{:S(2)}, u32[]{:S(2)}) collective-permute-start(f32[2,128]{1,0:T(2,128)S(1)} %bitcast_reduce_fusion), channel_id=1, source_target_pairs={{0,24},{8,16},{16,8},{24,0},{1,25},{9,17},{17,9},{25,1},{2,26},{10... | collective-permute-start | bytes 3080 | tf_op jit(solution)/shard_map/ppermute | solution.py:27
  40.7 3.6 %collective-permute-start.10 = (f32[2,128]{1,0:T(2,128)S(1)}, f32[2,128]{1,0:T(2,128)S(1)}, u32[]{:S(2)}, u32[]{:S(2)}) collective-permute-start(f32[2,128]{1,0:T(2,128)S(1)} %bitcast_reduce_fusion), channel_id=1, source_target_pairs={{0,16},{8,24},{16,0},{24,8},{1,17},{9,25},{17,1},{25,9},{2,18},{10... | collective-permute-start | bytes 3080 | tf_op jit(solution)/shard_map/ppermute | solution.py:27
  41.2 3.6 %collective-permute-start.9 = (f32[2,128]{1,0:T(2,128)S(1)}, f32[2,128]{1,0:T(2,128)S(1)}, u32[]{:S(2)}, u32[]{:S(2)}) collective-permute-start(f32[2,128]{1,0:T(2,128)S(1)} %bitcast_reduce_fusion), channel_id=1, source_target_pairs={{0,8},{8,0},{16,24},{24,16},{1,9},{9,1},{17,25},{25,17},{2,10},{10... | collective-permute-start | bytes 3080 | tf_op jit(solution)/shard_map/ppermute | solution.py:27
